TPU v7x, 128 devices: a whole 4x4x4 slice. The times are simulated.
128 devices in a mesh: src: 16 (over z, y_lo, core), tgt: 8 (over x, y_hi).
Axes of the slice: x: 4, y: 4 (y_hi: 2, y_lo: 2; y = y_hi * 2 + y_lo), z: 4, core: 2. Of those that a mesh axis runs over, the one named last changes fastest.
Arguments:
- charges: bfloat16 [2097152, 128], P(('src', 'tgt')), may hold values from -6 to 6
- project: bfloat16 [2048, 128, 1024], P(('src', 'tgt')), may hold values from -0.1875 to 0.1875
- own_transfer: bfloat16 [4, 2048, 64, 128], P(None, ('src', 'tgt')), may hold values from -0.375 to 0.375
- cross_transfer: bfloat16 [4, 2048, 64, 128], P(None, ('src', 'tgt')), may hold values from -0.375 to 0.375
- evaluate: bfloat16 [2048, 1024, 128], P(('src', 'tgt')), may hold values from -0.5 to 0.5
Outputs:
- potential: bfloat16 [2, 2097152, 128], P(None, ('src', 'tgt'))
All inputs are finite; a program needn't handle non-finite values.
Results may differ from a plain program's by a relative error of at most 0.009.
Values may be sent and summed in bfloat16 or wider, within the bound.
No kernel may reach another device: no remote copies, remote signals or barrier semaphores. Data moves between devices by JAX's collectives and lax.ppermute only.
A program may use at most 128 MiB of HBM per device.

v0:
```python
import jax
import jax.numpy as jnp
from jax import lax
from jax.sharding import PartitionSpec as P


def partner_2(value, axis, distance):
    mask = 2**distance
    pairs = [(source, source ^ mask) for source in range(lax.axis_size(axis))]
    return lax.ppermute(value, axis, pairs)


def rotate_pair(coeffs):
    half_rank = coeffs.shape[1] // 2
    real_rows = coeffs[:, :half_rank]
    imag_rows = coeffs[:, half_rank:]
    flipped = jnp.concatenate([real_rows, -imag_rows], axis=1)
    swapped = jnp.concatenate([imag_rows, real_rows], axis=1)
    return (flipped, swapped)


def complex_apply(matrices, coeffs):
    flipped, swapped = rotate_pair(coeffs)
    real_part = jnp.einsum("bkj,bjr->bkr", matrices, flipped, preferred_element_type=jnp.float32)
    imag_part = jnp.einsum("bkj,bjr->bkr", matrices, swapped, preferred_element_type=jnp.float32)
    return jnp.concatenate([real_part, imag_part], axis=1)


def level_update(own_level, cross_level, coeffs, partner):
    summed = complex_apply(own_level, coeffs) + complex_apply(cross_level, partner)
    return summed.astype(jnp.bfloat16)


def shards(charges, project, own_transfer, cross_transfer, evaluate):
    blocks, rank_rows, points = project.shape
    columns = charges.shape[1]
    charge_blocks = charges.reshape(blocks, points, columns)
    coeffs = jnp.einsum(
        "bkp,bpr->bkr", project, charge_blocks, preferred_element_type=jnp.float32
    ).astype(jnp.bfloat16)
    bit_count = lax.axis_size("src").bit_length() - 1
    level_count = own_transfer.shape[0]
    for height in range(level_count):
        level_bit = height % bit_count
        partner = partner_2(coeffs, "src", level_bit)
        coeffs = level_update(own_transfer[height], cross_transfer[height], coeffs, partner)
    received = lax.all_to_all(coeffs, "tgt", split_axis=0, concat_axis=0, tiled=True)
    flipped, swapped = rotate_pair(received)
    real_part = jnp.einsum("bpj,bjr->bpr", evaluate, flipped, preferred_element_type=jnp.float32)
    imag_part = jnp.einsum("bpj,bjr->bpr", evaluate, swapped, preferred_element_type=jnp.float32)
    stacked = jnp.stack([real_part, imag_part]).astype(jnp.bfloat16)
    return stacked.reshape(2, blocks * points, received.shape[2])


def solution(mesh):
    in_specs = (
        P(("src", "tgt"), None),
        P(("src", "tgt"), None, None),
        P(None, ("src", "tgt"), None, None),
        P(None, ("src", "tgt"), None, None),
        P(("src", "tgt"), None, None),
    )
    out_specs = P(None, ("src", "tgt"), None)
    return jax.shard_map(shards, mesh=mesh, in_specs=in_specs, out_specs=out_specs, check_vma=False)
```

profile of v0, /device:TPU:0, one launch (start us, length us, event | category | flops | bytes accessed | tf_op | source)
XLA Modules:
  0.0 97.0 jit_solution(10106244661928366967)
XLA Ops:
  0.0 4.8 %convolution_convert_fusion = bf16[16,128,128]{2,1,0:T(8,128)(2,1)S(1)} fusion(bf16[16,128,1024]{2,1,0:T(8,128)(2,1)} %param.6, bf16[16,1024,128]{2,1,0:T(8,128)(2,1)} %bitcast.85), kind=kOutput, calls=%fused_computation.3 | convolution fusion | flops 537133056 | bytes 8912896 | tf_op jit(solution)/shard_map/bkp,bpr->bkr/dot_general | solution.py:38
  4.8 0.0 copy-start.2
  4.8 0.1 collective-permute-start
  4.9 0.1 slice_negate_fusion.8
  5.0 0.0 copy-done.1
  5.0 0.3 convolution_bitcast_fusion.15
  5.3 0.3 convolution_bitcast_fusion.14
  5.5 1.3 %collective-permute-done = bf16[16,128,128]{2,1,0:T(8,128)(2,1)S(1)} collective-permute-done((bf16[16,128,128]{2,1,0:T(8,128)(2,1)S(1)}, bf16[16,128,128]{2,1,0:T(8,128)(2,1)S(1)}, u32[]{:S(2)}, u32[]{:S(2)}) %collective-permute-start) | collective-permute-done | bytes 524320 | tf_op jit(solution)/shard_map/ppermute | solution.py:10
  6.8 0.1 slice_negate_fusion.7
  6.9 0.0 copy-done.2
  6.9 0.3 convolution_bitcast_fusion.13
  7.1 0.3 convolution_bitcast_fusion.12
  7.4 0.1 fusion
  7.6 1.7 %collective-permute-start.1 = (bf16[16,128,128]{2,1,0:T(8,128)(2,1)S(1)}, bf16[16,128,128]{2,1,0:T(8,128)(2,1)S(1)}, u32[]{:S(2)}, u32[]{:S(2)}) collective-permute-start(bf16[16,128,128]{2,1,0:T(8,128)(2,1)S(1)} %fusion), channel_id=1, source_target_pairs={{0,16},{8,24},{16,0},{24,8},{32,48},{40,56},{48,32},{56,40},{64,80... | collective-permute-start | bytes 1572872 | tf_op jit(solution)/shard_map/ppermute | solution.py:10
  9.3 0.1 slice_negate_fusion.6
  9.4 0.3 convolution_bitcast_fusion.11
  9.6 0.3 convolution_bitcast_fusion.10
  9.9 11.7 %collective-permute-done.1 = bf16[16,128,128]{2,1,0:T(8,128)(2,1)S(1)} collective-permute-done((bf16[16,128,128]{2,1,0:T(8,128)(2,1)S(1)}, bf16[16,128,128]{2,1,0:T(8,128)(2,1)S(1)}, u32[]{:S(2)}, u32[]{:S(2)}) %collective-permute-start.1) | collective-permute-done | bytes 524320 | tf_op jit(solution)/shard_map/ppermute | solution.py:10
  21.6 0.1 slice_negate_fusion.5
  21.7 0.3 convolution_bitcast_fusion.9
  22.0 0.3 convolution_bitcast_fusion.8
  22.2 0.1 fusion.1
  22.4 2.1 %collective-permute-start.2 = (bf16[16,128,128]{2,1,0:T(8,128)(2,1)S(1)}, bf16[16,128,128]{2,1,0:T(8,128)(2,1)S(1)}, u32[]{:S(2)}, u32[]{:S(2)}) collective-permute-start(bf16[16,128,128]{2,1,0:T(8,128)(2,1)S(1)} %fusion.1), channel_id=1, source_target_pairs={{0,32},{8,40},{16,48},{24,56},{32,0},{40,8},{48,16},{56,24},{64,96... | collective-permute-start | bytes 1572872 | tf_op jit(solution)/shard_map/ppermute | solution.py:10
  24.4 0.1 slice_negate_fusion.4
  24.5 0.3 convolution_bitcast_fusion.7
  24.8 0.3 convolution_bitcast_fusion.6
  25.1 10.8 %collective-permute-done.2 = bf16[16,128,128]{2,1,0:T(8,128)(2,1)S(1)} collective-permute-done((bf16[16,128,128]{2,1,0:T(8,128)(2,1)S(1)}, bf16[16,128,128]{2,1,0:T(8,128)(2,1)S(1)}, u32[]{:S(2)}, u32[]{:S(2)}) %collective-permute-start.2) | collective-permute-done | bytes 524320 | tf_op jit(solution)/shard_map/ppermute | solution.py:10
  35.8 0.1 slice_negate_fusion.3
  35.9 0.3 convolution_bitcast_fusion.5
  36.2 0.3 convolution_bitcast_fusion.4
  36.5 0.1 fusion.2
  36.6 3.8 %collective-permute-start.3 = (bf16[16,128,128]{2,1,0:T(8,128)(2,1)S(1)}, bf16[16,128,128]{2,1,0:T(8,128)(2,1)S(1)}, u32[]{:S(2)}, u32[]{:S(2)}) collective-permute-start(bf16[16,128,128]{2,1,0:T(8,128)(2,1)S(1)} %fusion.2), channel_id=1, source_target_pairs={{0,64},{8,72},{16,80},{24,88},{32,96},{40,104},{48,112},{56,120},{... | collective-permute-start | bytes 1572872 | tf_op jit(solution)/shard_map/ppermute | solution.py:10
  40.4 0.1 slice_negate_fusion.2
  40.5 0.3 convolution_bitcast_fusion.3
  40.7 0.3 convolution_bitcast_fusion.2
  41.0 0.0 copy-start
  41.0 9.8 %collective-permute-done.3 = bf16[16,128,128]{2,1,0:T(8,128)(2,1)S(1)} collective-permute-done((bf16[16,128,128]{2,1,0:T(8,128)(2,1)S(1)}, bf16[16,128,128]{2,1,0:T(8,128)(2,1)S(1)}, u32[]{:S(2)}, u32[]{:S(2)}) %collective-permute-start.3) | collective-permute-done | bytes 524320 | tf_op jit(solution)/shard_map/ppermute | solution.py:10
  50.9 0.1 slice_negate_fusion.1
  50.9 0.3 convolution_bitcast_fusion.1
  51.2 0.3 convolution_bitcast_fusion
  51.5 0.1 fusion.3
  51.6 16.6 %all_to_all.5 = bf16[16,128,128]{2,1,0:T(8,128)(2,1)S(1)} all-to-all(bf16[16,128,128]{2,1,0:T(8,128)(2,1)S(1)} %fusion.3), channel_id=1, replica_groups=mesh['src'=16,'tgt'=8] {'tgt'}, dimensions={0} | all-to-all | bytes 1048576 | tf_op jit(solution)/shard_map/all_to_all | solution.py:47
  68.2 0.1 slice_negate_fusion
  68.3 3.3 %convert_bitcast_fusion.1 = bf16[16,1024,128]{1,2,0:T(8,128)(2,1)} fusion(bf16[16,1024,128]{2,1,0:T(8,128)(2,1)S(1)} %copy-done, bf16[16,64,128]{2,1,0:T(8,128)(2,1)S(1)} %get-tuple-element.5, bf16[16,64,128]{2,1,0:T(8,128)(2,1)S(1)} %get-tuple-element.7), kind=kOutput, calls=%fused_computation.2 | convolution fusion | flops 540016640 | bytes 8912896 | tf_op jit(solution)/shard_map/bpj,bjr->bpr/dot_general | solution.py:49
  71.6 6.4 %copy.9 = bf16[16,1024,128]{2,1,0:T(8,128)(2,1)} copy(bf16[16,1024,128]{1,2,0:T(8,128)(2,1)} %convert_bitcast_fusion.1) | data formatting | bytes 8388608 | tf_op jit(solution)/shard_map/bpj,bjr->bpr/dot_general | solution.py:49
  78.0 5.5 %convert_bitcast_fusion = bf16[16,1024,128]{1,2,0:T(8,128)(2,1)} fusion(bf16[16,1024,128]{2,1,0:T(8,128)(2,1)} %param.9, bf16[16,64,128]{2,1,0:T(8,128)(2,1)S(1)} %get-tuple-element.7, bf16[16,64,128]{2,1,0:T(8,128)(2,1)S(1)} %get-tuple-element.6), kind=kOutput, calls=%fused_computation.1 | convolution fusion | flops 540016640 | bytes 8912896 | tf_op jit(solution)/shard_map/bpj,bjr->bpr/dot_general | solution.py:50
  83.5 6.4 %copy.11 = bf16[16,1024,128]{2,1,0:T(8,128)(2,1)} copy(bf16[16,1024,128]{1,2,0:T(8,128)(2,1)} %convert_bitcast_fusion) | data formatting | bytes 8388608 | tf_op jit(solution)/shard_map/bpj,bjr->bpr/dot_general | solution.py:50
  89.9 7.1 %pad_maximum_fusion = bf16[2,16384,128]{2,1,0:T(8,128)(2,1)} fusion(bf16[1,16384,128]{2,1,0:T(8,128)(2,1)} %bitcast.84, bf16[1,16384,128]{2,1,0:T(8,128)(2,1)} %bitcast.83), kind=kLoop, calls=%fused_computation | loop fusion | flops 4194304 | bytes 16777216 | tf_op jit(solution)/shard_map/stack | solution.py:51
  (2 shorter events, 0.0 us)
Async XLA Ops:
  0.0 5.0 %copy-start.1 = (bf16[4,16,64,128]{3,2,1,0:T(8,128)(2,1)S(1)}, bf16[4,16,64,128]{3,2,1,0:T(8,128)(2,1)}, u32[]{:S(2)}) copy-start(bf16[4,16,64,128]{3,2,1,0:T(8,128)(2,1)} %param.7) | copy-start | bytes 3145732
  4.8 2.1 %copy-start.2 = (bf16[4,16,64,128]{3,2,1,0:T(8,128)(2,1)S(1)}, bf16[4,16,64,128]{3,2,1,0:T(8,128)(2,1)}, u32[]{:S(2)}) copy-start(bf16[4,16,64,128]{3,2,1,0:T(8,128)(2,1)} %param.8) | copy-start | bytes 3145732
  4.8 2.0 %collective-permute-start = (bf16[16,128,128]{2,1,0:T(8,128)(2,1)S(1)}, bf16[16,128,128]{2,1,0:T(8,128)(2,1)S(1)}, u32[]{:S(2)}, u32[]{:S(2)}) collective-permute-start(bf16[16,128,128]{2,1,0:T(8,128)(2,1)S(1)} %convolution_convert_fusion), channel_id=1, source_target_pairs={{0,8},{8,0},{16,24},{24,16},{32,40},{40,32},{48,56},{56,48},{64,72... | collective-permute-start | bytes 1572872 | tf_op jit(solution)/shard_map/ppermute | solution.py:10
  7.6 14.0 %collective-permute-start.1 = (bf16[16,128,128]{2,1,0:T(8,128)(2,1)S(1)}, bf16[16,128,128]{2,1,0:T(8,128)(2,1)S(1)}, u32[]{:S(2)}, u32[]{:S(2)}) collective-permute-start(bf16[16,128,128]{2,1,0:T(8,128)(2,1)S(1)} %fusion), channel_id=1, source_target_pairs={{0,16},{8,24},{16,0},{24,8},{32,48},{40,56},{48,32},{56,40},{64,80... | collective-permute-start | bytes 1572872 | tf_op jit(solution)/shard_map/ppermute | solution.py:10
  22.4 13.5 %collective-permute-start.2 = (bf16[16,128,128]{2,1,0:T(8,128)(2,1)S(1)}, bf16[16,128,128]{2,1,0:T(8,128)(2,1)S(1)}, u32[]{:S(2)}, u32[]{:S(2)}) collective-permute-start(bf16[16,128,128]{2,1,0:T(8,128)(2,1)S(1)} %fusion.1), channel_id=1, source_target_pairs={{0,32},{8,40},{16,48},{24,56},{32,0},{40,8},{48,16},{56,24},{64,96... | collective-permute-start | bytes 1572872 | tf_op jit(solution)/shard_map/ppermute | solution.py:10
  36.6 14.3 %collective-permute-start.3 = (bf16[16,128,128]{2,1,0:T(8,128)(2,1)S(1)}, bf16[16,128,128]{2,1,0:T(8,128)(2,1)S(1)}, u32[]{:S(2)}, u32[]{:S(2)}) collective-permute-start(bf16[16,128,128]{2,1,0:T(8,128)(2,1)S(1)} %fusion.2), channel_id=1, source_target_pairs={{0,64},{8,72},{16,80},{24,88},{32,96},{40,104},{48,112},{56,120},{... | collective-permute-start | bytes 1572872 | tf_op jit(solution)/shard_map/ppermute | solution.py:10
  41.0 27.3 %copy-start = (bf16[16,1024,128]{2,1,0:T(8,128)(2,1)S(1)}, bf16[16,1024,128]{2,1,0:T(8,128)(2,1)}, u32[]{:S(2)}) copy-start(bf16[16,1024,128]{2,1,0:T(8,128)(2,1)} %param.9) | copy-start | bytes 12582916
where the time goes:
time: 97.4 us; the launch traced here: 97 us
  waiting for transfers between devices  33.5 us (34%)
  matrix products  18 us (18%)
  blocking collectives  16.6 us (17%)
  local copies, waits for them, and re-layouts  12.8 us (13%)
  other arithmetic  8.24 us (8%)
  starting transfers between devices  7.69 us (8%)
    ppermute x4, waiting for transfers between devices, partner_2(): return lax.ppermute(value, axis, pairs)  33.5 us
    all_to_all x1, blocking collectives, shards(): lax.all_to_all(coeffs, 'tgt', split_axis=0, concat_axis=0, tiled=True)  16.6 us
    ppermute x4, starting transfers between devices, partner_2(): return lax.ppermute(value, axis, pairs)  7.69 us
    another operation x1, other arithmetic, shards(): stacked = jnp.stack([real_part, imag_part]).astype(jnp.bfloat16)  7.1 us
    dot_general x1, local copies, waits for them, and re-layouts, shards(): jnp.einsum('bpj,bjr->bpr', evaluate, flipped, preferred_element_type=jnp....  6.41 us
    dot_general x1, local copies, waits for them, and re-layouts, shards(): jnp.einsum('bpj,bjr->bpr', evaluate, swapped, preferred_element_type=jnp....  6.4 us
    dot_general x1, matrix products, shards(): jnp.einsum('bpj,bjr->bpr', evaluate, swapped, preferred_element_type=jnp....  5.5 us
    dot_general x1, matrix products, shards(): jnp.einsum('bkp,bpr->bkr', project, charge_blocks, preferred_element_type...  4.78 us
  transfers between devices with their start and end apart: 4, of which 4 were waited for; matrix products, arithmetic and copies ran while one was open for 3% of the time, Pallas kernels for 0%

commit v1 on v0

v1 whole, which is shorter than its diff:
```python
import jax
import jax.numpy as jnp
from jax import lax
from jax.experimental import pallas as pl
from jax.experimental.pallas import tpu as pltpu
from jax.sharding import PartitionSpec as P

F32 = jnp.float32
BF16 = jnp.bfloat16
RANK2 = 128
POINTS = 1024
COLS = 128
MIB = 1024 * 1024
VMEM = pl.BlockSpec(memory_space=pltpu.VMEM)
ANY = pl.BlockSpec(memory_space=pl.ANY)


def pairs_by(mask, size):
    return [(i, i ^ mask) for i in range(size)]


def pair_at(j, b):
    tgt = lax.axis_index("tgt")
    return tgt ^ (j * 2 + b)


def rotated(c):
    half = c.shape[0] // 2
    re, im = c[:half], c[half:]
    return jnp.concatenate([jnp.concatenate([re, -im], axis=0), jnp.concatenate([im, re], axis=0)], axis=1)


def butterfly(own, cross, own_rotated, partner_rotated):
    matrices = jnp.concatenate([own, cross], axis=1)
    operand = jnp.concatenate([own_rotated, partner_rotated], axis=0)
    both = jnp.dot(matrices, operand, preferred_element_type=F32)
    cols = both.shape[1] // 2
    return jnp.concatenate([both[:, :cols], both[:, cols:]], axis=0).astype(BF16)


def leaf(project, charges, chunk):
    def kernel(project, charges, out, rows, points, row_sems, point_sems):
        loads = []
        for j in range(4):
            pair = pair_at(j, chunk)
            row_load = pltpu.make_async_copy(project.at[pl.ds(pair * 2, 2)], rows.at[pl.ds(j * 2, 2)], row_sems.at[j])
            point_load = pltpu.make_async_copy(charges.at[pl.ds(pair * 2 * POINTS, 2 * POINTS)], points.at[j], point_sems.at[j])
            row_load.start()
            point_load.start()
            loads.append((row_load, point_load))
        for j, (row_load, point_load) in enumerate(loads):
            row_load.wait()
            point_load.wait()
            for v in range(2):
                block = points[j, v * POINTS : (v + 1) * POINTS, :]
                out[j, v] = jnp.dot(rows[j * 2 + v], block, preferred_element_type=F32).astype(BF16)

    return pl.pallas_call(
        kernel,
        in_specs=[ANY, ANY],
        out_specs=VMEM,
        out_shape=jax.ShapeDtypeStruct((4, 2, RANK2, COLS), BF16),
        scratch_shapes=[
            pltpu.VMEM((8, RANK2, POINTS), BF16),
            pltpu.VMEM((4, 2 * POINTS, COLS), BF16),
            pltpu.SemaphoreType.DMA((4,)),
            pltpu.SemaphoreType.DMA((4,)),
        ],
        compiler_params=pltpu.CompilerParams(vmem_limit_bytes=58 * MIB),
        cost_estimate=pl.CostEstimate(flops=8 * 2 * 128 * 128 * 1024, bytes_accessed=4 * MIB, transcendentals=0),
        name="leaf",
    )(project, charges)


def level(own, cross, coeffs, partner, height, chunk, split):
    def kernel(own, cross, coeffs, partner, *outs):
        for j in range(4):
            pair = pair_at(j, chunk)
            for v in range(2):
                m = pair * 2 + v
                new = butterfly(own[height, m], cross[height, m], rotated(coeffs[j, v]), rotated(partner[j, v]))
                if split:
                    outs[j][v] = new
                else:
                    outs[0][j, v] = new

    one = jax.ShapeDtypeStruct((2, RANK2, COLS), BF16)
    return pl.pallas_call(
        kernel,
        in_specs=[VMEM] * 4,
        out_specs=[VMEM] * 4 if split else VMEM,
        out_shape=[one] * 4 if split else jax.ShapeDtypeStruct((4, 2, RANK2, COLS), BF16),
        compiler_params=pltpu.CompilerParams(vmem_limit_bytes=8 * MIB),
        cost_estimate=pl.CostEstimate(flops=8 * 2 * 64 * 256 * 256, bytes_accessed=MIB, transcendentals=0),
        name="level",
    )(own, cross, coeffs, partner)


def far_field(pieces, evaluate, chunk, so_far=None):
    def kernel(c0, c1, c2, c3, matrices, *rest):
        out, results, sems = rest[-3:]
        copies = []
        for j, piece in enumerate((c0, c1, c2, c3)):
            pair = pair_at(j, chunk)
            for v in range(2):
                n, block = j * 2 + v, pair * 2 + v
                turned = rotated(piece[v])
                for part in range(4):
                    span = pl.ds(part * (POINTS // 4), POINTS // 4)
                    both = jnp.dot(matrices[block, span, :], turned, preferred_element_type=F32)
                    results[n, 0, span, :] = both[:, :COLS].astype(BF16)
                    results[n, 1, span, :] = both[:, COLS:].astype(BF16)
                for c in range(2):
                    copy = pltpu.make_async_copy(results.at[n, c], out.at[c, pl.ds(block * POINTS, POINTS)], sems.at[n * 2 + c])
                    copy.start()
                    copies.append(copy)
        for copy in copies:
            copy.wait()

    operands = [*pieces, evaluate] + ([] if so_far is None else [so_far])
    return pl.pallas_call(
        kernel,
        in_specs=[VMEM] * 5 + ([] if so_far is None else [ANY]),
        out_specs=ANY,
        out_shape=jax.ShapeDtypeStruct((2, 16 * POINTS, COLS), BF16),
        scratch_shapes=[pltpu.VMEM((8, 2, POINTS, COLS), BF16), pltpu.SemaphoreType.DMA((16,))],
        input_output_aliases={} if so_far is None else {5: 0},
        compiler_params=pltpu.CompilerParams(vmem_limit_bytes=16 * MIB),
        cost_estimate=pl.CostEstimate(flops=8 * 2 * 1024 * 128 * 256, bytes_accessed=6 * MIB, transcendentals=0),
        name="far_field",
    )(*operands)


def shards(charges, project, own_transfer, cross_transfer, evaluate):
    def levels(chunk):
        coeffs = leaf(project, charges, chunk)
        for height in range(4):
            partner = lax.ppermute(coeffs, "src", pairs_by(1 << height, 16))
            coeffs = level(own_transfer, cross_transfer, coeffs, partner, height, chunk, split=height == 3 and chunk == 0)
        if chunk:
            coeffs = lax.ppermute(coeffs, "tgt", pairs_by(1, 8))
            coeffs = [coeffs[j] for j in range(4)]
        return [lax.ppermute(coeffs[j], "tgt", pairs_by(2 * j, 8)) if j else coeffs[j] for j in range(4)]

    crossed = levels(1)
    straight = levels(0)
    potential = far_field(crossed, evaluate, 1)
    return far_field(straight, evaluate, 0, potential)


def solution(mesh):
    in_specs = (
        P(("src", "tgt"), None),
        P(("src", "tgt"), None, None),
        P(None, ("src", "tgt"), None, None),
        P(None, ("src", "tgt"), None, None),
        P(("src", "tgt"), None, None),
    )
    out_specs = P(None, ("src", "tgt"), None)
    return jax.shard_map(shards, mesh=mesh, in_specs=in_specs, out_specs=out_specs, check_vma=False)
```

time: 97.4 us -> 59.5 us (0.61)
  starting transfers between devices: 7.69 us -> 26.4 us
  matrix products: 18 us -> 0 us
  blocking collectives: 16.6 us -> 0 us
  waiting for transfers between devices: 33.5 us -> 17.1 us
  Pallas kernels: 0 us -> 13.8 us
  local copies, waits for them, and re-layouts: 12.8 us -> 1.93 us
  other arithmetic: 8.24 us -> 0 us
    ppermute x4 -> x15, starting transfers between devices: 7.69 us -> 26.4 us  [the longest x8 13.5 us: levels(): partner = lax.ppermute(coeffs, 'src', pairs_by(1 << height, 16))]
    dot_general x19 -> x0, matrix products: 18 us -> none  [the longest x1 5.5 us: shards(): jnp.einsum('bpj,bjr->bpr', evaluate, swapped, preferred_element_type=jnp....]
    all_to_all x1 -> x0, blocking collectives: 16.6 us -> none  [shards(): lax.all_to_all(coeffs, 'tgt', split_axis=0, concat_axis=0, tiled=True)]
    ppermute x4 -> x15, waiting for transfers between devices: 33.5 us -> 17.1 us  [the longest x8 14.4 us: levels(): partner = lax.ppermute(coeffs, 'src', pairs_by(1 << height, 16))]
    pallas_call x0 -> x12, Pallas kernels: none -> 13.8 us  [the longest x2 6.56 us: leaf(): pl.pallas_call(kernel, in_specs=[ANY, ANY], out_specs=VMEM, out_shape=jax...]
    dot_general x2 -> x0, local copies, waits for them, and re-layouts: 12.8 us -> none  [the longest x1 6.41 us: shards(): jnp.einsum('bpj,bjr->bpr', evaluate, flipped, preferred_element_type=jnp....]
    another operation x1 -> x0, other arithmetic: 7.1 us -> none  [shards(): stacked = jnp.stack([real_part, imag_part]).astype(jnp.bfloat16)]
    unnamed x6 -> x10, local copies, waits for them, and re-layouts: 0.01 us -> 1.92 us
  transfers between devices with their start and end apart: 4 -> 15, of which waited for: 4 -> 7; matrix products, arithmetic and copies ran while one was open for 3% -> 0% of each run, Pallas kernels for 0% -> 13%
where the time goes in v1:
time: 59.5 us; the launch traced here: 59.3 us
  starting transfers between devices  26.4 us (44%)
  waiting for transfers between devices  17.1 us (29%)
  Pallas kernels  13.8 us (23%)
  local copies, waits for them, and re-layouts  1.93 us (3%)
    ppermute x8, waiting for transfers between devices, levels(): partner = lax.ppermute(coeffs, 'src', pairs_by(1 << height, 16))  14.4 us
    ppermute x8, starting transfers between devices, levels(): partner = lax.ppermute(coeffs, 'src', pairs_by(1 << height, 16))  13.5 us
    ppermute x6, starting transfers between devices, levels(): lax.ppermute(coeffs[j], 'tgt', pairs_by(2 * j, 8))  9.55 us
    pallas_call x2, Pallas kernels, leaf(): pl.pallas_call(kernel, in_specs=[ANY, ANY], out_specs=VMEM, out_shape=jax...  6.56 us
    pallas_call x2, Pallas kernels, far_field(): pl.pallas_call(kernel, in_specs=[VMEM] * 5 + ([] if so_far is None else [...  4.82 us
    ppermute x1, starting transfers between devices, levels(): coeffs = lax.ppermute(coeffs, 'tgt', pairs_by(1, 8))  3.27 us
    pallas_call x8, Pallas kernels, level(): pl.pallas_call(kernel, in_specs=[VMEM] * 4, out_specs=[VMEM] * 4 if split...  2.38 us
    ppermute x6, waiting for transfers between devices, levels(): lax.ppermute(coeffs[j], 'tgt', pairs_by(2 * j, 8))  1.96 us
  transfers between devices with their start and end apart: 15, of which 7 were waited for; matrix products, arithmetic and copies ran while one was open for 0% of the time, Pallas kernels for 13%

profile of v1, /device:TPU:0, one launch (start us, length us, event | category | flops | bytes accessed | tf_op | source)
XLA Modules:
  0.0 59.3 jit_solution(16601408338773253932)
XLA Ops:
  0.0 3.4 %leaf.3.coeffs = bf16[4,2,128,128]{3,2,1,0:T(8,128)(2,1)} custom-call(bf16[16,128,1024]{2,1,0:T(8,128)(2,1)} %project.3, bf16[16384,128]{1,0:T(8,128)(2,1)} %charges.3), custom_call_target="tpu_custom_call" | custom-call | flops 268435456 | bytes 4194304 | tf_op jit(solution)/shard_map/leaf/pallas_call | solution.py:58
  3.4 0.1 collective-permute-start.7
  3.5 1.7 %collective-permute-done.7.partner = bf16[4,2,128,128]{3,2,1,0:T(8,128)(2,1)S(1)} collective-permute-done((bf16[4,2,128,128]{3,2,1,0:T(8,128)(2,1)}, bf16[4,2,128,128]{3,2,1,0:T(8,128)(2,1)S(1)}, u32[]{:S(2)}, u32[]{:S(2)}) %collective-permute-start.7) | collective-permute-done | bytes 262176 | tf_op jit(solution)/shard_map/ppermute | solution.py:138
  5.2 0.0 copy-done.1
  5.2 0.0 copy-done
  5.2 0.9 %copy-done.4 = bf16[4,2,128,128]{3,2,1,0:T(8,128)(2,1)S(1)} copy-done((bf16[4,2,128,128]{3,2,1,0:T(8,128)(2,1)S(1)}, bf16[4,2,128,128]{3,2,1,0:T(8,128)(2,1)}, u32[]{:S(2)}) %copy-start.4) | copy-done | bytes 262168
  6.1 0.3 level.12.coeffs
  6.5 1.7 %collective-permute-start.8 = (bf16[4,2,128,128]{3,2,1,0:T(8,128)(2,1)S(1)}, bf16[4,2,128,128]{3,2,1,0:T(8,128)(2,1)S(1)}, u32[]{:S(2)}, u32[]{:S(2)}) collective-permute-start(bf16[4,2,128,128]{3,2,1,0:T(8,128)(2,1)S(1)} %level.12.coeffs), channel_id=1, source_target_pairs={{0,16},{8,24},{16,0},{24,8},{32,48},{40,56},{48,32},{56,40},{64,80... | collective-permute-start | bytes 786440 | tf_op jit(solution)/shard_map/ppermute | solution.py:138
  8.2 3.2 %leaf.2.coeffs = bf16[4,2,128,128]{3,2,1,0:T(8,128)(2,1)} custom-call(bf16[16,128,1024]{2,1,0:T(8,128)(2,1)} %project.3, bf16[16384,128]{1,0:T(8,128)(2,1)} %charges.3), custom_call_target="tpu_custom_call" | custom-call | flops 268435456 | bytes 4194304 | tf_op jit(solution)/shard_map/leaf/pallas_call | solution.py:58
  11.4 0.1 collective-permute-start
  11.5 3.4 %collective-permute-done.8.partner = bf16[4,2,128,128]{3,2,1,0:T(8,128)(2,1)S(1)} collective-permute-done((bf16[4,2,128,128]{3,2,1,0:T(8,128)(2,1)S(1)}, bf16[4,2,128,128]{3,2,1,0:T(8,128)(2,1)S(1)}, u32[]{:S(2)}, u32[]{:S(2)}) %collective-permute-start.8) | collective-permute-done | bytes 262176 | tf_op jit(solution)/shard_map/ppermute | solution.py:138
  14.9 0.3 level.13.coeffs
  15.2 2.1 %collective-permute-start.9 = (bf16[4,2,128,128]{3,2,1,0:T(8,128)(2,1)S(1)}, bf16[4,2,128,128]{3,2,1,0:T(8,128)(2,1)S(1)}, u32[]{:S(2)}, u32[]{:S(2)}) collective-permute-start(bf16[4,2,128,128]{3,2,1,0:T(8,128)(2,1)S(1)} %level.13.coeffs), channel_id=1, source_target_pairs={{0,32},{8,40},{16,48},{24,56},{32,0},{40,8},{48,16},{56,24},{64,96... | collective-permute-start | bytes 786440 | tf_op jit(solution)/shard_map/ppermute | solution.py:138
  17.3 0.0 collective-permute-done.partner
  17.3 0.9 %copy-done.3 = bf16[4,2,128,128]{3,2,1,0:T(8,128)(2,1)S(1)} copy-done((bf16[4,2,128,128]{3,2,1,0:T(8,128)(2,1)S(1)}, bf16[4,2,128,128]{3,2,1,0:T(8,128)(2,1)}, u32[]{:S(2)}) %copy-start.3) | copy-done | bytes 262168
  18.2 0.3 level.8.coeffs
  18.5 1.7 %collective-permute-start.1 = (bf16[4,2,128,128]{3,2,1,0:T(8,128)(2,1)S(1)}, bf16[4,2,128,128]{3,2,1,0:T(8,128)(2,1)S(1)}, u32[]{:S(2)}, u32[]{:S(2)}) collective-permute-start(bf16[4,2,128,128]{3,2,1,0:T(8,128)(2,1)S(1)} %level.8.coeffs), channel_id=1, source_target_pairs={{0,16},{8,24},{16,0},{24,8},{32,48},{40,56},{48,32},{56,40},{64,80... | collective-permute-start | bytes 786440 | tf_op jit(solution)/shard_map/ppermute | solution.py:138
  20.2 2.9 %collective-permute-done.9.partner = bf16[4,2,128,128]{3,2,1,0:T(8,128)(2,1)S(1)} collective-permute-done((bf16[4,2,128,128]{3,2,1,0:T(8,128)(2,1)S(1)}, bf16[4,2,128,128]{3,2,1,0:T(8,128)(2,1)S(1)}, u32[]{:S(2)}, u32[]{:S(2)}) %collective-permute-start.9) | collective-permute-done | bytes 262176 | tf_op jit(solution)/shard_map/ppermute | solution.py:138
  23.0 0.3 level.14.coeffs
  23.3 3.8 %collective-permute-start.10 = (bf16[4,2,128,128]{3,2,1,0:T(8,128)(2,1)S(1)}, bf16[4,2,128,128]{3,2,1,0:T(8,128)(2,1)S(1)}, u32[]{:S(2)}, u32[]{:S(2)}) collective-permute-start(bf16[4,2,128,128]{3,2,1,0:T(8,128)(2,1)S(1)} %level.14.coeffs), channel_id=1, source_target_pairs={{0,64},{8,72},{16,80},{24,88},{32,96},{40,104},{48,112},{56,120},{... | collective-permute-start | bytes 786440 | tf_op jit(solution)/shard_map/ppermute | solution.py:138
  27.1 0.0 collective-permute-done.1.partner
  27.1 0.3 level.9.coeffs
  27.4 0.0 copy-start.2
  27.5 1.1 %collective-permute-start.2 = (bf16[4,2,128,128]{3,2,1,0:T(8,128)(2,1)S(1)}, bf16[4,2,128,128]{3,2,1,0:T(8,128)(2,1)S(1)}, u32[]{:S(2)}, u32[]{:S(2)}) collective-permute-start(bf16[4,2,128,128]{3,2,1,0:T(8,128)(2,1)S(1)} %level.9.coeffs), channel_id=1, source_target_pairs={{0,32},{8,40},{16,48},{24,56},{32,0},{40,8},{48,16},{56,24},{64,96... | collective-permute-start | bytes 786440 | tf_op jit(solution)/shard_map/ppermute | solution.py:138
  28.5 5.8 %collective-permute-done.10.partner = bf16[4,2,128,128]{3,2,1,0:T(8,128)(2,1)S(1)} collective-permute-done((bf16[4,2,128,128]{3,2,1,0:T(8,128)(2,1)S(1)}, bf16[4,2,128,128]{3,2,1,0:T(8,128)(2,1)S(1)}, u32[]{:S(2)}, u32[]{:S(2)}) %collective-permute-start.10) | collective-permute-done | bytes 262176 | tf_op jit(solution)/shard_map/ppermute | solution.py:138
  34.4 0.3 level.15
  34.7 3.3 %collective-permute-start.11 = (bf16[4,2,128,128]{3,2,1,0:T(8,128)(2,1)S(1)}, bf16[4,2,128,128]{3,2,1,0:T(8,128)(2,1)S(1)}, u32[]{:S(2)}, u32[]{:S(2)}) collective-permute-start(bf16[4,2,128,128]{3,2,1,0:T(8,128)(2,1)S(1)} %level.15), channel_id=1, source_target_pairs={{0,1},{1,0},{2,3},{3,2},{4,5},{5,4},{6,7},{7,6},{8,9},{9,8},{10,11... | collective-permute-start | bytes 786440 | tf_op jit(solution)/shard_map/ppermute | solution.py:141
  37.9 0.6 collective-permute-done.2.partner
  38.5 0.3 level.10.coeffs
  38.8 3.0 %collective-permute-start.3 = (bf16[4,2,128,128]{3,2,1,0:T(8,128)(2,1)S(1)}, bf16[4,2,128,128]{3,2,1,0:T(8,128)(2,1)S(1)}, u32[]{:S(2)}, u32[]{:S(2)}) collective-permute-start(bf16[4,2,128,128]{3,2,1,0:T(8,128)(2,1)S(1)} %level.10.coeffs), channel_id=1, source_target_pairs={{0,64},{8,72},{16,80},{24,88},{32,96},{40,104},{48,112},{56,120},{... | collective-permute-start | bytes 786440 | tf_op jit(solution)/shard_map/ppermute | solution.py:138
  41.8 0.8 %collective-permute-done.11 = bf16[4,2,128,128]{3,2,1,0:T(8,128)(2,1)S(1)} collective-permute-done((bf16[4,2,128,128]{3,2,1,0:T(8,128)(2,1)S(1)}, bf16[4,2,128,128]{3,2,1,0:T(8,128)(2,1)S(1)}, u32[]{:S(2)}, u32[]{:S(2)}) %collective-permute-start.11) | collective-permute-done | bytes 262176 | tf_op jit(solution)/shard_map/ppermute | solution.py:141
  42.6 2.8 %collective-permute-start.14 = (bf16[2,128,128]{2,1,0:T(8,128)(2,1)S(1)}, bf16[2,128,128]{2,1,0:T(8,128)(2,1)S(1)}, u32[]{:S(2)}, u32[]{:S(2)}) collective-permute-start(bf16[2,128,128]{2,1,0:T(8,128)(2,1)S(1)} %get-tuple-element.13), channel_id=1, source_target_pairs={{0,6},{1,7},{2,4},{3,5},{4,2},{5,3},{6,0},{7,1},{8,14},{9,15},{10,... | collective-permute-start | bytes 196616 | tf_op jit(solution)/shard_map/ppermute | solution.py:143
  45.5 0.8 %collective-permute-start.13 = (bf16[2,128,128]{2,1,0:T(8,128)(2,1)S(1)}, bf16[2,128,128]{2,1,0:T(8,128)(2,1)S(1)}, u32[]{:S(2)}, u32[]{:S(2)}) collective-permute-start(bf16[2,128,128]{2,1,0:T(8,128)(2,1)S(1)} %get-tuple-element.14), channel_id=1, source_target_pairs={{0,4},{1,5},{2,6},{3,7},{4,0},{5,1},{6,2},{7,3},{8,12},{9,13},{10,... | collective-permute-start | bytes 196616 | tf_op jit(solution)/shard_map/ppermute | solution.py:143
  46.3 0.5 collective-permute-start.12
  46.8 0.0 collective-permute-done.3.partner
  46.8 0.3 level.11
  47.1 1.6 %collective-permute-start.4 = (bf16[2,128,128]{2,1,0:T(8,128)(2,1)S(1)}, bf16[2,128,128]{2,1,0:T(8,128)(2,1)S(1)}, u32[]{:S(2)}, u32[]{:S(2)}) collective-permute-start(bf16[2,128,128]{2,1,0:T(8,128)(2,1)S(1)} %get-tuple-element.10), channel_id=1, source_target_pairs={{0,2},{1,3},{2,0},{3,1},{4,6},{5,7},{6,4},{7,5},{8,10},{9,11},{10,... | collective-permute-start | bytes 196616 | tf_op jit(solution)/shard_map/ppermute | solution.py:143
  48.7 2.7 %collective-permute-start.5 = (bf16[2,128,128]{2,1,0:T(8,128)(2,1)S(1)}, bf16[2,128,128]{2,1,0:T(8,128)(2,1)S(1)}, u32[]{:S(2)}, u32[]{:S(2)}) collective-permute-start(bf16[2,128,128]{2,1,0:T(8,128)(2,1)S(1)} %get-tuple-element.11), channel_id=1, source_target_pairs={{0,4},{1,5},{2,6},{3,7},{4,0},{5,1},{6,2},{7,3},{8,12},{9,13},{10,... | collective-permute-start | bytes 196616 | tf_op jit(solution)/shard_map/ppermute | solution.py:143
  51.4 0.0 collective-permute-done.14.c3
  51.4 1.1 %collective-permute-start.6 = (bf16[2,128,128]{2,1,0:T(8,128)(2,1)S(1)}, bf16[2,128,128]{2,1,0:T(8,128)(2,1)S(1)}, u32[]{:S(2)}, u32[]{:S(2)}) collective-permute-start(bf16[2,128,128]{2,1,0:T(8,128)(2,1)S(1)} %get-tuple-element.12), channel_id=1, source_target_pairs={{0,6},{1,7},{2,4},{3,5},{4,2},{5,3},{6,0},{7,1},{8,14},{9,15},{10,... | collective-permute-start | bytes 196616 | tf_op jit(solution)/shard_map/ppermute | solution.py:143
  52.5 0.0 collective-permute-done.13.c2
  52.5 0.0 collective-permute-done.12.c1
  52.5 0.0 copy-done.2
  52.5 2.4 %far_field.2.rest_0_ = bf16[2,16384,128]{2,1,0:T(8,128)(2,1)} custom-call(bf16[2,128,128]{2,1,0:T(8,128)(2,1)S(1)} %get-tuple-element.16.c0, bf16[2,128,128]{2,1,0:T(8,128)(2,1)S(1)} %collective-permute-done.12.c1, bf16[2,128,128]{2,1,0:T(8,128)(2,1)S(1)} %collective-permute-done.13.c2, bf16[2,128,128]{2,1,0:T(8,128)(2,1)S(1)} %collective-permute-done.14.c3, ...), custom_call_target="tpu_custom_call" | custom-call | flops 536870912 | bytes 6291456 | tf_op jit(solution)/shard_map/far_field/pallas_call | solution.py:121
  54.9 0.0 collective-permute-done.4.c1
  54.9 0.0 collective-permute-done.5.c2
  55.0 1.9 %collective-permute-done.6.c3 = bf16[2,128,128]{2,1,0:T(8,128)(2,1)S(1)} collective-permute-done((bf16[2,128,128]{2,1,0:T(8,128)(2,1)S(1)}, bf16[2,128,128]{2,1,0:T(8,128)(2,1)S(1)}, u32[]{:S(2)}, u32[]{:S(2)}) %collective-permute-start.6) | collective-permute-done | bytes 65568 | tf_op jit(solution)/shard_map/ppermute | solution.py:143
  56.9 2.4 %far_field.3 = bf16[2,16384,128]{2,1,0:T(8,128)(2,1)} custom-call(bf16[2,128,128]{2,1,0:T(8,128)(2,1)S(1)} %get-tuple-element.9.c0, bf16[2,128,128]{2,1,0:T(8,128)(2,1)S(1)} %collective-permute-done.4.c1, bf16[2,128,128]{2,1,0:T(8,128)(2,1)S(1)} %collective-permute-done.5.c2, ...), custom_call_target="tpu_custom_call", output_to_operand_aliasing={{}: (5, {})} | custom-call | flops 536870912 | bytes 6291456 | tf_op jit(solution)/shard_map/far_field/pallas_call | solution.py:121
  (5 shorter events, 0.0 us)
Async XLA Ops:
  0.0 5.2 %copy-start.1 = (bf16[4,16,64,128]{3,2,1,0:T(8,128)(2,1)S(1)}, bf16[4,16,64,128]{3,2,1,0:T(8,128)(2,1)}, u32[]{:S(2)}) copy-start(bf16[4,16,64,128]{3,2,1,0:T(8,128)(2,1)} %cross.15) | copy-start | bytes 3145732
  0.0 5.2 %copy-start = (bf16[4,16,64,128]{3,2,1,0:T(8,128)(2,1)S(1)}, bf16[4,16,64,128]{3,2,1,0:T(8,128)(2,1)}, u32[]{:S(2)}) copy-start(bf16[4,16,64,128]{3,2,1,0:T(8,128)(2,1)} %own.15) | copy-start | bytes 3145732
  3.4 1.8 %collective-permute-start.7 = (bf16[4,2,128,128]{3,2,1,0:T(8,128)(2,1)}, bf16[4,2,128,128]{3,2,1,0:T(8,128)(2,1)S(1)}, u32[]{:S(2)}, u32[]{:S(2)}) collective-permute-start(bf16[4,2,128,128]{3,2,1,0:T(8,128)(2,1)} %leaf.3.coeffs), channel_id=1, source_target_pairs={{0,8},{8,0},{16,24},{24,16},{32,40},{40,32},{48,56},{56,48},{64,72... | collective-permute-start | bytes 786440 | tf_op jit(solution)/shard_map/ppermute | solution.py:138
  5.2 1.0 %copy-start.4 = (bf16[4,2,128,128]{3,2,1,0:T(8,128)(2,1)S(1)}, bf16[4,2,128,128]{3,2,1,0:T(8,128)(2,1)}, u32[]{:S(2)}) copy-start(bf16[4,2,128,128]{3,2,1,0:T(8,128)(2,1)} %leaf.3.coeffs) | copy-start | bytes 786436
  6.5 8.4 %collective-permute-start.8 = (bf16[4,2,128,128]{3,2,1,0:T(8,128)(2,1)S(1)}, bf16[4,2,128,128]{3,2,1,0:T(8,128)(2,1)S(1)}, u32[]{:S(2)}, u32[]{:S(2)}) collective-permute-start(bf16[4,2,128,128]{3,2,1,0:T(8,128)(2,1)S(1)} %level.12.coeffs), channel_id=1, source_target_pairs={{0,16},{8,24},{16,0},{24,8},{32,48},{40,56},{48,32},{56,40},{64,80... | collective-permute-start | bytes 786440 | tf_op jit(solution)/shard_map/ppermute | solution.py:138
  11.4 5.9 %collective-permute-start = (bf16[4,2,128,128]{3,2,1,0:T(8,128)(2,1)}, bf16[4,2,128,128]{3,2,1,0:T(8,128)(2,1)S(1)}, u32[]{:S(2)}, u32[]{:S(2)}) collective-permute-start(bf16[4,2,128,128]{3,2,1,0:T(8,128)(2,1)} %leaf.2.coeffs), channel_id=1, source_target_pairs={{0,8},{8,0},{16,24},{24,16},{32,40},{40,32},{48,56},{56,48},{64,72... | collective-permute-start | bytes 786440 | tf_op jit(solution)/shard_map/ppermute | solution.py:138
  15.2 7.9 %collective-permute-start.9 = (bf16[4,2,128,128]{3,2,1,0:T(8,128)(2,1)S(1)}, bf16[4,2,128,128]{3,2,1,0:T(8,128)(2,1)S(1)}, u32[]{:S(2)}, u32[]{:S(2)}) collective-permute-start(bf16[4,2,128,128]{3,2,1,0:T(8,128)(2,1)S(1)} %level.13.coeffs), channel_id=1, source_target_pairs={{0,32},{8,40},{16,48},{24,56},{32,0},{40,8},{48,16},{56,24},{64,96... | collective-permute-start | bytes 786440 | tf_op jit(solution)/shard_map/ppermute | solution.py:138
  17.3 1.0 %copy-start.3 = (bf16[4,2,128,128]{3,2,1,0:T(8,128)(2,1)S(1)}, bf16[4,2,128,128]{3,2,1,0:T(8,128)(2,1)}, u32[]{:S(2)}) copy-start(bf16[4,2,128,128]{3,2,1,0:T(8,128)(2,1)} %leaf.2.coeffs) | copy-start | bytes 786436
  18.5 8.6 %collective-permute-start.1 = (bf16[4,2,128,128]{3,2,1,0:T(8,128)(2,1)S(1)}, bf16[4,2,128,128]{3,2,1,0:T(8,128)(2,1)S(1)}, u32[]{:S(2)}, u32[]{:S(2)}) collective-permute-start(bf16[4,2,128,128]{3,2,1,0:T(8,128)(2,1)S(1)} %level.8.coeffs), channel_id=1, source_target_pairs={{0,16},{8,24},{16,0},{24,8},{32,48},{40,56},{48,32},{56,40},{64,80... | collective-permute-start | bytes 786440 | tf_op jit(solution)/shard_map/ppermute | solution.py:138
  23.3 11.0 %collective-permute-start.10 = (bf16[4,2,128,128]{3,2,1,0:T(8,128)(2,1)S(1)}, bf16[4,2,128,128]{3,2,1,0:T(8,128)(2,1)S(1)}, u32[]{:S(2)}, u32[]{:S(2)}) collective-permute-start(bf16[4,2,128,128]{3,2,1,0:T(8,128)(2,1)S(1)} %level.14.coeffs), channel_id=1, source_target_pairs={{0,64},{8,72},{16,80},{24,88},{32,96},{40,104},{48,112},{56,120},{... | collective-permute-start | bytes 786440 | tf_op jit(solution)/shard_map/ppermute | solution.py:138
  27.4 25.1 %copy-start.2 = (bf16[16,1024,128]{2,1,0:T(8,128)(2,1)S(1)}, bf16[16,1024,128]{2,1,0:T(8,128)(2,1)}, u32[]{:S(2)}) copy-start(bf16[16,1024,128]{2,1,0:T(8,128)(2,1)} %matrices.3) | copy-start | bytes 12582916
  27.5 11.1 %collective-permute-start.2 = (bf16[4,2,128,128]{3,2,1,0:T(8,128)(2,1)S(1)}, bf16[4,2,128,128]{3,2,1,0:T(8,128)(2,1)S(1)}, u32[]{:S(2)}, u32[]{:S(2)}) collective-permute-start(bf16[4,2,128,128]{3,2,1,0:T(8,128)(2,1)S(1)} %level.9.coeffs), channel_id=1, source_target_pairs={{0,32},{8,40},{16,48},{24,56},{32,0},{40,8},{48,16},{56,24},{64,96... | collective-permute-start | bytes 786440 | tf_op jit(solution)/shard_map/ppermute | solution.py:138
  34.7 8.0 %collective-permute-start.11 = (bf16[4,2,128,128]{3,2,1,0:T(8,128)(2,1)S(1)}, bf16[4,2,128,128]{3,2,1,0:T(8,128)(2,1)S(1)}, u32[]{:S(2)}, u32[]{:S(2)}) collective-permute-start(bf16[4,2,128,128]{3,2,1,0:T(8,128)(2,1)S(1)} %level.15), channel_id=1, source_target_pairs={{0,1},{1,0},{2,3},{3,2},{4,5},{5,4},{6,7},{7,6},{8,9},{9,8},{10,11... | collective-permute-start | bytes 786440 | tf_op jit(solution)/shard_map/ppermute | solution.py:141
  38.8 8.0 %collective-permute-start.3 = (bf16[4,2,128,128]{3,2,1,0:T(8,128)(2,1)S(1)}, bf16[4,2,128,128]{3,2,1,0:T(8,128)(2,1)S(1)}, u32[]{:S(2)}, u32[]{:S(2)}) collective-permute-start(bf16[4,2,128,128]{3,2,1,0:T(8,128)(2,1)S(1)} %level.10.coeffs), channel_id=1, source_target_pairs={{0,64},{8,72},{16,80},{24,88},{32,96},{40,104},{48,112},{56,120},{... | collective-permute-start | bytes 786440 | tf_op jit(solution)/shard_map/ppermute | solution.py:138
  42.6 8.8 %collective-permute-start.14 = (bf16[2,128,128]{2,1,0:T(8,128)(2,1)S(1)}, bf16[2,128,128]{2,1,0:T(8,128)(2,1)S(1)}, u32[]{:S(2)}, u32[]{:S(2)}) collective-permute-start(bf16[2,128,128]{2,1,0:T(8,128)(2,1)S(1)} %get-tuple-element.13), channel_id=1, source_target_pairs={{0,6},{1,7},{2,4},{3,5},{4,2},{5,3},{6,0},{7,1},{8,14},{9,15},{10,... | collective-permute-start | bytes 196616 | tf_op jit(solution)/shard_map/ppermute | solution.py:143
  45.5 7.0 %collective-permute-start.13 = (bf16[2,128,128]{2,1,0:T(8,128)(2,1)S(1)}, bf16[2,128,128]{2,1,0:T(8,128)(2,1)S(1)}, u32[]{:S(2)}, u32[]{:S(2)}) collective-permute-start(bf16[2,128,128]{2,1,0:T(8,128)(2,1)S(1)} %get-tuple-element.14), channel_id=1, source_target_pairs={{0,4},{1,5},{2,6},{3,7},{4,0},{5,1},{6,2},{7,3},{8,12},{9,13},{10,... | collective-permute-start | bytes 196616 | tf_op jit(solution)/shard_map/ppermute | solution.py:143
  46.3 6.2 %collective-permute-start.12 = (bf16[2,128,128]{2,1,0:T(8,128)(2,1)S(1)}, bf16[2,128,128]{2,1,0:T(8,128)(2,1)S(1)}, u32[]{:S(2)}, u32[]{:S(2)}) collective-permute-start(bf16[2,128,128]{2,1,0:T(8,128)(2,1)S(1)} %get-tuple-element.15), channel_id=1, source_target_pairs={{0,2},{1,3},{2,0},{3,1},{4,6},{5,7},{6,4},{7,5},{8,10},{9,11},{10,... | collective-permute-start | bytes 196616 | tf_op jit(solution)/shard_map/ppermute | solution.py:143
  47.1 7.8 %collective-permute-start.4 = (bf16[2,128,128]{2,1,0:T(8,128)(2,1)S(1)}, bf16[2,128,128]{2,1,0:T(8,128)(2,1)S(1)}, u32[]{:S(2)}, u32[]{:S(2)}) collective-permute-start(bf16[2,128,128]{2,1,0:T(8,128)(2,1)S(1)} %get-tuple-element.10), channel_id=1, source_target_pairs={{0,2},{1,3},{2,0},{3,1},{4,6},{5,7},{6,4},{7,5},{8,10},{9,11},{10,... | collective-permute-start | bytes 196616 | tf_op jit(solution)/shard_map/ppermute | solution.py:143
  48.7 6.3 %collective-permute-start.5 = (bf16[2,128,128]{2,1,0:T(8,128)(2,1)S(1)}, bf16[2,128,128]{2,1,0:T(8,128)(2,1)S(1)}, u32[]{:S(2)}, u32[]{:S(2)}) collective-permute-start(bf16[2,128,128]{2,1,0:T(8,128)(2,1)S(1)} %get-tuple-element.11), channel_id=1, source_target_pairs={{0,4},{1,5},{2,6},{3,7},{4,0},{5,1},{6,2},{7,3},{8,12},{9,13},{10,... | collective-permute-start | bytes 196616 | tf_op jit(solution)/shard_map/ppermute | solution.py:143
  51.4 5.5 %collective-permute-start.6 = (bf16[2,128,128]{2,1,0:T(8,128)(2,1)S(1)}, bf16[2,128,128]{2,1,0:T(8,128)(2,1)S(1)}, u32[]{:S(2)}, u32[]{:S(2)}) collective-permute-start(bf16[2,128,128]{2,1,0:T(8,128)(2,1)S(1)} %get-tuple-element.12), channel_id=1, source_target_pairs={{0,6},{1,7},{2,4},{3,5},{4,2},{5,3},{6,0},{7,1},{8,14},{9,15},{10,... | collective-permute-start | bytes 196616 | tf_op jit(solution)/shard_map/ppermute | solution.py:143

commit v2 on v1

v2 whole, which is shorter than its diff:
```python
import jax
import jax.numpy as jnp
from jax import lax
from jax.experimental import pallas as pl
from jax.experimental.pallas import tpu as pltpu
from jax.sharding import PartitionSpec as P

F32 = jnp.float32
BF16 = jnp.bfloat16
RANK2 = 128
POINTS = 1024
COLS = 128
MIB = 1024 * 1024
VMEM = pl.BlockSpec(memory_space=pltpu.VMEM)
ANY = pl.BlockSpec(memory_space=pl.ANY)

CHUNKS = {"A": ((0, 1), (1, 1), (2, 1), (3, 1)), "B": ((0, 0), (1, 0), (2, 0), (3, 0))}


def pairs_by(mask, size):
    return [(i, i ^ mask) for i in range(size)]


def place_of(pair):
    return lax.axis_index("tgt") ^ (pair[0] * 2 + pair[1])


def rotated(c):
    half = c.shape[0] // 2
    re, im = c[:half], c[half:]
    return jnp.concatenate([jnp.concatenate([re, -im], axis=0), jnp.concatenate([im, re], axis=0)], axis=1)


def butterfly(own, cross, own_rotated, partner_rotated):
    matrices = jnp.concatenate([own, cross], axis=1)
    operand = jnp.concatenate([own_rotated, partner_rotated], axis=0)
    both = jnp.dot(matrices, operand, preferred_element_type=F32)
    cols = both.shape[1] // 2
    return jnp.concatenate([both[:, :cols], both[:, cols:]], axis=0).astype(BF16)


def coeffs_shape(pairs):
    return jax.ShapeDtypeStruct((len(pairs), 2, RANK2, COLS), BF16)


def leaf(after, project, charges, pairs):
    count = len(pairs)

    def kernel(project, charges, *rest):
        out, rows, points, row_sems, point_sems = rest[-5:]
        loads = []
        for n, pair in enumerate(pairs):
            place = place_of(pair)
            row_load = pltpu.make_async_copy(project.at[pl.ds(place * 2, 2)], rows.at[pl.ds(n * 2, 2)], row_sems.at[n])
            point_load = pltpu.make_async_copy(charges.at[pl.ds(place * 2 * POINTS, 2 * POINTS)], points.at[n], point_sems.at[n])
            row_load.start()
            point_load.start()
            loads.append((row_load, point_load))
        for n, (row_load, point_load) in enumerate(loads):
            row_load.wait()
            point_load.wait()
            for v in range(2):
                block = points[n, v * POINTS : (v + 1) * POINTS, :]
                out[n, v] = jnp.dot(rows[n * 2 + v], block, preferred_element_type=F32).astype(BF16)

    return pl.pallas_call(
        kernel,
        in_specs=[ANY] * (2 + len(after)),
        out_specs=VMEM,
        out_shape=coeffs_shape(pairs),
        scratch_shapes=[
            pltpu.VMEM((count * 2, RANK2, POINTS), BF16),
            pltpu.VMEM((count, 2 * POINTS, COLS), BF16),
            pltpu.SemaphoreType.DMA((count,)),
            pltpu.SemaphoreType.DMA((count,)),
        ],
        compiler_params=pltpu.CompilerParams(vmem_limit_bytes=50 * MIB),
        cost_estimate=pl.CostEstimate(flops=count * 4 * 128 * 128 * 1024, bytes_accessed=count * MIB, transcendentals=0),
        name="leaf",
    )(project, charges, *after)


def level(after, own, cross, coeffs, partner, height, pairs):
    def kernel(own, cross, coeffs, partner, *rest):
        out = rest[-1]
        for n, pair in enumerate(pairs):
            place = place_of(pair)
            for v in range(2):
                m = place * 2 + v
                out[n, v] = butterfly(own[height, m], cross[height, m], rotated(coeffs[n, v]), rotated(partner[n, v]))

    return pl.pallas_call(
        kernel,
        in_specs=[VMEM] * 4 + [ANY] * len(after),
        out_specs=VMEM,
        out_shape=coeffs_shape(pairs),
        compiler_params=pltpu.CompilerParams(vmem_limit_bytes=8 * MIB),
        cost_estimate=pl.CostEstimate(flops=len(pairs) * 4 * 64 * 256 * 256, bytes_accessed=MIB // 2, transcendentals=0),
        name="level",
    )(own, cross, coeffs, partner, *after)


def far_field(so_far, pieces, evaluate):
    count = len(pieces)

    def kernel(*refs):
        arrays, matrices = refs[:count], refs[count]
        out, results, sems = refs[-3:]
        copies = []
        for j, (pair, piece) in enumerate(zip(pieces, arrays)):
            place = place_of(pair)
            for v in range(2):
                n, block = j * 2 + v, place * 2 + v
                turned = rotated(piece[0, v])
                for part in range(4):
                    span = pl.ds(part * (POINTS // 4), POINTS // 4)
                    both = jnp.dot(matrices[block, span, :], turned, preferred_element_type=F32)
                    results[n, 0, span, :] = both[:, :COLS].astype(BF16)
                    results[n, 1, span, :] = both[:, COLS:].astype(BF16)
                for c in range(2):
                    copy = pltpu.make_async_copy(results.at[n, c], out.at[c, pl.ds(block * POINTS, POINTS)], sems.at[n * 2 + c])
                    copy.start()
                    copies.append(copy)
        for copy in copies:
            copy.wait()

    shape = jax.ShapeDtypeStruct((2, 16 * POINTS, COLS), BF16)
    first = so_far.shape != shape.shape
    return pl.pallas_call(
        kernel,
        in_specs=[VMEM] * (count + 1) + [ANY],
        out_specs=ANY,
        out_shape=shape,
        scratch_shapes=[pltpu.VMEM((count * 2, 2, POINTS, COLS), BF16), pltpu.SemaphoreType.DMA((count * 4,))],
        input_output_aliases={} if first else {count + 1: 0},
        compiler_params=pltpu.CompilerParams(vmem_limit_bytes=16 * MIB),
        cost_estimate=pl.CostEstimate(flops=count * 4 * 1024 * 128 * 256, bytes_accessed=count * MIB * 3 // 2, transcendentals=0),
        name="far_field",
    )(*pieces.values(), evaluate, so_far)


def shards(charges, project, own_transfer, cross_transfer, evaluate):
    now, partner, pieces = {}, {}, {}
    after = []

    def proceed(name, new, height):
        after[:] = [new]
        now[name] = new
        if height < 4:
            partner[name] = lax.ppermute(new, "src", pairs_by(1 << height, 16))
        elif CHUNKS[name][0][1]:
            now[name] = lax.ppermute(new, "tgt", pairs_by(1, 8))
        if height == 4:
            for n, (j, b) in enumerate(CHUNKS[name]):
                piece = now[name][n : n + 1]
                pieces[j, b] = lax.ppermute(piece, "tgt", pairs_by(2 * j, 8)) if j else piece

    potential = own_transfer
    for name, stage in ORDER:
        if stage == "leaf":
            proceed(name, leaf(after, project, charges, CHUNKS[name]), 0)
        elif stage == "far":
            potential = far_field(potential, {pair: pieces[pair] for pair in name}, evaluate)
        else:
            new = level(after, own_transfer, cross_transfer, now[name], partner[name], stage, CHUNKS[name])
            proceed(name, new, stage + 1)
    return potential


ORDER = (
    ("A", "leaf"), ("A", 0), ("B", "leaf"), ("A", 1), ("B", 0), ("A", 2), ("B", 1), ("A", 3), ("B", 2), ("B", 3),
    (((0, 1), (1, 1), (2, 1), (3, 1), (0, 0)), "far"), (((1, 0), (3, 0)), "far"), (((2, 0),), "far"),
)


def solution(mesh):
    in_specs = (
        P(("src", "tgt"), None),
        P(("src", "tgt"), None, None),
        P(None, ("src", "tgt"), None, None),
        P(None, ("src", "tgt"), None, None),
        P(("src", "tgt"), None, None),
    )
    out_specs = P(None, ("src", "tgt"), None)
    return jax.shard_map(shards, mesh=mesh, in_specs=in_specs, out_specs=out_specs, check_vma=False)
```

time: 59.5 us -> 55.9 us (0.939)
  local copies, waits for them, and re-layouts: 1.93 us -> 0.05 us
  starting transfers between devices: 26.4 us -> 25.7 us
  Pallas kernels: 13.8 us -> 13.2 us
    unnamed x10 -> x6, local copies, waits for them, and re-layouts: 1.92 us -> 0.01 us
    ppermute x15, starting transfers between devices: 26.4 us -> 25.7 us  [the longest x8 13.5 us: proceed(): partner[name] = lax.ppermute(new, 'src', pairs_by(1 << height, 16))]
    pallas_call x12 -> x13, Pallas kernels: 13.8 us -> 13.2 us  [the longest x3 5.71 us: far_field(): pl.pallas_call(kernel, in_specs=[VMEM] * (count + 1) + [ANY], out_specs=A...]
  transfers between devices with their start and end apart: 15 -> 15, of which waited for: 7 -> 6; matrix products, arithmetic and copies ran while one was open for 0% -> 0% of each run, Pallas kernels for 13% -> 16%
where the time goes in v2:
time: 55.9 us; the launch traced here: 55.8 us
  starting transfers between devices  25.7 us (46%)
  waiting for transfers between devices  16.6 us (30%)
  Pallas kernels  13.2 us (24%)
    ppermute x8, waiting for transfers between devices, proceed(): partner[name] = lax.ppermute(new, 'src', pairs_by(1 << height, 16))  15.8 us
    ppermute x8, starting transfers between devices, proceed(): partner[name] = lax.ppermute(new, 'src', pairs_by(1 << height, 16))  13.5 us
    ppermute x6, starting transfers between devices, proceed(): lax.ppermute(piece, 'tgt', pairs_by(2 * j, 8))  8.95 us
    pallas_call x3, Pallas kernels, far_field(): pl.pallas_call(kernel, in_specs=[VMEM] * (count + 1) + [ANY], out_specs=A...  5.71 us
    pallas_call x2, Pallas kernels, leaf(): pl.pallas_call(kernel, in_specs=[ANY] * (2 + len(after)), out_specs=VMEM,...  5.15 us
    ppermute x1, starting transfers between devices, proceed(): now[name] = lax.ppermute(new, 'tgt', pairs_by(1, 8))  3.27 us
    pallas_call x8, Pallas kernels, level(): pl.pallas_call(kernel, in_specs=[VMEM] * 4 + [ANY] * len(after), out_spec...  2.38 us
  transfers between devices with their start and end apart: 15, of which 6 were waited for; matrix products, arithmetic and copies ran while one was open for 0% of the time, Pallas kernels for 16%

profile of v2, /device:TPU:0, one launch (start us, length us, event | category | flops | bytes accessed | tf_op | source)
XLA Modules:
  0.0 55.8 jit_solution(1704367755558629183)
XLA Ops:
  0.0 0.0 copy-start
  0.0 2.7 %leaf.2.coeffs.rest_0_ = bf16[4,2,128,128]{3,2,1,0:T(8,128)(2,1)S(1)} custom-call(bf16[16,128,1024]{2,1,0:T(8,128)(2,1)} %project.3, bf16[16384,128]{1,0:T(8,128)(2,1)} %charges.3), custom_call_target="tpu_custom_call" | custom-call | flops 268435456 | bytes 4194304 | tf_op jit(solution)/shard_map/leaf/pallas_call | solution.py:66
  2.7 0.1 collective-permute-start
  2.8 1.5 %collective-permute-done.partner = bf16[4,2,128,128]{3,2,1,0:T(8,128)(2,1)S(1)} collective-permute-done((bf16[4,2,128,128]{3,2,1,0:T(8,128)(2,1)S(1)}, bf16[4,2,128,128]{3,2,1,0:T(8,128)(2,1)S(1)}, u32[]{:S(2)}, u32[]{:S(2)}) %collective-permute-start) | collective-permute-done | bytes 262176 | tf_op jit(solution)/shard_map/ppermute | solution.py:150
  4.3 0.0 copy-done
  4.3 0.0 copy-done.1
  4.3 0.3 level.8.rest_0_.coeffs
  4.6 1.7 %collective-permute-start.2 = (bf16[4,2,128,128]{3,2,1,0:T(8,128)(2,1)S(1)}, bf16[4,2,128,128]{3,2,1,0:T(8,128)(2,1)S(1)}, u32[]{:S(2)}, u32[]{:S(2)}) collective-permute-start(bf16[4,2,128,128]{3,2,1,0:T(8,128)(2,1)S(1)} %level.8.rest_0_.coeffs), channel_id=1, source_target_pairs={{0,16},{8,24},{16,0},{24,8},{32,48},{40,56},{48,32},{56,40},{64,80... | collective-permute-start | bytes 786440 | tf_op jit(solution)/shard_map/ppermute | solution.py:150
  6.3 2.5 %leaf.3.rest_0_.coeffs = bf16[4,2,128,128]{3,2,1,0:T(8,128)(2,1)S(1)} custom-call(bf16[16,128,1024]{2,1,0:T(8,128)(2,1)} %project.3, bf16[16384,128]{1,0:T(8,128)(2,1)} %charges.3, bf16[4,2,128,128]{3,2,1,0:T(8,128)(2,1)S(1)} %level.8.rest_0_.coeffs), custom_call_target="tpu_custom_call" | custom-call | flops 268435456 | bytes 4194304 | tf_op jit(solution)/shard_map/leaf/pallas_call | solution.py:66
  8.8 0.1 collective-permute-start.1
  8.9 4.1 %collective-permute-done.2.partner = bf16[4,2,128,128]{3,2,1,0:T(8,128)(2,1)S(1)} collective-permute-done((bf16[4,2,128,128]{3,2,1,0:T(8,128)(2,1)S(1)}, bf16[4,2,128,128]{3,2,1,0:T(8,128)(2,1)S(1)}, u32[]{:S(2)}, u32[]{:S(2)}) %collective-permute-start.2) | collective-permute-done | bytes 262176 | tf_op jit(solution)/shard_map/ppermute | solution.py:150
  13.0 0.3 level.9.rest_0_.coeffs
  13.3 2.1 %collective-permute-start.4 = (bf16[4,2,128,128]{3,2,1,0:T(8,128)(2,1)S(1)}, bf16[4,2,128,128]{3,2,1,0:T(8,128)(2,1)S(1)}, u32[]{:S(2)}, u32[]{:S(2)}) collective-permute-start(bf16[4,2,128,128]{3,2,1,0:T(8,128)(2,1)S(1)} %level.9.rest_0_.coeffs), channel_id=1, source_target_pairs={{0,32},{8,40},{16,48},{24,56},{32,0},{40,8},{48,16},{56,24},{64,96... | collective-permute-start | bytes 786440 | tf_op jit(solution)/shard_map/ppermute | solution.py:150
  15.4 0.0 collective-permute-done.1.partner
  15.4 0.3 level.10.rest_0_.coeffs
  15.7 0.0 copy-start.2
  15.7 1.7 %collective-permute-start.3 = (bf16[4,2,128,128]{3,2,1,0:T(8,128)(2,1)S(1)}, bf16[4,2,128,128]{3,2,1,0:T(8,128)(2,1)S(1)}, u32[]{:S(2)}, u32[]{:S(2)}) collective-permute-start(bf16[4,2,128,128]{3,2,1,0:T(8,128)(2,1)S(1)} %level.10.rest_0_.coeffs), channel_id=1, source_target_pairs={{0,16},{8,24},{16,0},{24,8},{32,48},{40,56},{48,32},{56,40},{64,80... | collective-permute-start | bytes 786440 | tf_op jit(solution)/shard_map/ppermute | solution.py:150
  17.4 3.8 %collective-permute-done.4.partner = bf16[4,2,128,128]{3,2,1,0:T(8,128)(2,1)S(1)} collective-permute-done((bf16[4,2,128,128]{3,2,1,0:T(8,128)(2,1)S(1)}, bf16[4,2,128,128]{3,2,1,0:T(8,128)(2,1)S(1)}, u32[]{:S(2)}, u32[]{:S(2)}) %collective-permute-start.4) | collective-permute-done | bytes 262176 | tf_op jit(solution)/shard_map/ppermute | solution.py:150
  21.2 0.3 level.11.rest_0_.coeffs
  21.5 3.8 %collective-permute-start.6 = (bf16[4,2,128,128]{3,2,1,0:T(8,128)(2,1)S(1)}, bf16[4,2,128,128]{3,2,1,0:T(8,128)(2,1)S(1)}, u32[]{:S(2)}, u32[]{:S(2)}) collective-permute-start(bf16[4,2,128,128]{3,2,1,0:T(8,128)(2,1)S(1)} %level.11.rest_0_.coeffs), channel_id=1, source_target_pairs={{0,64},{8,72},{16,80},{24,88},{32,96},{40,104},{48,112},{56,120},{... | collective-permute-start | bytes 786440 | tf_op jit(solution)/shard_map/ppermute | solution.py:150
  25.3 0.0 collective-permute-done.3.partner
  25.3 0.3 level.12.rest_0_.coeffs
  25.6 1.1 %collective-permute-start.5 = (bf16[4,2,128,128]{3,2,1,0:T(8,128)(2,1)S(1)}, bf16[4,2,128,128]{3,2,1,0:T(8,128)(2,1)S(1)}, u32[]{:S(2)}, u32[]{:S(2)}) collective-permute-start(bf16[4,2,128,128]{3,2,1,0:T(8,128)(2,1)S(1)} %level.12.rest_0_.coeffs), channel_id=1, source_target_pairs={{0,32},{8,40},{16,48},{24,56},{32,0},{40,8},{48,16},{56,24},{64,96... | collective-permute-start | bytes 786440 | tf_op jit(solution)/shard_map/ppermute | solution.py:150
  26.7 5.8 %collective-permute-done.6.partner = bf16[4,2,128,128]{3,2,1,0:T(8,128)(2,1)S(1)} collective-permute-done((bf16[4,2,128,128]{3,2,1,0:T(8,128)(2,1)S(1)}, bf16[4,2,128,128]{3,2,1,0:T(8,128)(2,1)S(1)}, u32[]{:S(2)}, u32[]{:S(2)}) %collective-permute-start.6) | collective-permute-done | bytes 262176 | tf_op jit(solution)/shard_map/ppermute | solution.py:150
  32.5 0.3 level.13.rest_0_
  32.8 3.3 %collective-permute-start.11 = (bf16[4,2,128,128]{3,2,1,0:T(8,128)(2,1)S(1)}, bf16[4,2,128,128]{3,2,1,0:T(8,128)(2,1)S(1)}, u32[]{:S(2)}, u32[]{:S(2)}) collective-permute-start(bf16[4,2,128,128]{3,2,1,0:T(8,128)(2,1)S(1)} %level.13.rest_0_), channel_id=1, source_target_pairs={{0,1},{1,0},{2,3},{3,2},{4,5},{5,4},{6,7},{7,6},{8,9},{9,8},{10,11... | collective-permute-start | bytes 786440 | tf_op jit(solution)/shard_map/ppermute | solution.py:152
  36.1 0.6 %collective-permute-done.5.partner = bf16[4,2,128,128]{3,2,1,0:T(8,128)(2,1)S(1)} collective-permute-done((bf16[4,2,128,128]{3,2,1,0:T(8,128)(2,1)S(1)}, bf16[4,2,128,128]{3,2,1,0:T(8,128)(2,1)S(1)}, u32[]{:S(2)}, u32[]{:S(2)}) %collective-permute-start.5) | collective-permute-done | bytes 262176 | tf_op jit(solution)/shard_map/ppermute | solution.py:150
  36.7 0.3 level.14.coeffs.rest_0_
  37.0 3.0 %collective-permute-start.7 = (bf16[4,2,128,128]{3,2,1,0:T(8,128)(2,1)S(1)}, bf16[4,2,128,128]{3,2,1,0:T(8,128)(2,1)S(1)}, u32[]{:S(2)}, u32[]{:S(2)}) collective-permute-start(bf16[4,2,128,128]{3,2,1,0:T(8,128)(2,1)S(1)} %level.14.coeffs.rest_0_), channel_id=1, source_target_pairs={{0,64},{8,72},{16,80},{24,88},{32,96},{40,104},{48,112},{56,120},{... | collective-permute-start | bytes 786440 | tf_op jit(solution)/shard_map/ppermute | solution.py:150
  40.0 0.8 %collective-permute-done.11 = bf16[4,2,128,128]{3,2,1,0:T(8,128)(2,1)S(1)} collective-permute-done((bf16[4,2,128,128]{3,2,1,0:T(8,128)(2,1)S(1)}, bf16[4,2,128,128]{3,2,1,0:T(8,128)(2,1)S(1)}, u32[]{:S(2)}, u32[]{:S(2)}) %collective-permute-start.11) | collective-permute-done | bytes 262176 | tf_op jit(solution)/shard_map/ppermute | solution.py:152
  40.8 2.8 %collective-permute-start.14 = (bf16[1,2,128,128]{3,2,1,0:T(8,128)(2,1)S(1)}, bf16[1,2,128,128]{3,2,1,0:T(8,128)(2,1)S(1)}, u32[]{:S(2)}, u32[]{:S(2)}) collective-permute-start(bf16[1,2,128,128]{3,2,1,0:T(8,128)(2,1)S(1)} %get-tuple-element.9), channel_id=1, source_target_pairs={{0,6},{1,7},{2,4},{3,5},{4,2},{5,3},{6,0},{7,1},{8,14},{9,15},{10,... | collective-permute-start | bytes 196616 | tf_op jit(solution)/shard_map/ppermute | solution.py:156
  43.6 0.8 %collective-permute-start.13 = (bf16[1,2,128,128]{3,2,1,0:T(8,128)(2,1)S(1)}, bf16[1,2,128,128]{3,2,1,0:T(8,128)(2,1)S(1)}, u32[]{:S(2)}, u32[]{:S(2)}) collective-permute-start(bf16[1,2,128,128]{3,2,1,0:T(8,128)(2,1)S(1)} %get-tuple-element.10), channel_id=1, source_target_pairs={{0,4},{1,5},{2,6},{3,7},{4,0},{5,1},{6,2},{7,3},{8,12},{9,13},{10,... | collective-permute-start | bytes 196616 | tf_op jit(solution)/shard_map/ppermute | solution.py:156
  44.4 0.5 collective-permute-start.12
  45.0 0.0 collective-permute-done.7.partner
  45.0 0.3 level.15
  45.3 2.8 %collective-permute-start.10 = (bf16[1,2,128,128]{3,2,1,0:T(8,128)(2,1)S(1)}, bf16[1,2,128,128]{3,2,1,0:T(8,128)(2,1)S(1)}, u32[]{:S(2)}, u32[]{:S(2)}) collective-permute-start(bf16[1,2,128,128]{3,2,1,0:T(8,128)(2,1)S(1)} %get-tuple-element.6), channel_id=1, source_target_pairs={{0,6},{1,7},{2,4},{3,5},{4,2},{5,3},{6,0},{7,1},{8,14},{9,15},{10,... | collective-permute-start | bytes 196616 | tf_op jit(solution)/shard_map/ppermute | solution.py:156
  48.1 0.3 collective-permute-start.9
  48.4 0.0 collective-permute-done.14.refs_3_
  48.4 1.7 %collective-permute-start.8 = (bf16[1,2,128,128]{3,2,1,0:T(8,128)(2,1)S(1)}, bf16[1,2,128,128]{3,2,1,0:T(8,128)(2,1)S(1)}, u32[]{:S(2)}, u32[]{:S(2)}) collective-permute-start(bf16[1,2,128,128]{3,2,1,0:T(8,128)(2,1)S(1)} %get-tuple-element.8), channel_id=1, source_target_pairs={{0,4},{1,5},{2,6},{3,7},{4,0},{5,1},{6,2},{7,3},{8,12},{9,13},{10,... | collective-permute-start | bytes 196616 | tf_op jit(solution)/shard_map/ppermute | solution.py:156
  50.1 0.0 collective-permute-done.13.refs_2_
  50.1 0.0 collective-permute-done.12.refs_1_
  50.1 0.0 copy-done.2
  50.1 2.8 %far_field.3.refs_3_ = bf16[2,16384,128]{2,1,0:T(8,128)(2,1)} custom-call(bf16[1,2,128,128]{3,2,1,0:T(8,128)(2,1)S(1)} %get-tuple-element.12.refs_0_, bf16[1,2,128,128]{3,2,1,0:T(8,128)(2,1)S(1)} %collective-permute-done.12.refs_1_, bf16[1,2,128,128]{3,2,1,0:T(8,128)(2,1)S(1)} %collective-permute-done.13.refs_2_, ...), custom_call_target="tpu_custom_call" | custom-call | flops 671088640 | bytes 7864320 | tf_op jit(solution)/shard_map/far_field/pallas_call | solution.py:129
  52.9 0.0 collective-permute-done.10.refs_1_
  52.9 0.0 collective-permute-done.9.refs_0_
  52.9 1.7 %far_field.4.refs_2_ = bf16[2,16384,128]{2,1,0:T(8,128)(2,1)} custom-call(bf16[1,2,128,128]{3,2,1,0:T(8,128)(2,1)S(1)} %collective-permute-done.9.refs_0_, bf16[1,2,128,128]{3,2,1,0:T(8,128)(2,1)S(1)} %collective-permute-done.10.refs_1_, bf16[16,1024,128]{2,1,0:T(8,128)(2,1)S(1)} %copy-done.2, ...), custom_call_target="tpu_custom_call", output_to_operand_aliasing={{}: (3, {})} | custom-call | flops 268435456 | bytes 3145728 | tf_op jit(solution)/shard_map/far_field/pallas_call | solution.py:129
  54.5 0.0 collective-permute-done.8.refs_0_
  54.6 1.3 %far_field.5 = bf16[2,16384,128]{2,1,0:T(8,128)(2,1)} custom-call(bf16[1,2,128,128]{3,2,1,0:T(8,128)(2,1)S(1)} %collective-permute-done.8.refs_0_, bf16[16,1024,128]{2,1,0:T(8,128)(2,1)S(1)} %copy-done.2, bf16[2,16384,128]{2,1,0:T(8,128)(2,1)} %far_field.4.refs_2_), custom_call_target="tpu_custom_call", output_to_operand_aliasing={{}: (2, {})} | custom-call | flops 134217728 | bytes 1572864 | tf_op jit(solution)/shard_map/far_field/pallas_call | solution.py:129
  (3 shorter events, 0.0 us)
Async XLA Ops:
  0.0 4.3 %copy-start = (bf16[4,16,64,128]{3,2,1,0:T(8,128)(2,1)S(1)}, bf16[4,16,64,128]{3,2,1,0:T(8,128)(2,1)}, u32[]{:S(2)}) copy-start(bf16[4,16,64,128]{3,2,1,0:T(8,128)(2,1)} %refs_6_.1) | copy-start | bytes 3145732
  0.0 4.3 %copy-start.1 = (bf16[4,16,64,128]{3,2,1,0:T(8,128)(2,1)S(1)}, bf16[4,16,64,128]{3,2,1,0:T(8,128)(2,1)}, u32[]{:S(2)}) copy-start(bf16[4,16,64,128]{3,2,1,0:T(8,128)(2,1)} %cross.15) | copy-start | bytes 3145732
  2.7 1.6 %collective-permute-start = (bf16[4,2,128,128]{3,2,1,0:T(8,128)(2,1)S(1)}, bf16[4,2,128,128]{3,2,1,0:T(8,128)(2,1)S(1)}, u32[]{:S(2)}, u32[]{:S(2)}) collective-permute-start(bf16[4,2,128,128]{3,2,1,0:T(8,128)(2,1)S(1)} %leaf.2.coeffs.rest_0_), channel_id=1, source_target_pairs={{0,8},{8,0},{16,24},{24,16},{32,40},{40,32},{48,56},{56,48},{64,72... | collective-permute-start | bytes 786440 | tf_op jit(solution)/shard_map/ppermute | solution.py:150
  4.6 8.4 %collective-permute-start.2 = (bf16[4,2,128,128]{3,2,1,0:T(8,128)(2,1)S(1)}, bf16[4,2,128,128]{3,2,1,0:T(8,128)(2,1)S(1)}, u32[]{:S(2)}, u32[]{:S(2)}) collective-permute-start(bf16[4,2,128,128]{3,2,1,0:T(8,128)(2,1)S(1)} %level.8.rest_0_.coeffs), channel_id=1, source_target_pairs={{0,16},{8,24},{16,0},{24,8},{32,48},{40,56},{48,32},{56,40},{64,80... | collective-permute-start | bytes 786440 | tf_op jit(solution)/shard_map/ppermute | solution.py:150
  8.8 6.6 %collective-permute-start.1 = (bf16[4,2,128,128]{3,2,1,0:T(8,128)(2,1)S(1)}, bf16[4,2,128,128]{3,2,1,0:T(8,128)(2,1)S(1)}, u32[]{:S(2)}, u32[]{:S(2)}) collective-permute-start(bf16[4,2,128,128]{3,2,1,0:T(8,128)(2,1)S(1)} %leaf.3.rest_0_.coeffs), channel_id=1, source_target_pairs={{0,8},{8,0},{16,24},{24,16},{32,40},{40,32},{48,56},{56,48},{64,72... | collective-permute-start | bytes 786440 | tf_op jit(solution)/shard_map/ppermute | solution.py:150
  13.3 7.9 %collective-permute-start.4 = (bf16[4,2,128,128]{3,2,1,0:T(8,128)(2,1)S(1)}, bf16[4,2,128,128]{3,2,1,0:T(8,128)(2,1)S(1)}, u32[]{:S(2)}, u32[]{:S(2)}) collective-permute-start(bf16[4,2,128,128]{3,2,1,0:T(8,128)(2,1)S(1)} %level.9.rest_0_.coeffs), channel_id=1, source_target_pairs={{0,32},{8,40},{16,48},{24,56},{32,0},{40,8},{48,16},{56,24},{64,96... | collective-permute-start | bytes 786440 | tf_op jit(solution)/shard_map/ppermute | solution.py:150
  15.7 34.4 %copy-start.2 = (bf16[16,1024,128]{2,1,0:T(8,128)(2,1)S(1)}, bf16[16,1024,128]{2,1,0:T(8,128)(2,1)}, u32[]{:S(2)}) copy-start(bf16[16,1024,128]{2,1,0:T(8,128)(2,1)} %refs_1_.1) | copy-start | bytes 12582916
  15.7 9.5 %collective-permute-start.3 = (bf16[4,2,128,128]{3,2,1,0:T(8,128)(2,1)S(1)}, bf16[4,2,128,128]{3,2,1,0:T(8,128)(2,1)S(1)}, u32[]{:S(2)}, u32[]{:S(2)}) collective-permute-start(bf16[4,2,128,128]{3,2,1,0:T(8,128)(2,1)S(1)} %level.10.rest_0_.coeffs), channel_id=1, source_target_pairs={{0,16},{8,24},{16,0},{24,8},{32,48},{40,56},{48,32},{56,40},{64,80... | collective-permute-start | bytes 786440 | tf_op jit(solution)/shard_map/ppermute | solution.py:150
  21.5 11.0 %collective-permute-start.6 = (bf16[4,2,128,128]{3,2,1,0:T(8,128)(2,1)S(1)}, bf16[4,2,128,128]{3,2,1,0:T(8,128)(2,1)S(1)}, u32[]{:S(2)}, u32[]{:S(2)}) collective-permute-start(bf16[4,2,128,128]{3,2,1,0:T(8,128)(2,1)S(1)} %level.11.rest_0_.coeffs), channel_id=1, source_target_pairs={{0,64},{8,72},{16,80},{24,88},{32,96},{40,104},{48,112},{56,120},{... | collective-permute-start | bytes 786440 | tf_op jit(solution)/shard_map/ppermute | solution.py:150
  25.6 11.1 %collective-permute-start.5 = (bf16[4,2,128,128]{3,2,1,0:T(8,128)(2,1)S(1)}, bf16[4,2,128,128]{3,2,1,0:T(8,128)(2,1)S(1)}, u32[]{:S(2)}, u32[]{:S(2)}) collective-permute-start(bf16[4,2,128,128]{3,2,1,0:T(8,128)(2,1)S(1)} %level.12.rest_0_.coeffs), channel_id=1, source_target_pairs={{0,32},{8,40},{16,48},{24,56},{32,0},{40,8},{48,16},{56,24},{64,96... | collective-permute-start | bytes 786440 | tf_op jit(solution)/shard_map/ppermute | solution.py:150
  32.8 8.0 %collective-permute-start.11 = (bf16[4,2,128,128]{3,2,1,0:T(8,128)(2,1)S(1)}, bf16[4,2,128,128]{3,2,1,0:T(8,128)(2,1)S(1)}, u32[]{:S(2)}, u32[]{:S(2)}) collective-permute-start(bf16[4,2,128,128]{3,2,1,0:T(8,128)(2,1)S(1)} %level.13.rest_0_), channel_id=1, source_target_pairs={{0,1},{1,0},{2,3},{3,2},{4,5},{5,4},{6,7},{7,6},{8,9},{9,8},{10,11... | collective-permute-start | bytes 786440 | tf_op jit(solution)/shard_map/ppermute | solution.py:152
  37.0 8.0 %collective-permute-start.7 = (bf16[4,2,128,128]{3,2,1,0:T(8,128)(2,1)S(1)}, bf16[4,2,128,128]{3,2,1,0:T(8,128)(2,1)S(1)}, u32[]{:S(2)}, u32[]{:S(2)}) collective-permute-start(bf16[4,2,128,128]{3,2,1,0:T(8,128)(2,1)S(1)} %level.14.coeffs.rest_0_), channel_id=1, source_target_pairs={{0,64},{8,72},{16,80},{24,88},{32,96},{40,104},{48,112},{56,120},{... | collective-permute-start | bytes 786440 | tf_op jit(solution)/shard_map/ppermute | solution.py:150
  40.8 7.6 %collective-permute-start.14 = (bf16[1,2,128,128]{3,2,1,0:T(8,128)(2,1)S(1)}, bf16[1,2,128,128]{3,2,1,0:T(8,128)(2,1)S(1)}, u32[]{:S(2)}, u32[]{:S(2)}) collective-permute-start(bf16[1,2,128,128]{3,2,1,0:T(8,128)(2,1)S(1)} %get-tuple-element.9), channel_id=1, source_target_pairs={{0,6},{1,7},{2,4},{3,5},{4,2},{5,3},{6,0},{7,1},{8,14},{9,15},{10,... | collective-permute-start | bytes 196616 | tf_op jit(solution)/shard_map/ppermute | solution.py:156
  43.6 6.5 %collective-permute-start.13 = (bf16[1,2,128,128]{3,2,1,0:T(8,128)(2,1)S(1)}, bf16[1,2,128,128]{3,2,1,0:T(8,128)(2,1)S(1)}, u32[]{:S(2)}, u32[]{:S(2)}) collective-permute-start(bf16[1,2,128,128]{3,2,1,0:T(8,128)(2,1)S(1)} %get-tuple-element.10), channel_id=1, source_target_pairs={{0,4},{1,5},{2,6},{3,7},{4,0},{5,1},{6,2},{7,3},{8,12},{9,13},{10,... | collective-permute-start | bytes 196616 | tf_op jit(solution)/shard_map/ppermute | solution.py:156
  44.4 5.7 %collective-permute-start.12 = (bf16[1,2,128,128]{3,2,1,0:T(8,128)(2,1)S(1)}, bf16[1,2,128,128]{3,2,1,0:T(8,128)(2,1)S(1)}, u32[]{:S(2)}, u32[]{:S(2)}) collective-permute-start(bf16[1,2,128,128]{3,2,1,0:T(8,128)(2,1)S(1)} %get-tuple-element.11), channel_id=1, source_target_pairs={{0,2},{1,3},{2,0},{3,1},{4,6},{5,7},{6,4},{7,5},{8,10},{9,11},{10,... | collective-permute-start | bytes 196616 | tf_op jit(solution)/shard_map/ppermute | solution.py:156
  45.3 7.6 %collective-permute-start.10 = (bf16[1,2,128,128]{3,2,1,0:T(8,128)(2,1)S(1)}, bf16[1,2,128,128]{3,2,1,0:T(8,128)(2,1)S(1)}, u32[]{:S(2)}, u32[]{:S(2)}) collective-permute-start(bf16[1,2,128,128]{3,2,1,0:T(8,128)(2,1)S(1)} %get-tuple-element.6), channel_id=1, source_target_pairs={{0,6},{1,7},{2,4},{3,5},{4,2},{5,3},{6,0},{7,1},{8,14},{9,15},{10,... | collective-permute-start | bytes 196616 | tf_op jit(solution)/shard_map/ppermute | solution.py:156
  48.1 4.7 %collective-permute-start.9 = (bf16[1,2,128,128]{3,2,1,0:T(8,128)(2,1)S(1)}, bf16[1,2,128,128]{3,2,1,0:T(8,128)(2,1)S(1)}, u32[]{:S(2)}, u32[]{:S(2)}) collective-permute-start(bf16[1,2,128,128]{3,2,1,0:T(8,128)(2,1)S(1)} %get-tuple-element.7), channel_id=1, source_target_pairs={{0,2},{1,3},{2,0},{3,1},{4,6},{5,7},{6,4},{7,5},{8,10},{9,11},{10,... | collective-permute-start | bytes 196616 | tf_op jit(solution)/shard_map/ppermute | solution.py:156
  48.4 6.2 %collective-permute-start.8 = (bf16[1,2,128,128]{3,2,1,0:T(8,128)(2,1)S(1)}, bf16[1,2,128,128]{3,2,1,0:T(8,128)(2,1)S(1)}, u32[]{:S(2)}, u32[]{:S(2)}) collective-permute-start(bf16[1,2,128,128]{3,2,1,0:T(8,128)(2,1)S(1)} %get-tuple-element.8), channel_id=1, source_target_pairs={{0,4},{1,5},{2,6},{3,7},{4,0},{5,1},{6,2},{7,3},{8,12},{9,13},{10,... | collective-permute-start | bytes 196616 | tf_op jit(solution)/shard_map/ppermute | solution.py:156

commit v3 on v2

--- a/solution.py
+++ b/solution.py
@@ -14,7 +14,7 @@
 VMEM = pl.BlockSpec(memory_space=pltpu.VMEM)
 ANY = pl.BlockSpec(memory_space=pl.ANY)
 
-CHUNKS = {"A": ((0, 1), (1, 1), (2, 1), (3, 1)), "B": ((0, 0), (1, 0), (2, 0), (3, 0))}
+CHUNKS = {"A": ((0, 1), (1, 1)), "B": ((2, 1), (3, 1)), "C": ((0, 0), (1, 0), (2, 0), (3, 0))}
 
 
 def pairs_by(mask, size):
@@ -43,11 +43,12 @@
     return jax.ShapeDtypeStruct((len(pairs), 2, RANK2, COLS), BF16)
 
 
-def leaf(after, project, charges, pairs):
+def leaf(after, project, charges, pairs, outs):
     count = len(pairs)
+    each = count // outs
 
     def kernel(project, charges, *rest):
-        out, rows, points, row_sems, point_sems = rest[-5:]
+        outputs, (rows, points, row_sems, point_sems) = rest[len(after) : -4], rest[-4:]
         loads = []
         for n, pair in enumerate(pairs):
             place = place_of(pair)
@@ -61,13 +62,13 @@
             point_load.wait()
             for v in range(2):
                 block = points[n, v * POINTS : (v + 1) * POINTS, :]
-                out[n, v] = jnp.dot(rows[n * 2 + v], block, preferred_element_type=F32).astype(BF16)
+                outputs[n // each][n % each, v] = jnp.dot(rows[n * 2 + v], block, preferred_element_type=F32).astype(BF16)
 
     return pl.pallas_call(
         kernel,
         in_specs=[ANY] * (2 + len(after)),
-        out_specs=VMEM,
-        out_shape=coeffs_shape(pairs),
+        out_specs=[VMEM] * outs,
+        out_shape=[coeffs_shape(pairs[:each])] * outs,
         scratch_shapes=[
             pltpu.VMEM((count * 2, RANK2, POINTS), BF16),
             pltpu.VMEM((count, 2 * POINTS, COLS), BF16),
@@ -80,24 +81,29 @@
     )(project, charges, *after)
 
 
-def level(after, own, cross, coeffs, partner, height, pairs):
-    def kernel(own, cross, coeffs, partner, *rest):
-        out = rest[-1]
+def level(after, own, cross, coeffs, partners, height, pairs, outs):
+    parts = len(coeffs)
+    each, out_each = len(pairs) // parts, len(pairs) // outs
+
+    def kernel(own, cross, *rest):
+        coeffs, partners, outputs = rest[:parts], rest[parts : 2 * parts], rest[2 * parts + len(after) :]
         for n, pair in enumerate(pairs):
             place = place_of(pair)
             for v in range(2):
                 m = place * 2 + v
-                out[n, v] = butterfly(own[height, m], cross[height, m], rotated(coeffs[n, v]), rotated(partner[n, v]))
+                mine, theirs = coeffs[n // each][n % each, v], partners[n // each][n % each, v]
+                new = butterfly(own[height, m], cross[height, m], rotated(mine), rotated(theirs))
+                outputs[n // out_each][n % out_each, v] = new
 
     return pl.pallas_call(
         kernel,
-        in_specs=[VMEM] * 4 + [ANY] * len(after),
-        out_specs=VMEM,
-        out_shape=coeffs_shape(pairs),
+        in_specs=[VMEM] * (2 + 2 * parts) + [ANY] * len(after),
+        out_specs=[VMEM] * outs,
+        out_shape=[coeffs_shape(pairs[:out_each])] * outs,
         compiler_params=pltpu.CompilerParams(vmem_limit_bytes=8 * MIB),
         cost_estimate=pl.CostEstimate(flops=len(pairs) * 4 * 64 * 256 * 256, bytes_accessed=MIB // 2, transcendentals=0),
         name="level",
-    )(own, cross, coeffs, partner, *after)
+    )(own, cross, *coeffs, *partners, *after)
 
 
 def far_field(so_far, pieces, evaluate):
@@ -143,34 +149,35 @@
     now, partner, pieces = {}, {}, {}
     after = []
 
-    def proceed(name, new, height):
-        after[:] = [new]
+    def proceed(name, height, new):
+        after[:] = new[:1]
         now[name] = new
-        if height < 4:
-            partner[name] = lax.ppermute(new, "src", pairs_by(1 << height, 16))
-        elif CHUNKS[name][0][1]:
-            now[name] = lax.ppermute(new, "tgt", pairs_by(1, 8))
-        if height == 4:
+        partner[name] = [lax.ppermute(part, "src", pairs_by(1 << height, 16)) for part in new]
+
+    for name, stage, outs in ORDER:
+        if stage == "leaf":
+            proceed(name, 0, leaf(after, project, charges, CHUNKS[name], outs))
+        elif stage < 3:
+            new = level(after, own_transfer, cross_transfer, now[name], partner[name], stage, CHUNKS[name], outs)
+            proceed(name, stage + 1, new)
+        else:
+            (new,) = level(after, own_transfer, cross_transfer, now[name], partner[name], stage, CHUNKS[name], 1)
+            after[:] = [new]
+            if CHUNKS[name][0][1]:
+                new = lax.ppermute(new, "tgt", pairs_by(1, 8))
             for n, (j, b) in enumerate(CHUNKS[name]):
-                piece = now[name][n : n + 1]
+                piece = new[n : n + 1]
                 pieces[j, b] = lax.ppermute(piece, "tgt", pairs_by(2 * j, 8)) if j else piece
-
     potential = own_transfer
-    for name, stage in ORDER:
-        if stage == "leaf":
-            proceed(name, leaf(after, project, charges, CHUNKS[name]), 0)
-        elif stage == "far":
-            potential = far_field(potential, {pair: pieces[pair] for pair in name}, evaluate)
-        else:
-            new = level(after, own_transfer, cross_transfer, now[name], partner[name], stage, CHUNKS[name])
-            proceed(name, new, stage + 1)
+    for group in FAR:
+        potential = far_field(potential, {pair: pieces[pair] for pair in group}, evaluate)
     return potential
 
 
 ORDER = (
-    ("A", "leaf"), ("A", 0), ("B", "leaf"), ("A", 1), ("B", 0), ("A", 2), ("B", 1), ("A", 3), ("B", 2), ("B", 3),
-    (((0, 1), (1, 1), (2, 1), (3, 1), (0, 0)), "far"), (((1, 0), (3, 0)), "far"), (((2, 0),), "far"),
+    ("A", "leaf", 1), ("B", "leaf", 1), ("A", 0, 1), ("B", 0, 1), ("C", "leaf", 2), ("A", 1, 1), ("B", 1, 1), ("C", 0, 2), ("A", 2, 1), ("B", 2, 1), ("C", 1, 2), ("A", 3, 1), ("B", 3, 1), ("C", 2, 1), ("C", 3, 1),
 )
+FAR = (((0, 1), (1, 1), (2, 1), (3, 1), (0, 0)), ((1, 0), (3, 0)), ((2, 0),))
 
 
 def solution(mesh):

time: 55.9 us -> 53.5 us (0.957)
  waiting for transfers between devices: 16.6 us -> 4.19 us
  starting transfers between devices: 25.7 us -> 33.9 us
  Pallas kernels: 13.2 us -> 14.9 us
    ppermute x15 -> x23, waiting for transfers between devices: 16.6 us -> 4.19 us  [the longest x15 3.99 us: proceed(): lax.ppermute(part, 'src', pairs_by(1 << height, 16))]
    ppermute x15 -> x23, starting transfers between devices: 25.7 us -> 33.9 us  [the longest x15 20.9 us: proceed(): lax.ppermute(part, 'src', pairs_by(1 << height, 16))]
    pallas_call x10 -> x15, Pallas kernels: 7.53 us -> 9.19 us  [the longest x3 6.34 us: leaf(): pl.pallas_call(kernel, in_specs=[ANY] * (2 + len(after)), out_specs=[VMEM...]
  transfers between devices with their start and end apart: 15 -> 23, of which waited for: 6 -> 4; matrix products, arithmetic and copies ran while one was open for 0% -> 0% of each run, Pallas kernels for 16% -> 22%
where the time goes in v3:
time: 53.5 us; the launch traced here: 53.4 us
  starting transfers between devices  33.9 us (63%)
  Pallas kernels  14.9 us (28%)
  waiting for transfers between devices  4.19 us (8%)
    ppermute x15, starting transfers between devices, proceed(): lax.ppermute(part, 'src', pairs_by(1 << height, 16))  20.9 us
    ppermute x6, starting transfers between devices, shards(): lax.ppermute(piece, 'tgt', pairs_by(2 * j, 8))  9.39 us
    pallas_call x3, Pallas kernels, leaf(): pl.pallas_call(kernel, in_specs=[ANY] * (2 + len(after)), out_specs=[VMEM...  6.34 us
    pallas_call x3, Pallas kernels, far_field(): pl.pallas_call(kernel, in_specs=[VMEM] * (count + 1) + [ANY], out_specs=A...  5.71 us
    ppermute x15, waiting for transfers between devices, proceed(): lax.ppermute(part, 'src', pairs_by(1 << height, 16))  3.99 us
    ppermute x2, starting transfers between devices, shards(): new = lax.ppermute(new, 'tgt', pairs_by(1, 8))  3.61 us
    pallas_call x12, Pallas kernels, level(): pl.pallas_call(kernel, in_specs=[VMEM] * (2 + 2 * parts) + [ANY] * len(af...  2.85 us
  transfers between devices with their start and end apart: 23, of which 4 were waited for; matrix products, arithmetic and copies ran while one was open for 0% of the time, Pallas kernels for 22%

profile of v3, /device:TPU:0, one launch (start us, length us, event | category | flops | bytes accessed | tf_op | source)
XLA Modules:
  0.0 53.4 jit_solution(5793164166182915294)
XLA Ops:
  0.0 2.0 %leaf.3.rest_0_ = bf16[2,2,128,128]{3,2,1,0:T(8,128)(2,1)S(1)} custom-call(bf16[16,128,1024]{2,1,0:T(8,128)(2,1)} %project.5, bf16[16384,128]{1,0:T(8,128)(2,1)} %charges.5), custom_call_target="tpu_custom_call" | custom-call | flops 134217728 | bytes 2097152 | tf_op jit(solution)/shard_map/leaf/pallas_call | solution.py:67
  2.0 0.1 collective-permute-start.1
  2.1 1.8 %leaf.4.rest_2_.rest_0_ = bf16[2,2,128,128]{3,2,1,0:T(8,128)(2,1)S(1)} custom-call(bf16[16,128,1024]{2,1,0:T(8,128)(2,1)} %project.5, bf16[16384,128]{1,0:T(8,128)(2,1)} %charges.5, bf16[2,2,128,128]{3,2,1,0:T(8,128)(2,1)S(1)} %leaf.3.rest_0_), custom_call_target="tpu_custom_call" | custom-call | flops 134217728 | bytes 2097152 | tf_op jit(solution)/shard_map/leaf/pallas_call | solution.py:67
  3.9 0.6 %collective-permute-start = (bf16[2,2,128,128]{3,2,1,0:T(8,128)(2,1)S(1)}, bf16[2,2,128,128]{3,2,1,0:T(8,128)(2,1)S(1)}, u32[]{:S(2)}, u32[]{:S(2)}) collective-permute-start(bf16[2,2,128,128]{3,2,1,0:T(8,128)(2,1)S(1)} %leaf.4.rest_2_.rest_0_), channel_id=1, source_target_pairs={{0,8},{8,0},{16,24},{24,16},{32,40},{40,32},{48,56},{56,48},{64,72... | collective-permute-start | bytes 393224 | tf_op jit(solution)/shard_map/ppermute | solution.py:155
  4.5 0.0 collective-permute-done.1.rest_1_
  4.5 0.2 level.12.rest_2_.rest_0_
  4.7 1.7 %collective-permute-start.5 = (bf16[2,2,128,128]{3,2,1,0:T(8,128)(2,1)S(1)}, bf16[2,2,128,128]{3,2,1,0:T(8,128)(2,1)S(1)}, u32[]{:S(2)}, u32[]{:S(2)}) collective-permute-start(bf16[2,2,128,128]{3,2,1,0:T(8,128)(2,1)S(1)} %level.12.rest_2_.rest_0_), channel_id=1, source_target_pairs={{0,16},{8,24},{16,0},{24,8},{32,48},{40,56},{48,32},{56,40},{64,80... | collective-permute-start | bytes 393224 | tf_op jit(solution)/shard_map/ppermute | solution.py:155
  6.5 0.2 level.13.rest_0_
  6.7 0.8 %collective-permute-start.4 = (bf16[2,2,128,128]{3,2,1,0:T(8,128)(2,1)S(1)}, bf16[2,2,128,128]{3,2,1,0:T(8,128)(2,1)S(1)}, u32[]{:S(2)}, u32[]{:S(2)}) collective-permute-start(bf16[2,2,128,128]{3,2,1,0:T(8,128)(2,1)S(1)} %level.13.rest_0_), channel_id=1, source_target_pairs={{0,16},{8,24},{16,0},{24,8},{32,48},{40,56},{48,32},{56,40},{64,80... | collective-permute-start | bytes 393224 | tf_op jit(solution)/shard_map/ppermute | solution.py:155
  7.5 2.5 %leaf.5 = (bf16[2,2,128,128]{3,2,1,0:T(8,128)(2,1)S(1)}, bf16[2,2,128,128]{3,2,1,0:T(8,128)(2,1)S(1)}) custom-call(bf16[16,128,1024]{2,1,0:T(8,128)(2,1)} %project.5, bf16[16384,128]{1,0:T(8,128)(2,1)} %charges.5, bf16[2,2,128,128]{3,2,1,0:T(8,128)(2,1)S(1)} %level.13.rest_0_), custom_call_target="tpu_custom_call" | custom-call | flops 268435456 | bytes 4194304 | tf_op jit(solution)/shard_map/leaf/pallas_call | solution.py:67
  10.0 0.1 collective-permute-start.3
  10.1 0.4 collective-permute-start.2
  10.6 0.6 %collective-permute-done.5.rest_1_ = bf16[2,2,128,128]{3,2,1,0:T(8,128)(2,1)S(1)} collective-permute-done((bf16[2,2,128,128]{3,2,1,0:T(8,128)(2,1)S(1)}, bf16[2,2,128,128]{3,2,1,0:T(8,128)(2,1)S(1)}, u32[]{:S(2)}, u32[]{:S(2)}) %collective-permute-start.5) | collective-permute-done | bytes 131104 | tf_op jit(solution)/shard_map/ppermute | solution.py:155
  11.2 0.2 level.14.rest_2_.rest_0_
  11.4 2.1 %collective-permute-start.9 = (bf16[2,2,128,128]{3,2,1,0:T(8,128)(2,1)S(1)}, bf16[2,2,128,128]{3,2,1,0:T(8,128)(2,1)S(1)}, u32[]{:S(2)}, u32[]{:S(2)}) collective-permute-start(bf16[2,2,128,128]{3,2,1,0:T(8,128)(2,1)S(1)} %level.14.rest_2_.rest_0_), channel_id=1, source_target_pairs={{0,32},{8,40},{16,48},{24,56},{32,0},{40,8},{48,16},{56,24},{64,96... | collective-permute-start | bytes 393224 | tf_op jit(solution)/shard_map/ppermute | solution.py:155
  13.5 0.0 collective-permute-done.4.rest_1_
  13.5 0.2 level.15.rest_4_.rest_0_
  13.7 1.7 %collective-permute-start.8 = (bf16[2,2,128,128]{3,2,1,0:T(8,128)(2,1)S(1)}, bf16[2,2,128,128]{3,2,1,0:T(8,128)(2,1)S(1)}, u32[]{:S(2)}, u32[]{:S(2)}) collective-permute-start(bf16[2,2,128,128]{3,2,1,0:T(8,128)(2,1)S(1)} %level.15.rest_4_.rest_0_), channel_id=1, source_target_pairs={{0,32},{8,40},{16,48},{24,56},{32,0},{40,8},{48,16},{56,24},{64,96... | collective-permute-start | bytes 393224 | tf_op jit(solution)/shard_map/ppermute | solution.py:155
  15.4 0.3 level.16
  15.7 1.7 %collective-permute-start.7 = (bf16[2,2,128,128]{3,2,1,0:T(8,128)(2,1)S(1)}, bf16[2,2,128,128]{3,2,1,0:T(8,128)(2,1)S(1)}, u32[]{:S(2)}, u32[]{:S(2)}) collective-permute-start(bf16[2,2,128,128]{3,2,1,0:T(8,128)(2,1)S(1)} %get-tuple-element.14.rest_1_), channel_id=1, source_target_pairs={{0,16},{8,24},{16,0},{24,8},{32,48},{40,56},{48,32},{56,40},{64,80... | collective-permute-start | bytes 393224 | tf_op jit(solution)/shard_map/ppermute | solution.py:155
  17.3 0.5 collective-permute-start.6
  17.8 0.2 level.17.rest_2_.rest_0_
  18.0 0.0 copy-start.2
  18.0 4.0 %collective-permute-start.13 = (bf16[2,2,128,128]{3,2,1,0:T(8,128)(2,1)S(1)}, bf16[2,2,128,128]{3,2,1,0:T(8,128)(2,1)S(1)}, u32[]{:S(2)}, u32[]{:S(2)}) collective-permute-start(bf16[2,2,128,128]{3,2,1,0:T(8,128)(2,1)S(1)} %level.17.rest_2_.rest_0_), channel_id=1, source_target_pairs={{0,64},{8,72},{16,80},{24,88},{32,96},{40,104},{48,112},{56,120},{... | collective-permute-start | bytes 393224 | tf_op jit(solution)/shard_map/ppermute | solution.py:155
  22.0 0.2 level.18.rest_4_.rest_0_
  22.2 2.6 %collective-permute-start.12 = (bf16[2,2,128,128]{3,2,1,0:T(8,128)(2,1)S(1)}, bf16[2,2,128,128]{3,2,1,0:T(8,128)(2,1)S(1)}, u32[]{:S(2)}, u32[]{:S(2)}) collective-permute-start(bf16[2,2,128,128]{3,2,1,0:T(8,128)(2,1)S(1)} %level.18.rest_4_.rest_0_), channel_id=1, source_target_pairs={{0,64},{8,72},{16,80},{24,88},{32,96},{40,104},{48,112},{56,120},{... | collective-permute-start | bytes 393224 | tf_op jit(solution)/shard_map/ppermute | solution.py:155
  24.8 0.3 level.19
  25.1 1.1 %collective-permute-start.11 = (bf16[2,2,128,128]{3,2,1,0:T(8,128)(2,1)S(1)}, bf16[2,2,128,128]{3,2,1,0:T(8,128)(2,1)S(1)}, u32[]{:S(2)}, u32[]{:S(2)}) collective-permute-start(bf16[2,2,128,128]{3,2,1,0:T(8,128)(2,1)S(1)} %get-tuple-element.16.rest_1_), channel_id=1, source_target_pairs={{0,32},{8,40},{16,48},{24,56},{32,0},{40,8},{48,16},{56,24},{64,96... | collective-permute-start | bytes 393224 | tf_op jit(solution)/shard_map/ppermute | solution.py:155
  26.2 1.0 %collective-permute-start.10 = (bf16[2,2,128,128]{3,2,1,0:T(8,128)(2,1)S(1)}, bf16[2,2,128,128]{3,2,1,0:T(8,128)(2,1)S(1)}, u32[]{:S(2)}, u32[]{:S(2)}) collective-permute-start(bf16[2,2,128,128]{3,2,1,0:T(8,128)(2,1)S(1)} %get-tuple-element.15.rest_2_.rest_0_), channel_id=1, source_target_pairs={{0,32},{8,40},{16,48},{24,56},{32,0},{40,8},{48,16},{56,24},{64,96... | collective-permute-start | bytes 393224 | tf_op jit(solution)/shard_map/ppermute | solution.py:155
  27.2 0.2 level.20.rest_2_
  27.4 2.8 %collective-permute-done.12.rest_1_ = bf16[2,2,128,128]{3,2,1,0:T(8,128)(2,1)S(1)} collective-permute-done((bf16[2,2,128,128]{3,2,1,0:T(8,128)(2,1)S(1)}, bf16[2,2,128,128]{3,2,1,0:T(8,128)(2,1)S(1)}, u32[]{:S(2)}, u32[]{:S(2)}) %collective-permute-start.12) | collective-permute-done | bytes 131104 | tf_op jit(solution)/shard_map/ppermute | solution.py:155
  30.2 0.2 level.21.rest_4_
  30.5 3.3 %collective-permute-start.20 = (bf16[2,2,128,128]{3,2,1,0:T(8,128)(2,1)S(1)}, bf16[2,2,128,128]{3,2,1,0:T(8,128)(2,1)S(1)}, u32[]{:S(2)}, u32[]{:S(2)}) collective-permute-start(bf16[2,2,128,128]{3,2,1,0:T(8,128)(2,1)S(1)} %level.21.rest_4_), channel_id=1, source_target_pairs={{0,1},{1,0},{2,3},{3,2},{4,5},{5,4},{6,7},{7,6},{8,9},{9,8},{10,11... | collective-permute-start | bytes 393224 | tf_op jit(solution)/shard_map/ppermute | solution.py:167
  33.7 0.3 collective-permute-start.18
  34.1 0.3 level.22.rest_0_.rest_2_
  34.4 2.6 %collective-permute-start.14 = (bf16[4,2,128,128]{3,2,1,0:T(8,128)(2,1)S(1)}, bf16[4,2,128,128]{3,2,1,0:T(8,128)(2,1)S(1)}, u32[]{:S(2)}, u32[]{:S(2)}) collective-permute-start(bf16[4,2,128,128]{3,2,1,0:T(8,128)(2,1)S(1)} %level.22.rest_0_.rest_2_), channel_id=1, source_target_pairs={{0,64},{8,72},{16,80},{24,88},{32,96},{40,104},{48,112},{56,120},{... | collective-permute-start | bytes 786440 | tf_op jit(solution)/shard_map/ppermute | solution.py:155
  37.0 0.2 collective-permute-done.20
  37.2 2.8 %collective-permute-start.22 = (bf16[1,2,128,128]{3,2,1,0:T(8,128)(2,1)S(1)}, bf16[1,2,128,128]{3,2,1,0:T(8,128)(2,1)S(1)}, u32[]{:S(2)}, u32[]{:S(2)}) collective-permute-start(bf16[1,2,128,128]{3,2,1,0:T(8,128)(2,1)S(1)} %get-tuple-element.21), channel_id=1, source_target_pairs={{0,6},{1,7},{2,4},{3,5},{4,2},{5,3},{6,0},{7,1},{8,14},{9,15},{10,... | collective-permute-start | bytes 196616 | tf_op jit(solution)/shard_map/ppermute | solution.py:170
  40.0 0.8 %collective-permute-start.21 = (bf16[1,2,128,128]{3,2,1,0:T(8,128)(2,1)S(1)}, bf16[1,2,128,128]{3,2,1,0:T(8,128)(2,1)S(1)}, u32[]{:S(2)}, u32[]{:S(2)}) collective-permute-start(bf16[1,2,128,128]{3,2,1,0:T(8,128)(2,1)S(1)} %get-tuple-element.22), channel_id=1, source_target_pairs={{0,4},{1,5},{2,6},{3,7},{4,0},{5,1},{6,2},{7,3},{8,12},{9,13},{10,... | collective-permute-start | bytes 196616 | tf_op jit(solution)/shard_map/ppermute | solution.py:170
  40.8 1.0 %collective-permute-start.19 = (bf16[1,2,128,128]{3,2,1,0:T(8,128)(2,1)S(1)}, bf16[1,2,128,128]{3,2,1,0:T(8,128)(2,1)S(1)}, u32[]{:S(2)}, u32[]{:S(2)}) collective-permute-start(bf16[1,2,128,128]{3,2,1,0:T(8,128)(2,1)S(1)} %get-tuple-element.23), channel_id=1, source_target_pairs={{0,2},{1,3},{2,0},{3,1},{4,6},{5,7},{6,4},{7,5},{8,10},{9,11},{10,... | collective-permute-start | bytes 196616 | tf_op jit(solution)/shard_map/ppermute | solution.py:170
  41.8 0.5 %collective-permute-done.14.rest_1_ = bf16[4,2,128,128]{3,2,1,0:T(8,128)(2,1)S(1)} collective-permute-done((bf16[4,2,128,128]{3,2,1,0:T(8,128)(2,1)S(1)}, bf16[4,2,128,128]{3,2,1,0:T(8,128)(2,1)S(1)}, u32[]{:S(2)}, u32[]{:S(2)}) %collective-permute-start.14) | collective-permute-done | bytes 262176 | tf_op jit(solution)/shard_map/ppermute | solution.py:155
  42.3 0.3 level.23
  42.7 2.8 %collective-permute-start.17 = (bf16[1,2,128,128]{3,2,1,0:T(8,128)(2,1)S(1)}, bf16[1,2,128,128]{3,2,1,0:T(8,128)(2,1)S(1)}, u32[]{:S(2)}, u32[]{:S(2)}) collective-permute-start(bf16[1,2,128,128]{3,2,1,0:T(8,128)(2,1)S(1)} %get-tuple-element.18), channel_id=1, source_target_pairs={{0,6},{1,7},{2,4},{3,5},{4,2},{5,3},{6,0},{7,1},{8,14},{9,15},{10,... | collective-permute-start | bytes 196616 | tf_op jit(solution)/shard_map/ppermute | solution.py:170
  45.5 0.2 collective-permute-start.16
  45.7 1.7 %collective-permute-start.15 = (bf16[1,2,128,128]{3,2,1,0:T(8,128)(2,1)S(1)}, bf16[1,2,128,128]{3,2,1,0:T(8,128)(2,1)S(1)}, u32[]{:S(2)}, u32[]{:S(2)}) collective-permute-start(bf16[1,2,128,128]{3,2,1,0:T(8,128)(2,1)S(1)} %get-tuple-element.20), channel_id=1, source_target_pairs={{0,4},{1,5},{2,6},{3,7},{4,0},{5,1},{6,2},{7,3},{8,12},{9,13},{10,... | collective-permute-start | bytes 196616 | tf_op jit(solution)/shard_map/ppermute | solution.py:170
  47.5 2.8 %far_field.3.refs_3_ = bf16[2,16384,128]{2,1,0:T(8,128)(2,1)} custom-call(bf16[1,2,128,128]{3,2,1,0:T(8,128)(2,1)S(1)} %get-tuple-element.24.refs_0_, bf16[1,2,128,128]{3,2,1,0:T(8,128)(2,1)S(1)} %collective-permute-done.19.refs_1_, bf16[1,2,128,128]{3,2,1,0:T(8,128)(2,1)S(1)} %collective-permute-done.21.refs_2_, ...), custom_call_target="tpu_custom_call" | custom-call | flops 671088640 | bytes 7864320 | tf_op jit(solution)/shard_map/far_field/pallas_call | solution.py:135
  50.3 1.7 %far_field.4.refs_2_ = bf16[2,16384,128]{2,1,0:T(8,128)(2,1)} custom-call(bf16[1,2,128,128]{3,2,1,0:T(8,128)(2,1)S(1)} %collective-permute-done.16.refs_0_, bf16[1,2,128,128]{3,2,1,0:T(8,128)(2,1)S(1)} %collective-permute-done.17.refs_1_, bf16[16,1024,128]{2,1,0:T(8,128)(2,1)S(1)} %copy-done.2, ...), custom_call_target="tpu_custom_call", output_to_operand_aliasing={{}: (3, {})} | custom-call | flops 268435456 | bytes 3145728 | tf_op jit(solution)/shard_map/far_field/pallas_call | solution.py:135
  51.9 1.3 %far_field.5 = bf16[2,16384,128]{2,1,0:T(8,128)(2,1)} custom-call(bf16[1,2,128,128]{3,2,1,0:T(8,128)(2,1)S(1)} %collective-permute-done.15.refs_0_, bf16[16,1024,128]{2,1,0:T(8,128)(2,1)S(1)} %copy-done.2, bf16[2,16384,128]{2,1,0:T(8,128)(2,1)} %far_field.4.refs_2_), custom_call_target="tpu_custom_call", output_to_operand_aliasing={{}: (2, {})} | custom-call | flops 134217728 | bytes 1572864 | tf_op jit(solution)/shard_map/far_field/pallas_call | solution.py:135
  (25 shorter events, 0.1 us)
Async XLA Ops:
  0.0 4.5 %copy-start = (bf16[4,16,64,128]{3,2,1,0:T(8,128)(2,1)S(1)}, bf16[4,16,64,128]{3,2,1,0:T(8,128)(2,1)}, u32[]{:S(2)}) copy-start(bf16[4,16,64,128]{3,2,1,0:T(8,128)(2,1)} %refs_6_.1) | copy-start | bytes 3145732
  0.0 4.5 %copy-start.1 = (bf16[4,16,64,128]{3,2,1,0:T(8,128)(2,1)S(1)}, bf16[4,16,64,128]{3,2,1,0:T(8,128)(2,1)}, u32[]{:S(2)}) copy-start(bf16[4,16,64,128]{3,2,1,0:T(8,128)(2,1)} %cross.23) | copy-start | bytes 3145732
  2.0 2.5 %collective-permute-start.1 = (bf16[2,2,128,128]{3,2,1,0:T(8,128)(2,1)S(1)}, bf16[2,2,128,128]{3,2,1,0:T(8,128)(2,1)S(1)}, u32[]{:S(2)}, u32[]{:S(2)}) collective-permute-start(bf16[2,2,128,128]{3,2,1,0:T(8,128)(2,1)S(1)} %leaf.3.rest_0_), channel_id=1, source_target_pairs={{0,8},{8,0},{16,24},{24,16},{32,40},{40,32},{48,56},{56,48},{64,72... | collective-permute-start | bytes 393224 | tf_op jit(solution)/shard_map/ppermute | solution.py:155
  3.9 2.5 %collective-permute-start = (bf16[2,2,128,128]{3,2,1,0:T(8,128)(2,1)S(1)}, bf16[2,2,128,128]{3,2,1,0:T(8,128)(2,1)S(1)}, u32[]{:S(2)}, u32[]{:S(2)}) collective-permute-start(bf16[2,2,128,128]{3,2,1,0:T(8,128)(2,1)S(1)} %leaf.4.rest_2_.rest_0_), channel_id=1, source_target_pairs={{0,8},{8,0},{16,24},{24,16},{32,40},{40,32},{48,56},{56,48},{64,72... | collective-permute-start | bytes 393224 | tf_op jit(solution)/shard_map/ppermute | solution.py:155
  4.7 6.4 %collective-permute-start.5 = (bf16[2,2,128,128]{3,2,1,0:T(8,128)(2,1)S(1)}, bf16[2,2,128,128]{3,2,1,0:T(8,128)(2,1)S(1)}, u32[]{:S(2)}, u32[]{:S(2)}) collective-permute-start(bf16[2,2,128,128]{3,2,1,0:T(8,128)(2,1)S(1)} %level.12.rest_2_.rest_0_), channel_id=1, source_target_pairs={{0,16},{8,24},{16,0},{24,8},{32,48},{40,56},{48,32},{56,40},{64,80... | collective-permute-start | bytes 393224 | tf_op jit(solution)/shard_map/ppermute | solution.py:155
  6.7 6.8 %collective-permute-start.4 = (bf16[2,2,128,128]{3,2,1,0:T(8,128)(2,1)S(1)}, bf16[2,2,128,128]{3,2,1,0:T(8,128)(2,1)S(1)}, u32[]{:S(2)}, u32[]{:S(2)}) collective-permute-start(bf16[2,2,128,128]{3,2,1,0:T(8,128)(2,1)S(1)} %level.13.rest_0_), channel_id=1, source_target_pairs={{0,16},{8,24},{16,0},{24,8},{32,48},{40,56},{48,32},{56,40},{64,80... | collective-permute-start | bytes 393224 | tf_op jit(solution)/shard_map/ppermute | solution.py:155
  10.0 5.4 %collective-permute-start.3 = (bf16[2,2,128,128]{3,2,1,0:T(8,128)(2,1)S(1)}, bf16[2,2,128,128]{3,2,1,0:T(8,128)(2,1)S(1)}, u32[]{:S(2)}, u32[]{:S(2)}) collective-permute-start(bf16[2,2,128,128]{3,2,1,0:T(8,128)(2,1)S(1)} %get-tuple-element.12.rest_1_), channel_id=1, source_target_pairs={{0,8},{8,0},{16,24},{24,16},{32,40},{40,32},{48,56},{56,48},{64,72... | collective-permute-start | bytes 393224 | tf_op jit(solution)/shard_map/ppermute | solution.py:155
  10.1 5.2 %collective-permute-start.2 = (bf16[2,2,128,128]{3,2,1,0:T(8,128)(2,1)S(1)}, bf16[2,2,128,128]{3,2,1,0:T(8,128)(2,1)S(1)}, u32[]{:S(2)}, u32[]{:S(2)}) collective-permute-start(bf16[2,2,128,128]{3,2,1,0:T(8,128)(2,1)S(1)} %get-tuple-element.11.rest_2_.rest_0_), channel_id=1, source_target_pairs={{0,8},{8,0},{16,24},{24,16},{32,40},{40,32},{48,56},{56,48},{64,72... | collective-permute-start | bytes 393224 | tf_op jit(solution)/shard_map/ppermute | solution.py:155
  11.4 6.4 %collective-permute-start.9 = (bf16[2,2,128,128]{3,2,1,0:T(8,128)(2,1)S(1)}, bf16[2,2,128,128]{3,2,1,0:T(8,128)(2,1)S(1)}, u32[]{:S(2)}, u32[]{:S(2)}) collective-permute-start(bf16[2,2,128,128]{3,2,1,0:T(8,128)(2,1)S(1)} %level.14.rest_2_.rest_0_), channel_id=1, source_target_pairs={{0,32},{8,40},{16,48},{24,56},{32,0},{40,8},{48,16},{56,24},{64,96... | collective-permute-start | bytes 393224 | tf_op jit(solution)/shard_map/ppermute | solution.py:155
  13.7 8.3 %collective-permute-start.8 = (bf16[2,2,128,128]{3,2,1,0:T(8,128)(2,1)S(1)}, bf16[2,2,128,128]{3,2,1,0:T(8,128)(2,1)S(1)}, u32[]{:S(2)}, u32[]{:S(2)}) collective-permute-start(bf16[2,2,128,128]{3,2,1,0:T(8,128)(2,1)S(1)} %level.15.rest_4_.rest_0_), channel_id=1, source_target_pairs={{0,32},{8,40},{16,48},{24,56},{32,0},{40,8},{48,16},{56,24},{64,96... | collective-permute-start | bytes 393224 | tf_op jit(solution)/shard_map/ppermute | solution.py:155
  15.7 9.1 %collective-permute-start.7 = (bf16[2,2,128,128]{3,2,1,0:T(8,128)(2,1)S(1)}, bf16[2,2,128,128]{3,2,1,0:T(8,128)(2,1)S(1)}, u32[]{:S(2)}, u32[]{:S(2)}) collective-permute-start(bf16[2,2,128,128]{3,2,1,0:T(8,128)(2,1)S(1)} %get-tuple-element.14.rest_1_), channel_id=1, source_target_pairs={{0,16},{8,24},{16,0},{24,8},{32,48},{40,56},{48,32},{56,40},{64,80... | collective-permute-start | bytes 393224 | tf_op jit(solution)/shard_map/ppermute | solution.py:155
  17.3 7.5 %collective-permute-start.6 = (bf16[2,2,128,128]{3,2,1,0:T(8,128)(2,1)S(1)}, bf16[2,2,128,128]{3,2,1,0:T(8,128)(2,1)S(1)}, u32[]{:S(2)}, u32[]{:S(2)}) collective-permute-start(bf16[2,2,128,128]{3,2,1,0:T(8,128)(2,1)S(1)} %get-tuple-element.13.rest_2_.rest_0_), channel_id=1, source_target_pairs={{0,16},{8,24},{16,0},{24,8},{32,48},{40,56},{48,32},{56,40},{64,80... | collective-permute-start | bytes 393224 | tf_op jit(solution)/shard_map/ppermute | solution.py:155
  18.0 29.5 %copy-start.2 = (bf16[16,1024,128]{2,1,0:T(8,128)(2,1)S(1)}, bf16[16,1024,128]{2,1,0:T(8,128)(2,1)}, u32[]{:S(2)}) copy-start(bf16[16,1024,128]{2,1,0:T(8,128)(2,1)} %refs_1_.1) | copy-start | bytes 12582916
  18.0 9.2 %collective-permute-start.13 = (bf16[2,2,128,128]{3,2,1,0:T(8,128)(2,1)S(1)}, bf16[2,2,128,128]{3,2,1,0:T(8,128)(2,1)S(1)}, u32[]{:S(2)}, u32[]{:S(2)}) collective-permute-start(bf16[2,2,128,128]{3,2,1,0:T(8,128)(2,1)S(1)} %level.17.rest_2_.rest_0_), channel_id=1, source_target_pairs={{0,64},{8,72},{16,80},{24,88},{32,96},{40,104},{48,112},{56,120},{... | collective-permute-start | bytes 393224 | tf_op jit(solution)/shard_map/ppermute | solution.py:155
  22.2 8.0 %collective-permute-start.12 = (bf16[2,2,128,128]{3,2,1,0:T(8,128)(2,1)S(1)}, bf16[2,2,128,128]{3,2,1,0:T(8,128)(2,1)S(1)}, u32[]{:S(2)}, u32[]{:S(2)}) collective-permute-start(bf16[2,2,128,128]{3,2,1,0:T(8,128)(2,1)S(1)} %level.18.rest_4_.rest_0_), channel_id=1, source_target_pairs={{0,64},{8,72},{16,80},{24,88},{32,96},{40,104},{48,112},{56,120},{... | collective-permute-start | bytes 393224 | tf_op jit(solution)/shard_map/ppermute | solution.py:155
  25.1 9.0 %collective-permute-start.11 = (bf16[2,2,128,128]{3,2,1,0:T(8,128)(2,1)S(1)}, bf16[2,2,128,128]{3,2,1,0:T(8,128)(2,1)S(1)}, u32[]{:S(2)}, u32[]{:S(2)}) collective-permute-start(bf16[2,2,128,128]{3,2,1,0:T(8,128)(2,1)S(1)} %get-tuple-element.16.rest_1_), channel_id=1, source_target_pairs={{0,32},{8,40},{16,48},{24,56},{32,0},{40,8},{48,16},{56,24},{64,96... | collective-permute-start | bytes 393224 | tf_op jit(solution)/shard_map/ppermute | solution.py:155
  26.2 7.9 %collective-permute-start.10 = (bf16[2,2,128,128]{3,2,1,0:T(8,128)(2,1)S(1)}, bf16[2,2,128,128]{3,2,1,0:T(8,128)(2,1)S(1)}, u32[]{:S(2)}, u32[]{:S(2)}) collective-permute-start(bf16[2,2,128,128]{3,2,1,0:T(8,128)(2,1)S(1)} %get-tuple-element.15.rest_2_.rest_0_), channel_id=1, source_target_pairs={{0,32},{8,40},{16,48},{24,56},{32,0},{40,8},{48,16},{56,24},{64,96... | collective-permute-start | bytes 393224 | tf_op jit(solution)/shard_map/ppermute | solution.py:155
  30.5 6.7 %collective-permute-start.20 = (bf16[2,2,128,128]{3,2,1,0:T(8,128)(2,1)S(1)}, bf16[2,2,128,128]{3,2,1,0:T(8,128)(2,1)S(1)}, u32[]{:S(2)}, u32[]{:S(2)}) collective-permute-start(bf16[2,2,128,128]{3,2,1,0:T(8,128)(2,1)S(1)} %level.21.rest_4_), channel_id=1, source_target_pairs={{0,1},{1,0},{2,3},{3,2},{4,5},{5,4},{6,7},{7,6},{8,9},{9,8},{10,11... | collective-permute-start | bytes 393224 | tf_op jit(solution)/shard_map/ppermute | solution.py:167
  33.7 7.1 %collective-permute-start.18 = (bf16[2,2,128,128]{3,2,1,0:T(8,128)(2,1)S(1)}, bf16[2,2,128,128]{3,2,1,0:T(8,128)(2,1)S(1)}, u32[]{:S(2)}, u32[]{:S(2)}) collective-permute-start(bf16[2,2,128,128]{3,2,1,0:T(8,128)(2,1)S(1)} %level.20.rest_2_), channel_id=1, source_target_pairs={{0,1},{1,0},{2,3},{3,2},{4,5},{5,4},{6,7},{7,6},{8,9},{9,8},{10,11... | collective-permute-start | bytes 393224 | tf_op jit(solution)/shard_map/ppermute | solution.py:167
  34.4 8.0 %collective-permute-start.14 = (bf16[4,2,128,128]{3,2,1,0:T(8,128)(2,1)S(1)}, bf16[4,2,128,128]{3,2,1,0:T(8,128)(2,1)S(1)}, u32[]{:S(2)}, u32[]{:S(2)}) collective-permute-start(bf16[4,2,128,128]{3,2,1,0:T(8,128)(2,1)S(1)} %level.22.rest_0_.rest_2_), channel_id=1, source_target_pairs={{0,64},{8,72},{16,80},{24,88},{32,96},{40,104},{48,112},{56,120},{... | collective-permute-start | bytes 786440 | tf_op jit(solution)/shard_map/ppermute | solution.py:155
  37.2 8.6 %collective-permute-start.22 = (bf16[1,2,128,128]{3,2,1,0:T(8,128)(2,1)S(1)}, bf16[1,2,128,128]{3,2,1,0:T(8,128)(2,1)S(1)}, u32[]{:S(2)}, u32[]{:S(2)}) collective-permute-start(bf16[1,2,128,128]{3,2,1,0:T(8,128)(2,1)S(1)} %get-tuple-element.21), channel_id=1, source_target_pairs={{0,6},{1,7},{2,4},{3,5},{4,2},{5,3},{6,0},{7,1},{8,14},{9,15},{10,... | collective-permute-start | bytes 196616 | tf_op jit(solution)/shard_map/ppermute | solution.py:170
  40.0 7.5 %collective-permute-start.21 = (bf16[1,2,128,128]{3,2,1,0:T(8,128)(2,1)S(1)}, bf16[1,2,128,128]{3,2,1,0:T(8,128)(2,1)S(1)}, u32[]{:S(2)}, u32[]{:S(2)}) collective-permute-start(bf16[1,2,128,128]{3,2,1,0:T(8,128)(2,1)S(1)} %get-tuple-element.22), channel_id=1, source_target_pairs={{0,4},{1,5},{2,6},{3,7},{4,0},{5,1},{6,2},{7,3},{8,12},{9,13},{10,... | collective-permute-start | bytes 196616 | tf_op jit(solution)/shard_map/ppermute | solution.py:170
  40.8 6.6 %collective-permute-start.19 = (bf16[1,2,128,128]{3,2,1,0:T(8,128)(2,1)S(1)}, bf16[1,2,128,128]{3,2,1,0:T(8,128)(2,1)S(1)}, u32[]{:S(2)}, u32[]{:S(2)}) collective-permute-start(bf16[1,2,128,128]{3,2,1,0:T(8,128)(2,1)S(1)} %get-tuple-element.23), channel_id=1, source_target_pairs={{0,2},{1,3},{2,0},{3,1},{4,6},{5,7},{6,4},{7,5},{8,10},{9,11},{10,... | collective-permute-start | bytes 196616 | tf_op jit(solution)/shard_map/ppermute | solution.py:170
  42.7 7.6 %collective-permute-start.17 = (bf16[1,2,128,128]{3,2,1,0:T(8,128)(2,1)S(1)}, bf16[1,2,128,128]{3,2,1,0:T(8,128)(2,1)S(1)}, u32[]{:S(2)}, u32[]{:S(2)}) collective-permute-start(bf16[1,2,128,128]{3,2,1,0:T(8,128)(2,1)S(1)} %get-tuple-element.18), channel_id=1, source_target_pairs={{0,6},{1,7},{2,4},{3,5},{4,2},{5,3},{6,0},{7,1},{8,14},{9,15},{10,... | collective-permute-start | bytes 196616 | tf_op jit(solution)/shard_map/ppermute | solution.py:170
  45.5 4.8 %collective-permute-start.16 = (bf16[1,2,128,128]{3,2,1,0:T(8,128)(2,1)S(1)}, bf16[1,2,128,128]{3,2,1,0:T(8,128)(2,1)S(1)}, u32[]{:S(2)}, u32[]{:S(2)}) collective-permute-start(bf16[1,2,128,128]{3,2,1,0:T(8,128)(2,1)S(1)} %get-tuple-element.19), channel_id=1, source_target_pairs={{0,2},{1,3},{2,0},{3,1},{4,6},{5,7},{6,4},{7,5},{8,10},{9,11},{10,... | collective-permute-start | bytes 196616 | tf_op jit(solution)/shard_map/ppermute | solution.py:170
  45.7 6.2 %collective-permute-start.15 = (bf16[1,2,128,128]{3,2,1,0:T(8,128)(2,1)S(1)}, bf16[1,2,128,128]{3,2,1,0:T(8,128)(2,1)S(1)}, u32[]{:S(2)}, u32[]{:S(2)}) collective-permute-start(bf16[1,2,128,128]{3,2,1,0:T(8,128)(2,1)S(1)} %get-tuple-element.20), channel_id=1, source_target_pairs={{0,4},{1,5},{2,6},{3,7},{4,0},{5,1},{6,2},{7,3},{8,12},{9,13},{10,... | collective-permute-start | bytes 196616 | tf_op jit(solution)/shard_map/ppermute | solution.py:170

commit v4 on v3

--- a/solution.py
+++ b/solution.py
@@ -177,7 +177,7 @@
 ORDER = (
     ("A", "leaf", 1), ("B", "leaf", 1), ("A", 0, 1), ("B", 0, 1), ("C", "leaf", 2), ("A", 1, 1), ("B", 1, 1), ("C", 0, 2), ("A", 2, 1), ("B", 2, 1), ("C", 1, 2), ("A", 3, 1), ("B", 3, 1), ("C", 2, 1), ("C", 3, 1),
 )
-FAR = (((0, 1), (1, 1), (2, 1), (3, 1), (0, 0)), ((1, 0), (3, 0)), ((2, 0),))
+FAR = (((0, 1), (1, 1), (2, 1), (3, 1), (0, 0)), ((1, 0), (2, 0), (3, 0)))
 
 
 def solution(mesh):

time: 53.5 us -> 53.3 us (level)
  waiting for transfers between devices: 4.19 us -> 5.97 us
  Pallas kernels: 14.9 us -> 14 us
  starting transfers between devices: 33.9 us -> 33 us
    ppermute x6, waiting for transfers between devices: 0.02 us -> 1.64 us  [shards(): lax.ppermute(piece, 'tgt', pairs_by(2 * j, 8))]
    pallas_call x3 -> x2, Pallas kernels: 5.71 us -> 4.81 us  [far_field(): pl.pallas_call(kernel, in_specs=[VMEM] * (count + 1) + [ANY], out_specs=A...]
    ppermute x6, starting transfers between devices: 9.39 us -> 8.78 us  [shards(): lax.ppermute(piece, 'tgt', pairs_by(2 * j, 8))]
  transfers between devices with their start and end apart: 23 -> 23, of which waited for: 4 -> 5; matrix products, arithmetic and copies ran while one was open for 0% -> 0% of each run, Pallas kernels for 22% -> 19%
where the time goes in v4:
time: 53.3 us; the launch traced here: 53.2 us
  starting transfers between devices  33 us (62%)
  Pallas kernels  14 us (26%)
  waiting for transfers between devices  5.97 us (11%)
    ppermute x15, starting transfers between devices, proceed(): lax.ppermute(part, 'src', pairs_by(1 << height, 16))  20.6 us
    ppermute x6, starting transfers between devices, shards(): lax.ppermute(piece, 'tgt', pairs_by(2 * j, 8))  8.78 us
    pallas_call x3, Pallas kernels, leaf(): pl.pallas_call(kernel, in_specs=[ANY] * (2 + len(after)), out_specs=[VMEM...  6.31 us
    pallas_call x2, Pallas kernels, far_field(): pl.pallas_call(kernel, in_specs=[VMEM] * (count + 1) + [ANY], out_specs=A...  4.81 us
    ppermute x15, waiting for transfers between devices, proceed(): lax.ppermute(part, 'src', pairs_by(1 << height, 16))  4.15 us
    ppermute x2, starting transfers between devices, shards(): new = lax.ppermute(new, 'tgt', pairs_by(1, 8))  3.61 us
    pallas_call x12, Pallas kernels, level(): pl.pallas_call(kernel, in_specs=[VMEM] * (2 + 2 * parts) + [ANY] * len(af...  2.85 us
    ppermute x6, waiting for transfers between devices, shards(): lax.ppermute(piece, 'tgt', pairs_by(2 * j, 8))  1.64 us
  transfers between devices with their start and end apart: 23, of which 5 were waited for; matrix products, arithmetic and copies ran while one was open for 0% of the time, Pallas kernels for 19%

profile of v4, /device:TPU:0, one launch (start us, length us, event | category | flops | bytes accessed | tf_op | source)
XLA Modules:
  0.0 53.2 jit_solution(15841802459404404651)
XLA Ops:
  0.0 1.8 %leaf.3.rest_0_ = bf16[2,2,128,128]{3,2,1,0:T(8,128)(2,1)S(1)} custom-call(bf16[16,128,1024]{2,1,0:T(8,128)(2,1)} %project.5, bf16[16384,128]{1,0:T(8,128)(2,1)} %charges.5), custom_call_target="tpu_custom_call" | custom-call | flops 134217728 | bytes 2097152 | tf_op jit(solution)/shard_map/leaf/pallas_call | solution.py:67
  1.8 0.0 copy-start
  1.9 0.0 copy-start.1
  1.9 0.1 collective-permute-start.1
  2.0 2.0 %leaf.4.rest_2_.rest_0_ = bf16[2,2,128,128]{3,2,1,0:T(8,128)(2,1)S(1)} custom-call(bf16[16,128,1024]{2,1,0:T(8,128)(2,1)} %project.5, bf16[16384,128]{1,0:T(8,128)(2,1)} %charges.5, bf16[2,2,128,128]{3,2,1,0:T(8,128)(2,1)S(1)} %leaf.3.rest_0_), custom_call_target="tpu_custom_call" | custom-call | flops 134217728 | bytes 2097152 | tf_op jit(solution)/shard_map/leaf/pallas_call | solution.py:67
  3.9 0.4 collective-permute-start
  4.4 0.2 level.12.rest_2_.rest_0_
  4.6 1.7 %collective-permute-start.5 = (bf16[2,2,128,128]{3,2,1,0:T(8,128)(2,1)S(1)}, bf16[2,2,128,128]{3,2,1,0:T(8,128)(2,1)S(1)}, u32[]{:S(2)}, u32[]{:S(2)}) collective-permute-start(bf16[2,2,128,128]{3,2,1,0:T(8,128)(2,1)S(1)} %level.12.rest_2_.rest_0_), channel_id=1, source_target_pairs={{0,16},{8,24},{16,0},{24,8},{32,48},{40,56},{48,32},{56,40},{64,80... | collective-permute-start | bytes 393224 | tf_op jit(solution)/shard_map/ppermute | solution.py:155
  6.4 0.2 level.13.rest_0_
  6.6 0.8 %collective-permute-start.4 = (bf16[2,2,128,128]{3,2,1,0:T(8,128)(2,1)S(1)}, bf16[2,2,128,128]{3,2,1,0:T(8,128)(2,1)S(1)}, u32[]{:S(2)}, u32[]{:S(2)}) collective-permute-start(bf16[2,2,128,128]{3,2,1,0:T(8,128)(2,1)S(1)} %level.13.rest_0_), channel_id=1, source_target_pairs={{0,16},{8,24},{16,0},{24,8},{32,48},{40,56},{48,32},{56,40},{64,80... | collective-permute-start | bytes 393224 | tf_op jit(solution)/shard_map/ppermute | solution.py:155
  7.3 2.5 %leaf.5 = (bf16[2,2,128,128]{3,2,1,0:T(8,128)(2,1)S(1)}, bf16[2,2,128,128]{3,2,1,0:T(8,128)(2,1)S(1)}) custom-call(bf16[16,128,1024]{2,1,0:T(8,128)(2,1)} %project.5, bf16[16384,128]{1,0:T(8,128)(2,1)} %charges.5, bf16[2,2,128,128]{3,2,1,0:T(8,128)(2,1)S(1)} %level.13.rest_0_), custom_call_target="tpu_custom_call" | custom-call | flops 268435456 | bytes 4194304 | tf_op jit(solution)/shard_map/leaf/pallas_call | solution.py:67
  9.8 0.1 collective-permute-start.3
  10.0 0.4 collective-permute-start.2
  10.4 0.6 %collective-permute-done.5.rest_1_ = bf16[2,2,128,128]{3,2,1,0:T(8,128)(2,1)S(1)} collective-permute-done((bf16[2,2,128,128]{3,2,1,0:T(8,128)(2,1)S(1)}, bf16[2,2,128,128]{3,2,1,0:T(8,128)(2,1)S(1)}, u32[]{:S(2)}, u32[]{:S(2)}) %collective-permute-start.5) | collective-permute-done | bytes 131104 | tf_op jit(solution)/shard_map/ppermute | solution.py:155
  11.0 0.2 level.14.rest_2_.rest_0_
  11.2 2.1 %collective-permute-start.9 = (bf16[2,2,128,128]{3,2,1,0:T(8,128)(2,1)S(1)}, bf16[2,2,128,128]{3,2,1,0:T(8,128)(2,1)S(1)}, u32[]{:S(2)}, u32[]{:S(2)}) collective-permute-start(bf16[2,2,128,128]{3,2,1,0:T(8,128)(2,1)S(1)} %level.14.rest_2_.rest_0_), channel_id=1, source_target_pairs={{0,32},{8,40},{16,48},{24,56},{32,0},{40,8},{48,16},{56,24},{64,96... | collective-permute-start | bytes 393224 | tf_op jit(solution)/shard_map/ppermute | solution.py:155
  13.3 0.2 level.15.rest_4_.rest_0_
  13.5 1.8 %collective-permute-start.8 = (bf16[2,2,128,128]{3,2,1,0:T(8,128)(2,1)S(1)}, bf16[2,2,128,128]{3,2,1,0:T(8,128)(2,1)S(1)}, u32[]{:S(2)}, u32[]{:S(2)}) collective-permute-start(bf16[2,2,128,128]{3,2,1,0:T(8,128)(2,1)S(1)} %level.15.rest_4_.rest_0_), channel_id=1, source_target_pairs={{0,32},{8,40},{16,48},{24,56},{32,0},{40,8},{48,16},{56,24},{64,96... | collective-permute-start | bytes 393224 | tf_op jit(solution)/shard_map/ppermute | solution.py:155
  15.4 0.3 level.16
  15.7 1.7 %collective-permute-start.7 = (bf16[2,2,128,128]{3,2,1,0:T(8,128)(2,1)S(1)}, bf16[2,2,128,128]{3,2,1,0:T(8,128)(2,1)S(1)}, u32[]{:S(2)}, u32[]{:S(2)}) collective-permute-start(bf16[2,2,128,128]{3,2,1,0:T(8,128)(2,1)S(1)} %get-tuple-element.14.rest_1_), channel_id=1, source_target_pairs={{0,16},{8,24},{16,0},{24,8},{32,48},{40,56},{48,32},{56,40},{64,80... | collective-permute-start | bytes 393224 | tf_op jit(solution)/shard_map/ppermute | solution.py:155
  17.3 0.4 collective-permute-start.6
  17.8 0.2 level.17.rest_2_.rest_0_
  18.0 3.7 %collective-permute-start.13 = (bf16[2,2,128,128]{3,2,1,0:T(8,128)(2,1)S(1)}, bf16[2,2,128,128]{3,2,1,0:T(8,128)(2,1)S(1)}, u32[]{:S(2)}, u32[]{:S(2)}) collective-permute-start(bf16[2,2,128,128]{3,2,1,0:T(8,128)(2,1)S(1)} %level.17.rest_2_.rest_0_), channel_id=1, source_target_pairs={{0,64},{8,72},{16,80},{24,88},{32,96},{40,104},{48,112},{56,120},{... | collective-permute-start | bytes 393224 | tf_op jit(solution)/shard_map/ppermute | solution.py:155
  21.7 0.2 level.18.rest_4_.rest_0_
  21.9 2.6 %collective-permute-start.12 = (bf16[2,2,128,128]{3,2,1,0:T(8,128)(2,1)S(1)}, bf16[2,2,128,128]{3,2,1,0:T(8,128)(2,1)S(1)}, u32[]{:S(2)}, u32[]{:S(2)}) collective-permute-start(bf16[2,2,128,128]{3,2,1,0:T(8,128)(2,1)S(1)} %level.18.rest_4_.rest_0_), channel_id=1, source_target_pairs={{0,64},{8,72},{16,80},{24,88},{32,96},{40,104},{48,112},{56,120},{... | collective-permute-start | bytes 393224 | tf_op jit(solution)/shard_map/ppermute | solution.py:155
  24.5 0.3 level.19
  24.8 1.1 %collective-permute-start.11 = (bf16[2,2,128,128]{3,2,1,0:T(8,128)(2,1)S(1)}, bf16[2,2,128,128]{3,2,1,0:T(8,128)(2,1)S(1)}, u32[]{:S(2)}, u32[]{:S(2)}) collective-permute-start(bf16[2,2,128,128]{3,2,1,0:T(8,128)(2,1)S(1)} %get-tuple-element.16.rest_1_), channel_id=1, source_target_pairs={{0,32},{8,40},{16,48},{24,56},{32,0},{40,8},{48,16},{56,24},{64,96... | collective-permute-start | bytes 393224 | tf_op jit(solution)/shard_map/ppermute | solution.py:155
  25.9 1.0 %collective-permute-start.10 = (bf16[2,2,128,128]{3,2,1,0:T(8,128)(2,1)S(1)}, bf16[2,2,128,128]{3,2,1,0:T(8,128)(2,1)S(1)}, u32[]{:S(2)}, u32[]{:S(2)}) collective-permute-start(bf16[2,2,128,128]{3,2,1,0:T(8,128)(2,1)S(1)} %get-tuple-element.15.rest_2_.rest_0_), channel_id=1, source_target_pairs={{0,32},{8,40},{16,48},{24,56},{32,0},{40,8},{48,16},{56,24},{64,96... | collective-permute-start | bytes 393224 | tf_op jit(solution)/shard_map/ppermute | solution.py:155
  26.9 0.2 level.20.rest_2_
  27.1 2.8 %collective-permute-done.12.rest_1_ = bf16[2,2,128,128]{3,2,1,0:T(8,128)(2,1)S(1)} collective-permute-done((bf16[2,2,128,128]{3,2,1,0:T(8,128)(2,1)S(1)}, bf16[2,2,128,128]{3,2,1,0:T(8,128)(2,1)S(1)}, u32[]{:S(2)}, u32[]{:S(2)}) %collective-permute-start.12) | collective-permute-done | bytes 131104 | tf_op jit(solution)/shard_map/ppermute | solution.py:155
  29.9 0.2 level.21.rest_4_
  30.1 3.3 %collective-permute-start.20 = (bf16[2,2,128,128]{3,2,1,0:T(8,128)(2,1)S(1)}, bf16[2,2,128,128]{3,2,1,0:T(8,128)(2,1)S(1)}, u32[]{:S(2)}, u32[]{:S(2)}) collective-permute-start(bf16[2,2,128,128]{3,2,1,0:T(8,128)(2,1)S(1)} %level.21.rest_4_), channel_id=1, source_target_pairs={{0,1},{1,0},{2,3},{3,2},{4,5},{5,4},{6,7},{7,6},{8,9},{9,8},{10,11... | collective-permute-start | bytes 393224 | tf_op jit(solution)/shard_map/ppermute | solution.py:167
  33.4 0.3 collective-permute-start.18
  33.8 0.0 collective-permute-done.10.rest_2_
  33.8 0.3 level.22.rest_0_.rest_2_
  34.1 2.6 %collective-permute-start.14 = (bf16[4,2,128,128]{3,2,1,0:T(8,128)(2,1)S(1)}, bf16[4,2,128,128]{3,2,1,0:T(8,128)(2,1)S(1)}, u32[]{:S(2)}, u32[]{:S(2)}) collective-permute-start(bf16[4,2,128,128]{3,2,1,0:T(8,128)(2,1)S(1)} %level.22.rest_0_.rest_2_), channel_id=1, source_target_pairs={{0,64},{8,72},{16,80},{24,88},{32,96},{40,104},{48,112},{56,120},{... | collective-permute-start | bytes 786440 | tf_op jit(solution)/shard_map/ppermute | solution.py:155
  36.7 0.2 collective-permute-done.20
  36.9 2.8 %collective-permute-start.22 = (bf16[1,2,128,128]{3,2,1,0:T(8,128)(2,1)S(1)}, bf16[1,2,128,128]{3,2,1,0:T(8,128)(2,1)S(1)}, u32[]{:S(2)}, u32[]{:S(2)}) collective-permute-start(bf16[1,2,128,128]{3,2,1,0:T(8,128)(2,1)S(1)} %get-tuple-element.21), channel_id=1, source_target_pairs={{0,6},{1,7},{2,4},{3,5},{4,2},{5,3},{6,0},{7,1},{8,14},{9,15},{10,... | collective-permute-start | bytes 196616 | tf_op jit(solution)/shard_map/ppermute | solution.py:170
  39.7 0.8 %collective-permute-start.21 = (bf16[1,2,128,128]{3,2,1,0:T(8,128)(2,1)S(1)}, bf16[1,2,128,128]{3,2,1,0:T(8,128)(2,1)S(1)}, u32[]{:S(2)}, u32[]{:S(2)}) collective-permute-start(bf16[1,2,128,128]{3,2,1,0:T(8,128)(2,1)S(1)} %get-tuple-element.22), channel_id=1, source_target_pairs={{0,4},{1,5},{2,6},{3,7},{4,0},{5,1},{6,2},{7,3},{8,12},{9,13},{10,... | collective-permute-start | bytes 196616 | tf_op jit(solution)/shard_map/ppermute | solution.py:170
  40.5 1.0 %collective-permute-start.19 = (bf16[1,2,128,128]{3,2,1,0:T(8,128)(2,1)S(1)}, bf16[1,2,128,128]{3,2,1,0:T(8,128)(2,1)S(1)}, u32[]{:S(2)}, u32[]{:S(2)}) collective-permute-start(bf16[1,2,128,128]{3,2,1,0:T(8,128)(2,1)S(1)} %get-tuple-element.23), channel_id=1, source_target_pairs={{0,2},{1,3},{2,0},{3,1},{4,6},{5,7},{6,4},{7,5},{8,10},{9,11},{10,... | collective-permute-start | bytes 196616 | tf_op jit(solution)/shard_map/ppermute | solution.py:170
  41.5 0.7 %collective-permute-done.14.rest_1_ = bf16[4,2,128,128]{3,2,1,0:T(8,128)(2,1)S(1)} collective-permute-done((bf16[4,2,128,128]{3,2,1,0:T(8,128)(2,1)S(1)}, bf16[4,2,128,128]{3,2,1,0:T(8,128)(2,1)S(1)}, u32[]{:S(2)}, u32[]{:S(2)}) %collective-permute-start.14) | collective-permute-done | bytes 262176 | tf_op jit(solution)/shard_map/ppermute | solution.py:155
  42.2 0.3 level.23
  42.5 2.8 %collective-permute-start.17 = (bf16[1,2,128,128]{3,2,1,0:T(8,128)(2,1)S(1)}, bf16[1,2,128,128]{3,2,1,0:T(8,128)(2,1)S(1)}, u32[]{:S(2)}, u32[]{:S(2)}) collective-permute-start(bf16[1,2,128,128]{3,2,1,0:T(8,128)(2,1)S(1)} %get-tuple-element.18), channel_id=1, source_target_pairs={{0,6},{1,7},{2,4},{3,5},{4,2},{5,3},{6,0},{7,1},{8,14},{9,15},{10,... | collective-permute-start | bytes 196616 | tf_op jit(solution)/shard_map/ppermute | solution.py:170
  45.4 0.8 %collective-permute-start.16 = (bf16[1,2,128,128]{3,2,1,0:T(8,128)(2,1)S(1)}, bf16[1,2,128,128]{3,2,1,0:T(8,128)(2,1)S(1)}, u32[]{:S(2)}, u32[]{:S(2)}) collective-permute-start(bf16[1,2,128,128]{3,2,1,0:T(8,128)(2,1)S(1)} %get-tuple-element.19), channel_id=1, source_target_pairs={{0,4},{1,5},{2,6},{3,7},{4,0},{5,1},{6,2},{7,3},{8,12},{9,13},{10,... | collective-permute-start | bytes 196616 | tf_op jit(solution)/shard_map/ppermute | solution.py:170
  46.2 0.5 %collective-permute-start.15 = (bf16[1,2,128,128]{3,2,1,0:T(8,128)(2,1)S(1)}, bf16[1,2,128,128]{3,2,1,0:T(8,128)(2,1)S(1)}, u32[]{:S(2)}, u32[]{:S(2)}) collective-permute-start(bf16[1,2,128,128]{3,2,1,0:T(8,128)(2,1)S(1)} %get-tuple-element.20), channel_id=1, source_target_pairs={{0,2},{1,3},{2,0},{3,1},{4,6},{5,7},{6,4},{7,5},{8,10},{9,11},{10,... | collective-permute-start | bytes 196616 | tf_op jit(solution)/shard_map/ppermute | solution.py:170
  46.7 2.8 %far_field.2.refs_4_ = bf16[2,16384,128]{2,1,0:T(8,128)(2,1)} custom-call(bf16[1,2,128,128]{3,2,1,0:T(8,128)(2,1)S(1)} %get-tuple-element.24.refs_0_, bf16[1,2,128,128]{3,2,1,0:T(8,128)(2,1)S(1)} %collective-permute-done.19.refs_1_, bf16[1,2,128,128]{3,2,1,0:T(8,128)(2,1)S(1)} %collective-permute-done.21.refs_2_, ...), custom_call_target="tpu_custom_call" | custom-call | flops 671088640 | bytes 7864320 | tf_op jit(solution)/shard_map/far_field/pallas_call | solution.py:135
  49.5 1.6 %collective-permute-done.16.refs_1_ = bf16[1,2,128,128]{3,2,1,0:T(8,128)(2,1)S(1)} collective-permute-done((bf16[1,2,128,128]{3,2,1,0:T(8,128)(2,1)S(1)}, bf16[1,2,128,128]{3,2,1,0:T(8,128)(2,1)S(1)}, u32[]{:S(2)}, u32[]{:S(2)}) %collective-permute-start.16) | collective-permute-done | bytes 65568 | tf_op jit(solution)/shard_map/ppermute | solution.py:170
  51.1 2.0 %far_field.3 = bf16[2,16384,128]{2,1,0:T(8,128)(2,1)} custom-call(bf16[1,2,128,128]{3,2,1,0:T(8,128)(2,1)S(1)} %collective-permute-done.15.refs_0_, bf16[1,2,128,128]{3,2,1,0:T(8,128)(2,1)S(1)} %collective-permute-done.16.refs_1_, bf16[1,2,128,128]{3,2,1,0:T(8,128)(2,1)S(1)} %collective-permute-done.17.refs_2_, ...), custom_call_target="tpu_custom_call", output_to_operand_aliasing={{}: (4, {})} | custom-call | flops 402653184 | bytes 4718592 | tf_op jit(solution)/shard_map/far_field/pallas_call | solution.py:135
  (24 shorter events, 0.1 us)
Async XLA Ops:
  1.8 2.5 %copy-start = (bf16[4,16,64,128]{3,2,1,0:T(8,128)(2,1)S(1)}, bf16[4,16,64,128]{3,2,1,0:T(8,128)(2,1)}, u32[]{:S(2)}) copy-start(bf16[4,16,64,128]{3,2,1,0:T(8,128)(2,1)} %refs_6_.1) | copy-start | bytes 3145732
  1.9 2.5 %copy-start.1 = (bf16[4,16,64,128]{3,2,1,0:T(8,128)(2,1)S(1)}, bf16[4,16,64,128]{3,2,1,0:T(8,128)(2,1)}, u32[]{:S(2)}) copy-start(bf16[4,16,64,128]{3,2,1,0:T(8,128)(2,1)} %cross.23) | copy-start | bytes 3145732
  1.9 2.5 %collective-permute-start.1 = (bf16[2,2,128,128]{3,2,1,0:T(8,128)(2,1)S(1)}, bf16[2,2,128,128]{3,2,1,0:T(8,128)(2,1)S(1)}, u32[]{:S(2)}, u32[]{:S(2)}) collective-permute-start(bf16[2,2,128,128]{3,2,1,0:T(8,128)(2,1)S(1)} %leaf.3.rest_0_), channel_id=1, source_target_pairs={{0,8},{8,0},{16,24},{24,16},{32,40},{40,32},{48,56},{56,48},{64,72... | collective-permute-start | bytes 393224 | tf_op jit(solution)/shard_map/ppermute | solution.py:155
  3.9 2.4 %collective-permute-start = (bf16[2,2,128,128]{3,2,1,0:T(8,128)(2,1)S(1)}, bf16[2,2,128,128]{3,2,1,0:T(8,128)(2,1)S(1)}, u32[]{:S(2)}, u32[]{:S(2)}) collective-permute-start(bf16[2,2,128,128]{3,2,1,0:T(8,128)(2,1)S(1)} %leaf.4.rest_2_.rest_0_), channel_id=1, source_target_pairs={{0,8},{8,0},{16,24},{24,16},{32,40},{40,32},{48,56},{56,48},{64,72... | collective-permute-start | bytes 393224 | tf_op jit(solution)/shard_map/ppermute | solution.py:155
  4.6 6.4 %collective-permute-start.5 = (bf16[2,2,128,128]{3,2,1,0:T(8,128)(2,1)S(1)}, bf16[2,2,128,128]{3,2,1,0:T(8,128)(2,1)S(1)}, u32[]{:S(2)}, u32[]{:S(2)}) collective-permute-start(bf16[2,2,128,128]{3,2,1,0:T(8,128)(2,1)S(1)} %level.12.rest_2_.rest_0_), channel_id=1, source_target_pairs={{0,16},{8,24},{16,0},{24,8},{32,48},{40,56},{48,32},{56,40},{64,80... | collective-permute-start | bytes 393224 | tf_op jit(solution)/shard_map/ppermute | solution.py:155
  6.6 6.8 %collective-permute-start.4 = (bf16[2,2,128,128]{3,2,1,0:T(8,128)(2,1)S(1)}, bf16[2,2,128,128]{3,2,1,0:T(8,128)(2,1)S(1)}, u32[]{:S(2)}, u32[]{:S(2)}) collective-permute-start(bf16[2,2,128,128]{3,2,1,0:T(8,128)(2,1)S(1)} %level.13.rest_0_), channel_id=1, source_target_pairs={{0,16},{8,24},{16,0},{24,8},{32,48},{40,56},{48,32},{56,40},{64,80... | collective-permute-start | bytes 393224 | tf_op jit(solution)/shard_map/ppermute | solution.py:155
  9.8 5.5 %collective-permute-start.3 = (bf16[2,2,128,128]{3,2,1,0:T(8,128)(2,1)S(1)}, bf16[2,2,128,128]{3,2,1,0:T(8,128)(2,1)S(1)}, u32[]{:S(2)}, u32[]{:S(2)}) collective-permute-start(bf16[2,2,128,128]{3,2,1,0:T(8,128)(2,1)S(1)} %get-tuple-element.12.rest_1_), channel_id=1, source_target_pairs={{0,8},{8,0},{16,24},{24,16},{32,40},{40,32},{48,56},{56,48},{64,72... | collective-permute-start | bytes 393224 | tf_op jit(solution)/shard_map/ppermute | solution.py:155
  10.0 5.4 %collective-permute-start.2 = (bf16[2,2,128,128]{3,2,1,0:T(8,128)(2,1)S(1)}, bf16[2,2,128,128]{3,2,1,0:T(8,128)(2,1)S(1)}, u32[]{:S(2)}, u32[]{:S(2)}) collective-permute-start(bf16[2,2,128,128]{3,2,1,0:T(8,128)(2,1)S(1)} %get-tuple-element.11.rest_2_.rest_0_), channel_id=1, source_target_pairs={{0,8},{8,0},{16,24},{24,16},{32,40},{40,32},{48,56},{56,48},{64,72... | collective-permute-start | bytes 393224 | tf_op jit(solution)/shard_map/ppermute | solution.py:155
  11.2 6.5 %collective-permute-start.9 = (bf16[2,2,128,128]{3,2,1,0:T(8,128)(2,1)S(1)}, bf16[2,2,128,128]{3,2,1,0:T(8,128)(2,1)S(1)}, u32[]{:S(2)}, u32[]{:S(2)}) collective-permute-start(bf16[2,2,128,128]{3,2,1,0:T(8,128)(2,1)S(1)} %level.14.rest_2_.rest_0_), channel_id=1, source_target_pairs={{0,32},{8,40},{16,48},{24,56},{32,0},{40,8},{48,16},{56,24},{64,96... | collective-permute-start | bytes 393224 | tf_op jit(solution)/shard_map/ppermute | solution.py:155
  13.5 8.1 %collective-permute-start.8 = (bf16[2,2,128,128]{3,2,1,0:T(8,128)(2,1)S(1)}, bf16[2,2,128,128]{3,2,1,0:T(8,128)(2,1)S(1)}, u32[]{:S(2)}, u32[]{:S(2)}) collective-permute-start(bf16[2,2,128,128]{3,2,1,0:T(8,128)(2,1)S(1)} %level.15.rest_4_.rest_0_), channel_id=1, source_target_pairs={{0,32},{8,40},{16,48},{24,56},{32,0},{40,8},{48,16},{56,24},{64,96... | collective-permute-start | bytes 393224 | tf_op jit(solution)/shard_map/ppermute | solution.py:155
  15.7 8.8 %collective-permute-start.7 = (bf16[2,2,128,128]{3,2,1,0:T(8,128)(2,1)S(1)}, bf16[2,2,128,128]{3,2,1,0:T(8,128)(2,1)S(1)}, u32[]{:S(2)}, u32[]{:S(2)}) collective-permute-start(bf16[2,2,128,128]{3,2,1,0:T(8,128)(2,1)S(1)} %get-tuple-element.14.rest_1_), channel_id=1, source_target_pairs={{0,16},{8,24},{16,0},{24,8},{32,48},{40,56},{48,32},{56,40},{64,80... | collective-permute-start | bytes 393224 | tf_op jit(solution)/shard_map/ppermute | solution.py:155
  17.3 7.2 %collective-permute-start.6 = (bf16[2,2,128,128]{3,2,1,0:T(8,128)(2,1)S(1)}, bf16[2,2,128,128]{3,2,1,0:T(8,128)(2,1)S(1)}, u32[]{:S(2)}, u32[]{:S(2)}) collective-permute-start(bf16[2,2,128,128]{3,2,1,0:T(8,128)(2,1)S(1)} %get-tuple-element.13.rest_2_.rest_0_), channel_id=1, source_target_pairs={{0,16},{8,24},{16,0},{24,8},{32,48},{40,56},{48,32},{56,40},{64,80... | collective-permute-start | bytes 393224 | tf_op jit(solution)/shard_map/ppermute | solution.py:155
  18.0 8.9 %collective-permute-start.13 = (bf16[2,2,128,128]{3,2,1,0:T(8,128)(2,1)S(1)}, bf16[2,2,128,128]{3,2,1,0:T(8,128)(2,1)S(1)}, u32[]{:S(2)}, u32[]{:S(2)}) collective-permute-start(bf16[2,2,128,128]{3,2,1,0:T(8,128)(2,1)S(1)} %level.17.rest_2_.rest_0_), channel_id=1, source_target_pairs={{0,64},{8,72},{16,80},{24,88},{32,96},{40,104},{48,112},{56,120},{... | collective-permute-start | bytes 393224 | tf_op jit(solution)/shard_map/ppermute | solution.py:155
  21.9 8.0 %collective-permute-start.12 = (bf16[2,2,128,128]{3,2,1,0:T(8,128)(2,1)S(1)}, bf16[2,2,128,128]{3,2,1,0:T(8,128)(2,1)S(1)}, u32[]{:S(2)}, u32[]{:S(2)}) collective-permute-start(bf16[2,2,128,128]{3,2,1,0:T(8,128)(2,1)S(1)} %level.18.rest_4_.rest_0_), channel_id=1, source_target_pairs={{0,64},{8,72},{16,80},{24,88},{32,96},{40,104},{48,112},{56,120},{... | collective-permute-start | bytes 393224 | tf_op jit(solution)/shard_map/ppermute | solution.py:155
  24.8 9.0 %collective-permute-start.11 = (bf16[2,2,128,128]{3,2,1,0:T(8,128)(2,1)S(1)}, bf16[2,2,128,128]{3,2,1,0:T(8,128)(2,1)S(1)}, u32[]{:S(2)}, u32[]{:S(2)}) collective-permute-start(bf16[2,2,128,128]{3,2,1,0:T(8,128)(2,1)S(1)} %get-tuple-element.16.rest_1_), channel_id=1, source_target_pairs={{0,32},{8,40},{16,48},{24,56},{32,0},{40,8},{48,16},{56,24},{64,96... | collective-permute-start | bytes 393224 | tf_op jit(solution)/shard_map/ppermute | solution.py:155
  25.9 7.9 %collective-permute-start.10 = (bf16[2,2,128,128]{3,2,1,0:T(8,128)(2,1)S(1)}, bf16[2,2,128,128]{3,2,1,0:T(8,128)(2,1)S(1)}, u32[]{:S(2)}, u32[]{:S(2)}) collective-permute-start(bf16[2,2,128,128]{3,2,1,0:T(8,128)(2,1)S(1)} %get-tuple-element.15.rest_2_.rest_0_), channel_id=1, source_target_pairs={{0,32},{8,40},{16,48},{24,56},{32,0},{40,8},{48,16},{56,24},{64,96... | collective-permute-start | bytes 393224 | tf_op jit(solution)/shard_map/ppermute | solution.py:155
  30.1 16.6 %copy-start.2 = (bf16[16,1024,128]{2,1,0:T(8,128)(2,1)S(1)}, bf16[16,1024,128]{2,1,0:T(8,128)(2,1)}, u32[]{:S(2)}) copy-start(bf16[16,1024,128]{2,1,0:T(8,128)(2,1)} %refs_3_.1) | copy-start | bytes 12582916
  30.1 6.7 %collective-permute-start.20 = (bf16[2,2,128,128]{3,2,1,0:T(8,128)(2,1)S(1)}, bf16[2,2,128,128]{3,2,1,0:T(8,128)(2,1)S(1)}, u32[]{:S(2)}, u32[]{:S(2)}) collective-permute-start(bf16[2,2,128,128]{3,2,1,0:T(8,128)(2,1)S(1)} %level.21.rest_4_), channel_id=1, source_target_pairs={{0,1},{1,0},{2,3},{3,2},{4,5},{5,4},{6,7},{7,6},{8,9},{9,8},{10,11... | collective-permute-start | bytes 393224 | tf_op jit(solution)/shard_map/ppermute | solution.py:167
  33.4 7.1 %collective-permute-start.18 = (bf16[2,2,128,128]{3,2,1,0:T(8,128)(2,1)S(1)}, bf16[2,2,128,128]{3,2,1,0:T(8,128)(2,1)S(1)}, u32[]{:S(2)}, u32[]{:S(2)}) collective-permute-start(bf16[2,2,128,128]{3,2,1,0:T(8,128)(2,1)S(1)} %level.20.rest_2_), channel_id=1, source_target_pairs={{0,1},{1,0},{2,3},{3,2},{4,5},{5,4},{6,7},{7,6},{8,9},{9,8},{10,11... | collective-permute-start | bytes 393224 | tf_op jit(solution)/shard_map/ppermute | solution.py:167
  34.1 8.1 %collective-permute-start.14 = (bf16[4,2,128,128]{3,2,1,0:T(8,128)(2,1)S(1)}, bf16[4,2,128,128]{3,2,1,0:T(8,128)(2,1)S(1)}, u32[]{:S(2)}, u32[]{:S(2)}) collective-permute-start(bf16[4,2,128,128]{3,2,1,0:T(8,128)(2,1)S(1)} %level.22.rest_0_.rest_2_), channel_id=1, source_target_pairs={{0,64},{8,72},{16,80},{24,88},{32,96},{40,104},{48,112},{56,120},{... | collective-permute-start | bytes 786440 | tf_op jit(solution)/shard_map/ppermute | solution.py:155
  36.9 9.3 %collective-permute-start.22 = (bf16[1,2,128,128]{3,2,1,0:T(8,128)(2,1)S(1)}, bf16[1,2,128,128]{3,2,1,0:T(8,128)(2,1)S(1)}, u32[]{:S(2)}, u32[]{:S(2)}) collective-permute-start(bf16[1,2,128,128]{3,2,1,0:T(8,128)(2,1)S(1)} %get-tuple-element.21), channel_id=1, source_target_pairs={{0,6},{1,7},{2,4},{3,5},{4,2},{5,3},{6,0},{7,1},{8,14},{9,15},{10,... | collective-permute-start | bytes 196616 | tf_op jit(solution)/shard_map/ppermute | solution.py:170
  39.7 7.0 %collective-permute-start.21 = (bf16[1,2,128,128]{3,2,1,0:T(8,128)(2,1)S(1)}, bf16[1,2,128,128]{3,2,1,0:T(8,128)(2,1)S(1)}, u32[]{:S(2)}, u32[]{:S(2)}) collective-permute-start(bf16[1,2,128,128]{3,2,1,0:T(8,128)(2,1)S(1)} %get-tuple-element.22), channel_id=1, source_target_pairs={{0,4},{1,5},{2,6},{3,7},{4,0},{5,1},{6,2},{7,3},{8,12},{9,13},{10,... | collective-permute-start | bytes 196616 | tf_op jit(solution)/shard_map/ppermute | solution.py:170
  40.5 6.2 %collective-permute-start.19 = (bf16[1,2,128,128]{3,2,1,0:T(8,128)(2,1)S(1)}, bf16[1,2,128,128]{3,2,1,0:T(8,128)(2,1)S(1)}, u32[]{:S(2)}, u32[]{:S(2)}) collective-permute-start(bf16[1,2,128,128]{3,2,1,0:T(8,128)(2,1)S(1)} %get-tuple-element.23), channel_id=1, source_target_pairs={{0,2},{1,3},{2,0},{3,1},{4,6},{5,7},{6,4},{7,5},{8,10},{9,11},{10,... | collective-permute-start | bytes 196616 | tf_op jit(solution)/shard_map/ppermute | solution.py:170
  42.5 7.0 %collective-permute-start.17 = (bf16[1,2,128,128]{3,2,1,0:T(8,128)(2,1)S(1)}, bf16[1,2,128,128]{3,2,1,0:T(8,128)(2,1)S(1)}, u32[]{:S(2)}, u32[]{:S(2)}) collective-permute-start(bf16[1,2,128,128]{3,2,1,0:T(8,128)(2,1)S(1)} %get-tuple-element.18), channel_id=1, source_target_pairs={{0,6},{1,7},{2,4},{3,5},{4,2},{5,3},{6,0},{7,1},{8,14},{9,15},{10,... | collective-permute-start | bytes 196616 | tf_op jit(solution)/shard_map/ppermute | solution.py:170
  45.4 5.8 %collective-permute-start.16 = (bf16[1,2,128,128]{3,2,1,0:T(8,128)(2,1)S(1)}, bf16[1,2,128,128]{3,2,1,0:T(8,128)(2,1)S(1)}, u32[]{:S(2)}, u32[]{:S(2)}) collective-permute-start(bf16[1,2,128,128]{3,2,1,0:T(8,128)(2,1)S(1)} %get-tuple-element.19), channel_id=1, source_target_pairs={{0,4},{1,5},{2,6},{3,7},{4,0},{5,1},{6,2},{7,3},{8,12},{9,13},{10,... | collective-permute-start | bytes 196616 | tf_op jit(solution)/shard_map/ppermute | solution.py:170
  46.2 5.0 %collective-permute-start.15 = (bf16[1,2,128,128]{3,2,1,0:T(8,128)(2,1)S(1)}, bf16[1,2,128,128]{3,2,1,0:T(8,128)(2,1)S(1)}, u32[]{:S(2)}, u32[]{:S(2)}) collective-permute-start(bf16[1,2,128,128]{3,2,1,0:T(8,128)(2,1)S(1)} %get-tuple-element.20), channel_id=1, source_target_pairs={{0,2},{1,3},{2,0},{3,1},{4,6},{5,7},{6,4},{7,5},{8,10},{9,11},{10,... | collective-permute-start | bytes 196616 | tf_op jit(solution)/shard_map/ppermute | solution.py:170

commit v5 on v4

--- a/solution.py
+++ b/solution.py
@@ -177,7 +177,7 @@
 ORDER = (
     ("A", "leaf", 1), ("B", "leaf", 1), ("A", 0, 1), ("B", 0, 1), ("C", "leaf", 2), ("A", 1, 1), ("B", 1, 1), ("C", 0, 2), ("A", 2, 1), ("B", 2, 1), ("C", 1, 2), ("A", 3, 1), ("B", 3, 1), ("C", 2, 1), ("C", 3, 1),
 )
-FAR = (((0, 1), (1, 1), (2, 1), (3, 1), (0, 0)), ((1, 0), (2, 0), (3, 0)))
+FAR = (((2, 1), (3, 1), (0, 1), (1, 1), (0, 0)), ((1, 0), (2, 0), (3, 0)))
 
 
 def solution(mesh):

time: 53.3 us -> 53.3 us (level)
  no operation moved by 1% of the time
where the time goes in v5:
time: 53.3 us; the launch traced here: 53.2 us
  starting transfers between devices  33 us (62%)
  Pallas kernels  14 us (26%)
  waiting for transfers between devices  5.97 us (11%)
    ppermute x15, starting transfers between devices, proceed(): lax.ppermute(part, 'src', pairs_by(1 << height, 16))  20.6 us
    ppermute x6, starting transfers between devices, shards(): lax.ppermute(piece, 'tgt', pairs_by(2 * j, 8))  8.78 us
    pallas_call x3, Pallas kernels, leaf(): pl.pallas_call(kernel, in_specs=[ANY] * (2 + len(after)), out_specs=[VMEM...  6.31 us
    pallas_call x2, Pallas kernels, far_field(): pl.pallas_call(kernel, in_specs=[VMEM] * (count + 1) + [ANY], out_specs=A...  4.81 us
    ppermute x15, waiting for transfers between devices, proceed(): lax.ppermute(part, 'src', pairs_by(1 << height, 16))  4.15 us
    ppermute x2, starting transfers between devices, shards(): new = lax.ppermute(new, 'tgt', pairs_by(1, 8))  3.61 us
    pallas_call x12, Pallas kernels, level(): pl.pallas_call(kernel, in_specs=[VMEM] * (2 + 2 * parts) + [ANY] * len(af...  2.85 us
    ppermute x6, waiting for transfers between devices, shards(): lax.ppermute(piece, 'tgt', pairs_by(2 * j, 8))  1.64 us
  transfers between devices with their start and end apart: 23, of which 5 were waited for; matrix products, arithmetic and copies ran while one was open for 0% of the time, Pallas kernels for 19%

profile of v5, /device:TPU:0, one launch (start us, length us, event | category | flops | bytes accessed | tf_op | source)
XLA Modules:
  0.0 53.2 jit_solution(13394613921796434149)
XLA Ops:
  0.0 1.8 %leaf.3.rest_0_ = bf16[2,2,128,128]{3,2,1,0:T(8,128)(2,1)S(1)} custom-call(bf16[16,128,1024]{2,1,0:T(8,128)(2,1)} %project.5, bf16[16384,128]{1,0:T(8,128)(2,1)} %charges.5), custom_call_target="tpu_custom_call" | custom-call | flops 134217728 | bytes 2097152 | tf_op jit(solution)/shard_map/leaf/pallas_call | solution.py:67
  1.8 0.0 copy-start
  1.9 0.0 copy-start.1
  1.9 0.1 collective-permute-start.1
  2.0 2.0 %leaf.4.rest_2_.rest_0_ = bf16[2,2,128,128]{3,2,1,0:T(8,128)(2,1)S(1)} custom-call(bf16[16,128,1024]{2,1,0:T(8,128)(2,1)} %project.5, bf16[16384,128]{1,0:T(8,128)(2,1)} %charges.5, bf16[2,2,128,128]{3,2,1,0:T(8,128)(2,1)S(1)} %leaf.3.rest_0_), custom_call_target="tpu_custom_call" | custom-call | flops 134217728 | bytes 2097152 | tf_op jit(solution)/shard_map/leaf/pallas_call | solution.py:67
  3.9 0.4 collective-permute-start
  4.4 0.2 level.12.rest_2_.rest_0_
  4.6 1.7 %collective-permute-start.5 = (bf16[2,2,128,128]{3,2,1,0:T(8,128)(2,1)S(1)}, bf16[2,2,128,128]{3,2,1,0:T(8,128)(2,1)S(1)}, u32[]{:S(2)}, u32[]{:S(2)}) collective-permute-start(bf16[2,2,128,128]{3,2,1,0:T(8,128)(2,1)S(1)} %level.12.rest_2_.rest_0_), channel_id=1, source_target_pairs={{0,16},{8,24},{16,0},{24,8},{32,48},{40,56},{48,32},{56,40},{64,80... | collective-permute-start | bytes 393224 | tf_op jit(solution)/shard_map/ppermute | solution.py:155
  6.4 0.2 level.13.rest_0_
  6.6 0.8 %collective-permute-start.4 = (bf16[2,2,128,128]{3,2,1,0:T(8,128)(2,1)S(1)}, bf16[2,2,128,128]{3,2,1,0:T(8,128)(2,1)S(1)}, u32[]{:S(2)}, u32[]{:S(2)}) collective-permute-start(bf16[2,2,128,128]{3,2,1,0:T(8,128)(2,1)S(1)} %level.13.rest_0_), channel_id=1, source_target_pairs={{0,16},{8,24},{16,0},{24,8},{32,48},{40,56},{48,32},{56,40},{64,80... | collective-permute-start | bytes 393224 | tf_op jit(solution)/shard_map/ppermute | solution.py:155
  7.3 2.5 %leaf.5 = (bf16[2,2,128,128]{3,2,1,0:T(8,128)(2,1)S(1)}, bf16[2,2,128,128]{3,2,1,0:T(8,128)(2,1)S(1)}) custom-call(bf16[16,128,1024]{2,1,0:T(8,128)(2,1)} %project.5, bf16[16384,128]{1,0:T(8,128)(2,1)} %charges.5, bf16[2,2,128,128]{3,2,1,0:T(8,128)(2,1)S(1)} %level.13.rest_0_), custom_call_target="tpu_custom_call" | custom-call | flops 268435456 | bytes 4194304 | tf_op jit(solution)/shard_map/leaf/pallas_call | solution.py:67
  9.8 0.1 collective-permute-start.3
  10.0 0.4 collective-permute-start.2
  10.4 0.6 %collective-permute-done.5.rest_1_ = bf16[2,2,128,128]{3,2,1,0:T(8,128)(2,1)S(1)} collective-permute-done((bf16[2,2,128,128]{3,2,1,0:T(8,128)(2,1)S(1)}, bf16[2,2,128,128]{3,2,1,0:T(8,128)(2,1)S(1)}, u32[]{:S(2)}, u32[]{:S(2)}) %collective-permute-start.5) | collective-permute-done | bytes 131104 | tf_op jit(solution)/shard_map/ppermute | solution.py:155
  11.0 0.2 level.14.rest_2_.rest_0_
  11.2 2.1 %collective-permute-start.9 = (bf16[2,2,128,128]{3,2,1,0:T(8,128)(2,1)S(1)}, bf16[2,2,128,128]{3,2,1,0:T(8,128)(2,1)S(1)}, u32[]{:S(2)}, u32[]{:S(2)}) collective-permute-start(bf16[2,2,128,128]{3,2,1,0:T(8,128)(2,1)S(1)} %level.14.rest_2_.rest_0_), channel_id=1, source_target_pairs={{0,32},{8,40},{16,48},{24,56},{32,0},{40,8},{48,16},{56,24},{64,96... | collective-permute-start | bytes 393224 | tf_op jit(solution)/shard_map/ppermute | solution.py:155
  13.3 0.2 level.15.rest_4_.rest_0_
  13.5 1.8 %collective-permute-start.8 = (bf16[2,2,128,128]{3,2,1,0:T(8,128)(2,1)S(1)}, bf16[2,2,128,128]{3,2,1,0:T(8,128)(2,1)S(1)}, u32[]{:S(2)}, u32[]{:S(2)}) collective-permute-start(bf16[2,2,128,128]{3,2,1,0:T(8,128)(2,1)S(1)} %level.15.rest_4_.rest_0_), channel_id=1, source_target_pairs={{0,32},{8,40},{16,48},{24,56},{32,0},{40,8},{48,16},{56,24},{64,96... | collective-permute-start | bytes 393224 | tf_op jit(solution)/shard_map/ppermute | solution.py:155
  15.4 0.3 level.16
  15.7 1.7 %collective-permute-start.7 = (bf16[2,2,128,128]{3,2,1,0:T(8,128)(2,1)S(1)}, bf16[2,2,128,128]{3,2,1,0:T(8,128)(2,1)S(1)}, u32[]{:S(2)}, u32[]{:S(2)}) collective-permute-start(bf16[2,2,128,128]{3,2,1,0:T(8,128)(2,1)S(1)} %get-tuple-element.14.rest_1_), channel_id=1, source_target_pairs={{0,16},{8,24},{16,0},{24,8},{32,48},{40,56},{48,32},{56,40},{64,80... | collective-permute-start | bytes 393224 | tf_op jit(solution)/shard_map/ppermute | solution.py:155
  17.3 0.4 collective-permute-start.6
  17.8 0.2 level.17.rest_2_.rest_0_
  18.0 3.7 %collective-permute-start.13 = (bf16[2,2,128,128]{3,2,1,0:T(8,128)(2,1)S(1)}, bf16[2,2,128,128]{3,2,1,0:T(8,128)(2,1)S(1)}, u32[]{:S(2)}, u32[]{:S(2)}) collective-permute-start(bf16[2,2,128,128]{3,2,1,0:T(8,128)(2,1)S(1)} %level.17.rest_2_.rest_0_), channel_id=1, source_target_pairs={{0,64},{8,72},{16,80},{24,88},{32,96},{40,104},{48,112},{56,120},{... | collective-permute-start | bytes 393224 | tf_op jit(solution)/shard_map/ppermute | solution.py:155
  21.7 0.2 level.18.rest_4_.rest_0_
  21.9 2.6 %collective-permute-start.12 = (bf16[2,2,128,128]{3,2,1,0:T(8,128)(2,1)S(1)}, bf16[2,2,128,128]{3,2,1,0:T(8,128)(2,1)S(1)}, u32[]{:S(2)}, u32[]{:S(2)}) collective-permute-start(bf16[2,2,128,128]{3,2,1,0:T(8,128)(2,1)S(1)} %level.18.rest_4_.rest_0_), channel_id=1, source_target_pairs={{0,64},{8,72},{16,80},{24,88},{32,96},{40,104},{48,112},{56,120},{... | collective-permute-start | bytes 393224 | tf_op jit(solution)/shard_map/ppermute | solution.py:155
  24.5 0.3 level.19
  24.8 1.1 %collective-permute-start.11 = (bf16[2,2,128,128]{3,2,1,0:T(8,128)(2,1)S(1)}, bf16[2,2,128,128]{3,2,1,0:T(8,128)(2,1)S(1)}, u32[]{:S(2)}, u32[]{:S(2)}) collective-permute-start(bf16[2,2,128,128]{3,2,1,0:T(8,128)(2,1)S(1)} %get-tuple-element.16.rest_1_), channel_id=1, source_target_pairs={{0,32},{8,40},{16,48},{24,56},{32,0},{40,8},{48,16},{56,24},{64,96... | collective-permute-start | bytes 393224 | tf_op jit(solution)/shard_map/ppermute | solution.py:155
  25.9 1.0 %collective-permute-start.10 = (bf16[2,2,128,128]{3,2,1,0:T(8,128)(2,1)S(1)}, bf16[2,2,128,128]{3,2,1,0:T(8,128)(2,1)S(1)}, u32[]{:S(2)}, u32[]{:S(2)}) collective-permute-start(bf16[2,2,128,128]{3,2,1,0:T(8,128)(2,1)S(1)} %get-tuple-element.15.rest_2_.rest_0_), channel_id=1, source_target_pairs={{0,32},{8,40},{16,48},{24,56},{32,0},{40,8},{48,16},{56,24},{64,96... | collective-permute-start | bytes 393224 | tf_op jit(solution)/shard_map/ppermute | solution.py:155
  26.9 0.2 level.20.rest_2_
  27.1 2.8 %collective-permute-done.12.rest_1_ = bf16[2,2,128,128]{3,2,1,0:T(8,128)(2,1)S(1)} collective-permute-done((bf16[2,2,128,128]{3,2,1,0:T(8,128)(2,1)S(1)}, bf16[2,2,128,128]{3,2,1,0:T(8,128)(2,1)S(1)}, u32[]{:S(2)}, u32[]{:S(2)}) %collective-permute-start.12) | collective-permute-done | bytes 131104 | tf_op jit(solution)/shard_map/ppermute | solution.py:155
  29.9 0.2 level.21.rest_4_
  30.1 3.3 %collective-permute-start.18 = (bf16[2,2,128,128]{3,2,1,0:T(8,128)(2,1)S(1)}, bf16[2,2,128,128]{3,2,1,0:T(8,128)(2,1)S(1)}, u32[]{:S(2)}, u32[]{:S(2)}) collective-permute-start(bf16[2,2,128,128]{3,2,1,0:T(8,128)(2,1)S(1)} %level.21.rest_4_), channel_id=1, source_target_pairs={{0,1},{1,0},{2,3},{3,2},{4,5},{5,4},{6,7},{7,6},{8,9},{9,8},{10,11... | collective-permute-start | bytes 393224 | tf_op jit(solution)/shard_map/ppermute | solution.py:167
  33.4 0.3 collective-permute-start.21
  33.8 0.0 collective-permute-done.10.rest_2_
  33.8 0.3 level.22.rest_0_.rest_2_
  34.1 2.6 %collective-permute-start.14 = (bf16[4,2,128,128]{3,2,1,0:T(8,128)(2,1)S(1)}, bf16[4,2,128,128]{3,2,1,0:T(8,128)(2,1)S(1)}, u32[]{:S(2)}, u32[]{:S(2)}) collective-permute-start(bf16[4,2,128,128]{3,2,1,0:T(8,128)(2,1)S(1)} %level.22.rest_0_.rest_2_), channel_id=1, source_target_pairs={{0,64},{8,72},{16,80},{24,88},{32,96},{40,104},{48,112},{56,120},{... | collective-permute-start | bytes 786440 | tf_op jit(solution)/shard_map/ppermute | solution.py:155
  36.7 0.2 collective-permute-done.18
  36.9 2.8 %collective-permute-start.20 = (bf16[1,2,128,128]{3,2,1,0:T(8,128)(2,1)S(1)}, bf16[1,2,128,128]{3,2,1,0:T(8,128)(2,1)S(1)}, u32[]{:S(2)}, u32[]{:S(2)}) collective-permute-start(bf16[1,2,128,128]{3,2,1,0:T(8,128)(2,1)S(1)} %get-tuple-element.23), channel_id=1, source_target_pairs={{0,6},{1,7},{2,4},{3,5},{4,2},{5,3},{6,0},{7,1},{8,14},{9,15},{10,... | collective-permute-start | bytes 196616 | tf_op jit(solution)/shard_map/ppermute | solution.py:170
  39.7 0.8 %collective-permute-start.19 = (bf16[1,2,128,128]{3,2,1,0:T(8,128)(2,1)S(1)}, bf16[1,2,128,128]{3,2,1,0:T(8,128)(2,1)S(1)}, u32[]{:S(2)}, u32[]{:S(2)}) collective-permute-start(bf16[1,2,128,128]{3,2,1,0:T(8,128)(2,1)S(1)} %get-tuple-element.24), channel_id=1, source_target_pairs={{0,4},{1,5},{2,6},{3,7},{4,0},{5,1},{6,2},{7,3},{8,12},{9,13},{10,... | collective-permute-start | bytes 196616 | tf_op jit(solution)/shard_map/ppermute | solution.py:170
  40.5 1.0 %collective-permute-start.22 = (bf16[1,2,128,128]{3,2,1,0:T(8,128)(2,1)S(1)}, bf16[1,2,128,128]{3,2,1,0:T(8,128)(2,1)S(1)}, u32[]{:S(2)}, u32[]{:S(2)}) collective-permute-start(bf16[1,2,128,128]{3,2,1,0:T(8,128)(2,1)S(1)} %get-tuple-element.21), channel_id=1, source_target_pairs={{0,2},{1,3},{2,0},{3,1},{4,6},{5,7},{6,4},{7,5},{8,10},{9,11},{10,... | collective-permute-start | bytes 196616 | tf_op jit(solution)/shard_map/ppermute | solution.py:170
  41.5 0.7 %collective-permute-done.14.rest_1_ = bf16[4,2,128,128]{3,2,1,0:T(8,128)(2,1)S(1)} collective-permute-done((bf16[4,2,128,128]{3,2,1,0:T(8,128)(2,1)S(1)}, bf16[4,2,128,128]{3,2,1,0:T(8,128)(2,1)S(1)}, u32[]{:S(2)}, u32[]{:S(2)}) %collective-permute-start.14) | collective-permute-done | bytes 262176 | tf_op jit(solution)/shard_map/ppermute | solution.py:155
  42.2 0.3 level.23
  42.5 2.8 %collective-permute-start.17 = (bf16[1,2,128,128]{3,2,1,0:T(8,128)(2,1)S(1)}, bf16[1,2,128,128]{3,2,1,0:T(8,128)(2,1)S(1)}, u32[]{:S(2)}, u32[]{:S(2)}) collective-permute-start(bf16[1,2,128,128]{3,2,1,0:T(8,128)(2,1)S(1)} %get-tuple-element.18), channel_id=1, source_target_pairs={{0,6},{1,7},{2,4},{3,5},{4,2},{5,3},{6,0},{7,1},{8,14},{9,15},{10,... | collective-permute-start | bytes 196616 | tf_op jit(solution)/shard_map/ppermute | solution.py:170
  45.4 0.8 %collective-permute-start.16 = (bf16[1,2,128,128]{3,2,1,0:T(8,128)(2,1)S(1)}, bf16[1,2,128,128]{3,2,1,0:T(8,128)(2,1)S(1)}, u32[]{:S(2)}, u32[]{:S(2)}) collective-permute-start(bf16[1,2,128,128]{3,2,1,0:T(8,128)(2,1)S(1)} %get-tuple-element.19), channel_id=1, source_target_pairs={{0,4},{1,5},{2,6},{3,7},{4,0},{5,1},{6,2},{7,3},{8,12},{9,13},{10,... | collective-permute-start | bytes 196616 | tf_op jit(solution)/shard_map/ppermute | solution.py:170
  46.2 0.5 %collective-permute-start.15 = (bf16[1,2,128,128]{3,2,1,0:T(8,128)(2,1)S(1)}, bf16[1,2,128,128]{3,2,1,0:T(8,128)(2,1)S(1)}, u32[]{:S(2)}, u32[]{:S(2)}) collective-permute-start(bf16[1,2,128,128]{3,2,1,0:T(8,128)(2,1)S(1)} %get-tuple-element.20), channel_id=1, source_target_pairs={{0,2},{1,3},{2,0},{3,1},{4,6},{5,7},{6,4},{7,5},{8,10},{9,11},{10,... | collective-permute-start | bytes 196616 | tf_op jit(solution)/shard_map/ppermute | solution.py:170
  46.7 2.8 %far_field.2.refs_4_ = bf16[2,16384,128]{2,1,0:T(8,128)(2,1)} custom-call(bf16[1,2,128,128]{3,2,1,0:T(8,128)(2,1)S(1)} %collective-permute-done.19.refs_0_, bf16[1,2,128,128]{3,2,1,0:T(8,128)(2,1)S(1)} %collective-permute-done.20.refs_1_, bf16[1,2,128,128]{3,2,1,0:T(8,128)(2,1)S(1)} %get-tuple-element.22.refs_2_, ...), custom_call_target="tpu_custom_call" | custom-call | flops 671088640 | bytes 7864320 | tf_op jit(solution)/shard_map/far_field/pallas_call | solution.py:135
  49.5 1.6 %collective-permute-done.16.refs_1_ = bf16[1,2,128,128]{3,2,1,0:T(8,128)(2,1)S(1)} collective-permute-done((bf16[1,2,128,128]{3,2,1,0:T(8,128)(2,1)S(1)}, bf16[1,2,128,128]{3,2,1,0:T(8,128)(2,1)S(1)}, u32[]{:S(2)}, u32[]{:S(2)}) %collective-permute-start.16) | collective-permute-done | bytes 65568 | tf_op jit(solution)/shard_map/ppermute | solution.py:170
  51.1 2.0 %far_field.3 = bf16[2,16384,128]{2,1,0:T(8,128)(2,1)} custom-call(bf16[1,2,128,128]{3,2,1,0:T(8,128)(2,1)S(1)} %collective-permute-done.15.refs_0_, bf16[1,2,128,128]{3,2,1,0:T(8,128)(2,1)S(1)} %collective-permute-done.16.refs_1_, bf16[1,2,128,128]{3,2,1,0:T(8,128)(2,1)S(1)} %collective-permute-done.17.refs_2_, ...), custom_call_target="tpu_custom_call", output_to_operand_aliasing={{}: (4, {})} | custom-call | flops 402653184 | bytes 4718592 | tf_op jit(solution)/shard_map/far_field/pallas_call | solution.py:135
  (24 shorter events, 0.1 us)
Async XLA Ops:
  1.8 2.5 %copy-start = (bf16[4,16,64,128]{3,2,1,0:T(8,128)(2,1)S(1)}, bf16[4,16,64,128]{3,2,1,0:T(8,128)(2,1)}, u32[]{:S(2)}) copy-start(bf16[4,16,64,128]{3,2,1,0:T(8,128)(2,1)} %refs_6_.1) | copy-start | bytes 3145732
  1.9 2.5 %copy-start.1 = (bf16[4,16,64,128]{3,2,1,0:T(8,128)(2,1)S(1)}, bf16[4,16,64,128]{3,2,1,0:T(8,128)(2,1)}, u32[]{:S(2)}) copy-start(bf16[4,16,64,128]{3,2,1,0:T(8,128)(2,1)} %cross.23) | copy-start | bytes 3145732
  1.9 2.5 %collective-permute-start.1 = (bf16[2,2,128,128]{3,2,1,0:T(8,128)(2,1)S(1)}, bf16[2,2,128,128]{3,2,1,0:T(8,128)(2,1)S(1)}, u32[]{:S(2)}, u32[]{:S(2)}) collective-permute-start(bf16[2,2,128,128]{3,2,1,0:T(8,128)(2,1)S(1)} %leaf.3.rest_0_), channel_id=1, source_target_pairs={{0,8},{8,0},{16,24},{24,16},{32,40},{40,32},{48,56},{56,48},{64,72... | collective-permute-start | bytes 393224 | tf_op jit(solution)/shard_map/ppermute | solution.py:155
  3.9 2.4 %collective-permute-start = (bf16[2,2,128,128]{3,2,1,0:T(8,128)(2,1)S(1)}, bf16[2,2,128,128]{3,2,1,0:T(8,128)(2,1)S(1)}, u32[]{:S(2)}, u32[]{:S(2)}) collective-permute-start(bf16[2,2,128,128]{3,2,1,0:T(8,128)(2,1)S(1)} %leaf.4.rest_2_.rest_0_), channel_id=1, source_target_pairs={{0,8},{8,0},{16,24},{24,16},{32,40},{40,32},{48,56},{56,48},{64,72... | collective-permute-start | bytes 393224 | tf_op jit(solution)/shard_map/ppermute | solution.py:155
  4.6 6.4 %collective-permute-start.5 = (bf16[2,2,128,128]{3,2,1,0:T(8,128)(2,1)S(1)}, bf16[2,2,128,128]{3,2,1,0:T(8,128)(2,1)S(1)}, u32[]{:S(2)}, u32[]{:S(2)}) collective-permute-start(bf16[2,2,128,128]{3,2,1,0:T(8,128)(2,1)S(1)} %level.12.rest_2_.rest_0_), channel_id=1, source_target_pairs={{0,16},{8,24},{16,0},{24,8},{32,48},{40,56},{48,32},{56,40},{64,80... | collective-permute-start | bytes 393224 | tf_op jit(solution)/shard_map/ppermute | solution.py:155
  6.6 6.8 %collective-permute-start.4 = (bf16[2,2,128,128]{3,2,1,0:T(8,128)(2,1)S(1)}, bf16[2,2,128,128]{3,2,1,0:T(8,128)(2,1)S(1)}, u32[]{:S(2)}, u32[]{:S(2)}) collective-permute-start(bf16[2,2,128,128]{3,2,1,0:T(8,128)(2,1)S(1)} %level.13.rest_0_), channel_id=1, source_target_pairs={{0,16},{8,24},{16,0},{24,8},{32,48},{40,56},{48,32},{56,40},{64,80... | collective-permute-start | bytes 393224 | tf_op jit(solution)/shard_map/ppermute | solution.py:155
  9.8 5.5 %collective-permute-start.3 = (bf16[2,2,128,128]{3,2,1,0:T(8,128)(2,1)S(1)}, bf16[2,2,128,128]{3,2,1,0:T(8,128)(2,1)S(1)}, u32[]{:S(2)}, u32[]{:S(2)}) collective-permute-start(bf16[2,2,128,128]{3,2,1,0:T(8,128)(2,1)S(1)} %get-tuple-element.12.rest_1_), channel_id=1, source_target_pairs={{0,8},{8,0},{16,24},{24,16},{32,40},{40,32},{48,56},{56,48},{64,72... | collective-permute-start | bytes 393224 | tf_op jit(solution)/shard_map/ppermute | solution.py:155
  10.0 5.4 %collective-permute-start.2 = (bf16[2,2,128,128]{3,2,1,0:T(8,128)(2,1)S(1)}, bf16[2,2,128,128]{3,2,1,0:T(8,128)(2,1)S(1)}, u32[]{:S(2)}, u32[]{:S(2)}) collective-permute-start(bf16[2,2,128,128]{3,2,1,0:T(8,128)(2,1)S(1)} %get-tuple-element.11.rest_2_.rest_0_), channel_id=1, source_target_pairs={{0,8},{8,0},{16,24},{24,16},{32,40},{40,32},{48,56},{56,48},{64,72... | collective-permute-start | bytes 393224 | tf_op jit(solution)/shard_map/ppermute | solution.py:155
  11.2 6.5 %collective-permute-start.9 = (bf16[2,2,128,128]{3,2,1,0:T(8,128)(2,1)S(1)}, bf16[2,2,128,128]{3,2,1,0:T(8,128)(2,1)S(1)}, u32[]{:S(2)}, u32[]{:S(2)}) collective-permute-start(bf16[2,2,128,128]{3,2,1,0:T(8,128)(2,1)S(1)} %level.14.rest_2_.rest_0_), channel_id=1, source_target_pairs={{0,32},{8,40},{16,48},{24,56},{32,0},{40,8},{48,16},{56,24},{64,96... | collective-permute-start | bytes 393224 | tf_op jit(solution)/shard_map/ppermute | solution.py:155
  13.5 8.1 %collective-permute-start.8 = (bf16[2,2,128,128]{3,2,1,0:T(8,128)(2,1)S(1)}, bf16[2,2,128,128]{3,2,1,0:T(8,128)(2,1)S(1)}, u32[]{:S(2)}, u32[]{:S(2)}) collective-permute-start(bf16[2,2,128,128]{3,2,1,0:T(8,128)(2,1)S(1)} %level.15.rest_4_.rest_0_), channel_id=1, source_target_pairs={{0,32},{8,40},{16,48},{24,56},{32,0},{40,8},{48,16},{56,24},{64,96... | collective-permute-start | bytes 393224 | tf_op jit(solution)/shard_map/ppermute | solution.py:155
  15.7 8.8 %collective-permute-start.7 = (bf16[2,2,128,128]{3,2,1,0:T(8,128)(2,1)S(1)}, bf16[2,2,128,128]{3,2,1,0:T(8,128)(2,1)S(1)}, u32[]{:S(2)}, u32[]{:S(2)}) collective-permute-start(bf16[2,2,128,128]{3,2,1,0:T(8,128)(2,1)S(1)} %get-tuple-element.14.rest_1_), channel_id=1, source_target_pairs={{0,16},{8,24},{16,0},{24,8},{32,48},{40,56},{48,32},{56,40},{64,80... | collective-permute-start | bytes 393224 | tf_op jit(solution)/shard_map/ppermute | solution.py:155
  17.3 7.2 %collective-permute-start.6 = (bf16[2,2,128,128]{3,2,1,0:T(8,128)(2,1)S(1)}, bf16[2,2,128,128]{3,2,1,0:T(8,128)(2,1)S(1)}, u32[]{:S(2)}, u32[]{:S(2)}) collective-permute-start(bf16[2,2,128,128]{3,2,1,0:T(8,128)(2,1)S(1)} %get-tuple-element.13.rest_2_.rest_0_), channel_id=1, source_target_pairs={{0,16},{8,24},{16,0},{24,8},{32,48},{40,56},{48,32},{56,40},{64,80... | collective-permute-start | bytes 393224 | tf_op jit(solution)/shard_map/ppermute | solution.py:155
  18.0 8.9 %collective-permute-start.13 = (bf16[2,2,128,128]{3,2,1,0:T(8,128)(2,1)S(1)}, bf16[2,2,128,128]{3,2,1,0:T(8,128)(2,1)S(1)}, u32[]{:S(2)}, u32[]{:S(2)}) collective-permute-start(bf16[2,2,128,128]{3,2,1,0:T(8,128)(2,1)S(1)} %level.17.rest_2_.rest_0_), channel_id=1, source_target_pairs={{0,64},{8,72},{16,80},{24,88},{32,96},{40,104},{48,112},{56,120},{... | collective-permute-start | bytes 393224 | tf_op jit(solution)/shard_map/ppermute | solution.py:155
  21.9 8.0 %collective-permute-start.12 = (bf16[2,2,128,128]{3,2,1,0:T(8,128)(2,1)S(1)}, bf16[2,2,128,128]{3,2,1,0:T(8,128)(2,1)S(1)}, u32[]{:S(2)}, u32[]{:S(2)}) collective-permute-start(bf16[2,2,128,128]{3,2,1,0:T(8,128)(2,1)S(1)} %level.18.rest_4_.rest_0_), channel_id=1, source_target_pairs={{0,64},{8,72},{16,80},{24,88},{32,96},{40,104},{48,112},{56,120},{... | collective-permute-start | bytes 393224 | tf_op jit(solution)/shard_map/ppermute | solution.py:155
  24.8 9.0 %collective-permute-start.11 = (bf16[2,2,128,128]{3,2,1,0:T(8,128)(2,1)S(1)}, bf16[2,2,128,128]{3,2,1,0:T(8,128)(2,1)S(1)}, u32[]{:S(2)}, u32[]{:S(2)}) collective-permute-start(bf16[2,2,128,128]{3,2,1,0:T(8,128)(2,1)S(1)} %get-tuple-element.16.rest_1_), channel_id=1, source_target_pairs={{0,32},{8,40},{16,48},{24,56},{32,0},{40,8},{48,16},{56,24},{64,96... | collective-permute-start | bytes 393224 | tf_op jit(solution)/shard_map/ppermute | solution.py:155
  25.9 7.9 %collective-permute-start.10 = (bf16[2,2,128,128]{3,2,1,0:T(8,128)(2,1)S(1)}, bf16[2,2,128,128]{3,2,1,0:T(8,128)(2,1)S(1)}, u32[]{:S(2)}, u32[]{:S(2)}) collective-permute-start(bf16[2,2,128,128]{3,2,1,0:T(8,128)(2,1)S(1)} %get-tuple-element.15.rest_2_.rest_0_), channel_id=1, source_target_pairs={{0,32},{8,40},{16,48},{24,56},{32,0},{40,8},{48,16},{56,24},{64,96... | collective-permute-start | bytes 393224 | tf_op jit(solution)/shard_map/ppermute | solution.py:155
  30.1 16.6 %copy-start.2 = (bf16[16,1024,128]{2,1,0:T(8,128)(2,1)S(1)}, bf16[16,1024,128]{2,1,0:T(8,128)(2,1)}, u32[]{:S(2)}) copy-start(bf16[16,1024,128]{2,1,0:T(8,128)(2,1)} %refs_3_.1) | copy-start | bytes 12582916
  30.1 6.7 %collective-permute-start.18 = (bf16[2,2,128,128]{3,2,1,0:T(8,128)(2,1)S(1)}, bf16[2,2,128,128]{3,2,1,0:T(8,128)(2,1)S(1)}, u32[]{:S(2)}, u32[]{:S(2)}) collective-permute-start(bf16[2,2,128,128]{3,2,1,0:T(8,128)(2,1)S(1)} %level.21.rest_4_), channel_id=1, source_target_pairs={{0,1},{1,0},{2,3},{3,2},{4,5},{5,4},{6,7},{7,6},{8,9},{9,8},{10,11... | collective-permute-start | bytes 393224 | tf_op jit(solution)/shard_map/ppermute | solution.py:167
  33.4 7.1 %collective-permute-start.21 = (bf16[2,2,128,128]{3,2,1,0:T(8,128)(2,1)S(1)}, bf16[2,2,128,128]{3,2,1,0:T(8,128)(2,1)S(1)}, u32[]{:S(2)}, u32[]{:S(2)}) collective-permute-start(bf16[2,2,128,128]{3,2,1,0:T(8,128)(2,1)S(1)} %level.20.rest_2_), channel_id=1, source_target_pairs={{0,1},{1,0},{2,3},{3,2},{4,5},{5,4},{6,7},{7,6},{8,9},{9,8},{10,11... | collective-permute-start | bytes 393224 | tf_op jit(solution)/shard_map/ppermute | solution.py:167
  34.1 8.1 %collective-permute-start.14 = (bf16[4,2,128,128]{3,2,1,0:T(8,128)(2,1)S(1)}, bf16[4,2,128,128]{3,2,1,0:T(8,128)(2,1)S(1)}, u32[]{:S(2)}, u32[]{:S(2)}) collective-permute-start(bf16[4,2,128,128]{3,2,1,0:T(8,128)(2,1)S(1)} %level.22.rest_0_.rest_2_), channel_id=1, source_target_pairs={{0,64},{8,72},{16,80},{24,88},{32,96},{40,104},{48,112},{56,120},{... | collective-permute-start | bytes 786440 | tf_op jit(solution)/shard_map/ppermute | solution.py:155
  36.9 9.3 %collective-permute-start.20 = (bf16[1,2,128,128]{3,2,1,0:T(8,128)(2,1)S(1)}, bf16[1,2,128,128]{3,2,1,0:T(8,128)(2,1)S(1)}, u32[]{:S(2)}, u32[]{:S(2)}) collective-permute-start(bf16[1,2,128,128]{3,2,1,0:T(8,128)(2,1)S(1)} %get-tuple-element.23), channel_id=1, source_target_pairs={{0,6},{1,7},{2,4},{3,5},{4,2},{5,3},{6,0},{7,1},{8,14},{9,15},{10,... | collective-permute-start | bytes 196616 | tf_op jit(solution)/shard_map/ppermute | solution.py:170
  39.7 7.0 %collective-permute-start.19 = (bf16[1,2,128,128]{3,2,1,0:T(8,128)(2,1)S(1)}, bf16[1,2,128,128]{3,2,1,0:T(8,128)(2,1)S(1)}, u32[]{:S(2)}, u32[]{:S(2)}) collective-permute-start(bf16[1,2,128,128]{3,2,1,0:T(8,128)(2,1)S(1)} %get-tuple-element.24), channel_id=1, source_target_pairs={{0,4},{1,5},{2,6},{3,7},{4,0},{5,1},{6,2},{7,3},{8,12},{9,13},{10,... | collective-permute-start | bytes 196616 | tf_op jit(solution)/shard_map/ppermute | solution.py:170
  40.5 6.2 %collective-permute-start.22 = (bf16[1,2,128,128]{3,2,1,0:T(8,128)(2,1)S(1)}, bf16[1,2,128,128]{3,2,1,0:T(8,128)(2,1)S(1)}, u32[]{:S(2)}, u32[]{:S(2)}) collective-permute-start(bf16[1,2,128,128]{3,2,1,0:T(8,128)(2,1)S(1)} %get-tuple-element.21), channel_id=1, source_target_pairs={{0,2},{1,3},{2,0},{3,1},{4,6},{5,7},{6,4},{7,5},{8,10},{9,11},{10,... | collective-permute-start | bytes 196616 | tf_op jit(solution)/shard_map/ppermute | solution.py:170
  42.5 7.0 %collective-permute-start.17 = (bf16[1,2,128,128]{3,2,1,0:T(8,128)(2,1)S(1)}, bf16[1,2,128,128]{3,2,1,0:T(8,128)(2,1)S(1)}, u32[]{:S(2)}, u32[]{:S(2)}) collective-permute-start(bf16[1,2,128,128]{3,2,1,0:T(8,128)(2,1)S(1)} %get-tuple-element.18), channel_id=1, source_target_pairs={{0,6},{1,7},{2,4},{3,5},{4,2},{5,3},{6,0},{7,1},{8,14},{9,15},{10,... | collective-permute-start | bytes 196616 | tf_op jit(solution)/shard_map/ppermute | solution.py:170
  45.4 5.8 %collective-permute-start.16 = (bf16[1,2,128,128]{3,2,1,0:T(8,128)(2,1)S(1)}, bf16[1,2,128,128]{3,2,1,0:T(8,128)(2,1)S(1)}, u32[]{:S(2)}, u32[]{:S(2)}) collective-permute-start(bf16[1,2,128,128]{3,2,1,0:T(8,128)(2,1)S(1)} %get-tuple-element.19), channel_id=1, source_target_pairs={{0,4},{1,5},{2,6},{3,7},{4,0},{5,1},{6,2},{7,3},{8,12},{9,13},{10,... | collective-permute-start | bytes 196616 | tf_op jit(solution)/shard_map/ppermute | solution.py:170
  46.2 5.0 %collective-permute-start.15 = (bf16[1,2,128,128]{3,2,1,0:T(8,128)(2,1)S(1)}, bf16[1,2,128,128]{3,2,1,0:T(8,128)(2,1)S(1)}, u32[]{:S(2)}, u32[]{:S(2)}) collective-permute-start(bf16[1,2,128,128]{3,2,1,0:T(8,128)(2,1)S(1)} %get-tuple-element.20), channel_id=1, source_target_pairs={{0,2},{1,3},{2,0},{3,1},{4,6},{5,7},{6,4},{7,5},{8,10},{9,11},{10,... | collective-permute-start | bytes 196616 | tf_op jit(solution)/shard_map/ppermute | solution.py:170
